TPU v7x, 768 devices: a whole 4x8x12 slice. The times are simulated.
768 devices in a mesh: blk: 64 (over x, y, core), row: 12 (over z).
Axes of the slice: x: 4, y: 8, z: 12, core: 2. Of those that a mesh axis runs over, the one named last changes fastest.
Arguments:
- fields: float32 [256, 48, 5, 512], P('blk', 'row'), may hold values from -6 to 6
- orders: int32 [256, 48], P('blk', 'row'), may hold values from 3 to 7
- metric: float32 [3, 256, 48], P(None, 'blk', 'row'), may hold values from 0.5 to 2
- face_turn: int32 [2, 256, 48], P(None, 'blk', 'row'), may hold values from 0 to 3, as said below
- migration: int32 [64, 12, 16, 1], P('blk', 'row'), may hold values from 0 to 4; in each aligned block of 16 rows (0 to 15, 16 to 31, ..., all dimensions but the last counted through in order) at most 5 rows name the same one
Outputs:
- moved: float32 [64, 12, 25, 5, 512], P('blk', 'row')
Inputs may be any that keep to these rules, and one draw needn't show every extreme that they name: face_turn[0, x, y] equals face_turn[1, x - 1, y], x counted around the closed curve. `migration`: at most 5 elements of one device share a destination, and some device sends exactly 5 to one destination.
All inputs are finite; a program needn't handle non-finite values.
Results may differ from a plain program's by a relative error of at most 0.0003.
Values sent between devices are 32-bit elements; how exact they have to be, the bound alone decides.
No kernel may reach another device: no remote copies, remote signals or barrier semaphores. Data moves between devices by JAX's collectives and lax.ppermute only.
A program may use at most 128 MiB of HBM per device.

v0:
```python
import functools

import jax
import jax.numpy as jnp
import numpy as np
from jax import lax
from jax.experimental import pallas as pl
from jax.experimental.pallas import tpu as pltpu
from jax.sharding import PartitionSpec as P

PMAX = 7
PMIN = 3
VARS = 5
NQ = 8
NB = 16
SPREAD = 5
CAP = 5
LANES = 128

mean_flow = (0.4, 0.0, 0.2)
time_step = 0.008


def legendre_points(degree):
    point_count = degree + 1
    estimate = np.cos(np.pi * np.arange(point_count) / degree)
    for sweep_idx in range(40):
        values = np.zeros((point_count, point_count))
        values[:, 0] = 1.0
        values[:, 1] = estimate
        for order_idx in range(2, point_count):
            values[:, order_idx] = (
                (2 * order_idx - 1) * estimate * values[:, order_idx - 1]
                - (order_idx - 1) * values[:, order_idx - 2]
            ) / order_idx
        estimate = estimate - (estimate * values[:, degree] - values[:, degree - 1]) / (
            point_count * values[:, degree]
        )
    return np.sort(estimate)


def lagrange_matrix(points, targets):
    result = np.ones((len(targets), len(points)))
    for column in range(len(points)):
        for other_idx in range(len(points)):
            if other_idx != column:
                result[:, column] *= (targets - points[other_idx]) / (
                    points[column] - points[other_idx]
                )
    return result


def build_tables(lowest, highest):
    node_count = highest + 1
    level_count = highest - lowest + 1
    common = legendre_points(highest)
    derive = np.zeros((level_count, node_count, node_count))
    to_grid = np.zeros((level_count, node_count, node_count))
    from_grid = np.zeros((level_count, node_count, node_count))
    lifting = np.zeros((level_count,))
    last_node = np.zeros((level_count, node_count))
    active = np.zeros((level_count, node_count))
    for level_idx in range(level_count):
        degree = lowest + level_idx
        points = legendre_points(degree)
        filled = degree + 1
        weights = np.array(
            [
                1.0
                / np.prod(
                    [
                        points[column] - points[other_idx]
                        for other_idx in range(filled)
                        if other_idx != column
                    ]
                )
                for column in range(filled)
            ]
        )
        local_diff = np.zeros((filled, filled))
        for row_idx in range(filled):
            for column in range(filled):
                if column != row_idx:
                    local_diff[row_idx, column] = (
                        weights[column] / weights[row_idx] / (points[row_idx] - points[column])
                    )
            local_diff[row_idx, row_idx] = -np.sum(local_diff[row_idx])
        derive[level_idx, :filled, :filled] = local_diff
        to_grid[level_idx, :, :filled] = lagrange_matrix(points, common)
        from_grid[level_idx, :filled, :] = lagrange_matrix(common, points)
        lifting[level_idx] = degree * (degree + 1) / 2.0
        last_node[level_idx, degree] = 1.0
        active[level_idx, :filled] = 1.0
    return derive, to_grid, from_grid, lifting, last_node, active


D_AT, DK_AT, I_AT, IK_AT, B_AT, BK_AT, W_AT, A_AT, LIFT_AT = (
    0, 64, 128, 192, 256, 320, 384, 392, 400)
TAB_ROWS = 408


def table_rows():
    derive, to_grid, from_grid, lifting, last_node, active = build_tables(PMIN, PMAX)
    rows = np.zeros((TAB_ROWS, LANES))
    for level in range(PMAX - PMIN + 1):
        for at, turned_at, mat in (
            (D_AT, DK_AT, derive[level]),
            (I_AT, IK_AT, to_grid[level]),
            (B_AT, BK_AT, from_grid[level]),
        ):
            rows[at : at + 64, level] = mat.reshape(-1)
            for turn in range(8):
                for a in range(8):
                    rows[turned_at + turn * 8 + a, level] = mat[a, (a + turn) % 8]
        rows[W_AT : W_AT + 8, level] = last_node[level]
        rows[A_AT : A_AT + 8, level] = active[level]
        rows[LIFT_AT : LIFT_AT + 8, level] = lifting[level]
    return rows.astype(np.float32)


def lane_ids():
    lane = lax.broadcasted_iota(jnp.int32, (8, LANES), 1)
    return lane, lane & 15, lane >> 4


def spread(read, dtype):
    _, elem, _ = lane_ids()
    out = jnp.zeros((8, LANES), dtype)
    for e in range(NB):
        out = jnp.where(elem == e, read(e // 4, e % 4), out)
    return out


def rolled(x, by):
    return pltpu.roll(x, by % LANES, 1)


def subrolled(x, by):
    return x if by % 8 == 0 else pltpu.roll(x, by % 8, 0)


def row_of(ref, at):
    return jnp.broadcast_to(ref[pl.ds(at, 1), :], (8, LANES))


def along_first(tab, at, face):
    out = []
    for a in range(8):
        total = row_of(tab, at + a * 8) * face[0]
        for j in range(1, 8):
            total = total + row_of(tab, at + a * 8 + j) * face[j]
        out.append(total)
    return out


def along_second(tab, at, face):
    coefs = [tab[pl.ds(at + 8 * turn, 8), :] for turn in range(8)]
    out = []
    for x in face:
        total = coefs[0] * x
        for turn in range(1, 8):
            total = total + coefs[turn] * subrolled(x, -turn)
        out.append(total)
    return out


def to_common(tab, face):
    return along_second(tab, IK_AT, along_first(tab, I_AT, face))


def from_common(tab, face):
    return along_second(tab, BK_AT, along_first(tab, B_AT, face))


def turned(face, codes, buf):
    for a in range(8):
        buf[pl.ds(8 * a, 8), :] = face[a]
    back = lax.broadcasted_iota(jnp.int32, (8, LANES), 0) * -1 + 7
    out = []
    for a in range(8):
        x = jnp.where(codes == 1, face[7 - a], face[a])
        x = jnp.where(codes == 2, jnp.take_along_axis(face[a], back, axis=0), x)
        x = jnp.where(codes == 3, buf[pl.ds(a, 8, stride=8), :], x)
        out.append(x)
    return out


def coupling_of(direction):
    lane, elem, var = lane_ids()
    vel = elem + 16 * (1 + direction)
    source = jnp.where((var == 0) | (var == 4), vel, lane)
    source = jnp.where(var == 1 + direction, elem + 64, source)
    has = (var == 0) | (var == 4) | (var == 1 + direction)
    return source, jnp.where(has, 1.0, 0.0).astype(jnp.float32)


def jump_flux(gap, direction, sign):
    source, has = coupling_of(direction)
    speed = abs(mean_flow[direction]) + 1.0
    factor = 0.5 * (mean_flow[direction] + sign * speed)
    half = 0.5 * has
    return [factor * x + half * jnp.take_along_axis(x, source, axis=1) for x in gap]


def load_face(ref):
    return [ref[pl.ds(8 * a, 8), :] for a in range(8)]


def store_face(ref, face):
    for a in range(8):
        ref[pl.ds(8 * a, 8), :] = face[a]


def picked(tab, read):
    out = None
    for n in range(PMIN, NQ):
        w = row_of(tab, W_AT + n)
        layer = [w * x for x in read(n)]
        out = layer if out is None else [s + x for s, x in zip(out, layer)]
    return out


def node(i, j):
    return pl.ds((i * 8 + j) * 8, 8)


def x_faces(q, tab):
    low = [q[node(0, j), :] for j in range(8)]
    high = picked(tab, lambda n: [q[node(n, j), :] for j in range(8)])
    return low, high


def y_faces(q, tab):
    low = [q[node(i, 0), :] for i in range(8)]
    high = picked(tab, lambda n: [q[node(i, n), :] for i in range(8)])
    return low, high


def z_faces(q, tab):
    low = [q[pl.ds(i * 64, 8, stride=8), :] for i in range(8)]
    high = picked(tab, lambda n: [q[pl.ds(i * 64 + n, 8, stride=8), :] for i in range(8)])
    return low, high


def make_traces(q, tab, code_low, code_high, outs, buf):
    tx_low, tx_high, ty_low, ty_high, right, left, up, down = outs
    low, high = x_faces(q, tab)
    face = turned(to_common(tab, low), code_low, buf)
    store_face(tx_low, face)
    store_face(left, [rolled(x, 12) for x in face])
    face = turned(to_common(tab, high), code_high, buf)
    store_face(tx_high, face)
    store_face(right, [rolled(x, -12) for x in face])
    low, high = y_faces(q, tab)
    face = to_common(tab, low)
    store_face(ty_low, face)
    store_face(down, [rolled(x, 3) for x in face])
    face = to_common(tab, high)
    store_face(ty_high, face)
    store_face(up, [rolled(x, -3) for x in face])


def gaps_to(q, tab, lift, traces, arrived, wall, metric, out):
    tx_low, tx_high, ty_low, ty_high = traces
    from_left, from_right, from_below, from_above = arrived
    _, elem, var = lane_ids()
    scale = lift * metric[0]
    low, high = x_faces(q, tab)
    near = [
        jnp.where(elem < 4, r, rolled(t, 4))
        for r, t in zip(load_face(from_left), load_face(tx_high))
    ]
    gap = jump_flux([n - o for n, o in zip(from_common(tab, near), low)], 0, 1.0)
    for j in range(8):
        out[node(0, j), :] = out[node(0, j), :] + scale * gap[j]
    near = [
        jnp.where(elem >= 12, r, rolled(t, -4))
        for r, t in zip(load_face(from_right), load_face(tx_low))
    ]
    gap = jump_flux([n - o for n, o in zip(from_common(tab, near), high)], 0, -1.0)
    gap = [scale * x for x in gap]
    for n in range(PMIN, NQ):
        w = row_of(tab, W_AT + n)
        for j in range(8):
            out[node(n, j), :] = out[node(n, j), :] - w * gap[j]
    scale = lift * metric[1]
    low, high = y_faces(q, tab)
    own_low = load_face(ty_low)
    flip = jnp.where(var == 2, -1.0, 1.0).astype(jnp.float32)
    first = (elem & 3) == 0
    near = [
        jnp.where(first, jnp.where(wall, flip * o, r), rolled(t, 1))
        for r, t, o in zip(load_face(from_below), load_face(ty_high), own_low)
    ]
    gap = jump_flux([n - o for n, o in zip(from_common(tab, near), low)], 1, 1.0)
    for i in range(8):
        out[node(i, 0), :] = out[node(i, 0), :] + scale * gap[i]
    near = [
        jnp.where((elem & 3) == 3, r, rolled(t, -1))
        for r, t in zip(load_face(from_above), own_low)
    ]
    gap = jump_flux([n - o for n, o in zip(from_common(tab, near), high)], 1, -1.0)
    gap = [scale * x for x in gap]
    for n in range(PMIN, NQ):
        w = row_of(tab, W_AT + n)
        for i in range(8):
            out[node(i, n), :] = out[node(i, n), :] - w * gap[i]
    scale = lift * metric[2]
    low, high = z_faces(q, tab)
    gap_low = jump_flux([h - o for h, o in zip(high, low)], 2, 1.0)
    gap_high = jump_flux([o - h for h, o in zip(high, low)], 2, -1.0)
    sub = lax.broadcasted_iota(jnp.int32, (8, LANES), 0)
    at_low = jnp.where(sub == 0, scale, 0.0)
    at_high = -scale * tab[pl.ds(W_AT, 8), :]
    for i in range(8):
        for j in range(8):
            pick = jnp.full((8, LANES), j, jnp.int32)
            lo = jnp.take_along_axis(gap_low[i], pick, axis=0)
            hi = jnp.take_along_axis(gap_high[i], pick, axis=0)
            out[node(i, j), :] = out[node(i, j), :] + at_low * lo + at_high * hi


def volume_terms(q, tab, metric, out):
    couplings = [coupling_of(d) for d in range(3)]

    def flux(x, d):
        source, has = couplings[d]
        y = metric[d] * x
        mixed = has * jnp.take_along_axis(y, source, axis=1)
        return mixed if mean_flow[d] == 0.0 else mean_flow[d] * y + mixed

    def along_x(j, carry):
        face = [q[node(i, j), :] for i in range(8)]
        for i, x in enumerate(along_first(tab, D_AT, face)):
            out[node(i, j), :] = -flux(x, 0)
        return carry

    lax.fori_loop(0, 8, along_x, 0)

    def along_yz(i, carry):
        face = [q[node(i, j), :] for j in range(8)]
        by_y = along_first(tab, D_AT, face)
        by_z = along_second(tab, DK_AT, face)
        for j in range(8):
            out[node(i, j), :] = out[node(i, j), :] - (flux(by_y[j], 1) + flux(by_z[j], 2))
        return carry

    lax.fori_loop(0, 8, along_yz, 0)


def all_metrics(metric_ref):
    return [spread(lambda x, y, d=d: metric_ref[d, x, y], jnp.float32) for d in range(3)]


def all_codes(turn_ref):
    return [spread(lambda x, y, s=s: turn_ref[s, x, y], jnp.int32) for s in range(2)]


def first_kernel(fields, orders, turn, rows, q, tab, *rest):
    outs, flat, buf = rest[:8], rest[8], rest[9]
    order = spread(lambda x, y: orders[x, y], jnp.int32)
    level = lax.broadcasted_iota(jnp.int32, (LANES, LANES), 0) + PMIN
    one_hot = jnp.where(
        level == jnp.broadcast_to(order[0:1, :], (LANES, LANES)), 1.0, 0.0
    ).astype(jnp.float32)
    tab[...] = jnp.dot(
        rows[...], one_hot, precision=lax.Precision.HIGHEST, preferred_element_type=jnp.float32
    )
    flat[pl.ds(80, 48), :] = jnp.zeros((48, 512), jnp.float32)
    for v in range(VARS):
        for x in range(4):
            flat[pl.ds(v * 16 + x * 4, 4), :] = fields[x, v]
    in_k = tab[pl.ds(A_AT, 8), :]
    for part in range(4):
        block = flat[:, pl.ds(part * LANES, LANES)].T
        for half in range(2):
            in_ik = in_k * row_of(tab, A_AT + part * 2 + half)
            for j in range(8):
                at = (half * 8 + j) * 8
                q[node(part * 2 + half, j), :] = (
                    block[at : at + 8] * in_ik * row_of(tab, A_AT + j)
                )
    code_low, code_high = all_codes(turn)
    make_traces(q, tab, code_low, code_high, outs, buf)


def second_kernel(q, tab, metric_ref, turn, wall_ref, *rest):
    traces, arrived = rest[:4], rest[4:8]
    rate, middle = rest[8], rest[9]
    outs, buf = rest[10:18], rest[18]
    metric = all_metrics(metric_ref)
    lift = tab[pl.ds(LIFT_AT, 8), :]
    volume_terms(q, tab, metric, rate)
    gaps_to(q, tab, lift, traces, arrived, wall_ref[0] == 0, metric, rate)
    for n in range(64):
        at = pl.ds(8 * n, 8)
        middle[at, :] = q[at, :] + time_step * rate[at, :]
    code_low, code_high = all_codes(turn)
    make_traces(middle, tab, code_low, code_high, outs, buf)


def third_kernel(rate, middle, tab, metric_ref, migration, wall_ref, *rest):
    traces, arrived = rest[:4], rest[4:8]
    outs = rest[8:13]
    second, flat, slots, count = rest[13:]
    metric = all_metrics(metric_ref)
    lift = tab[pl.ds(LIFT_AT, 8), :]
    volume_terms(middle, tab, metric, second)
    gaps_to(middle, tab, lift, traces, arrived, wall_ref[0] == 0, metric, second)
    for part in range(4):
        at = pl.ds(part * LANES, LANES)
        flat[at, :] = ((0.5 * time_step) * (rate[at, :] + second[at, :])).T
    slots[...] = jnp.zeros_like(slots)
    for m in range(SPREAD):
        count[m] = 0
    for e in range(NB):
        m = migration[0, 0, e, 0]
        c = count[m]
        count[m] = c + 1
        row = m * 104 + c * 20
        for part in range(4):
            slots[pl.ds(row + part, VARS, stride=4), :] = flat[
                pl.ds(part * LANES + e, VARS, stride=16), :
            ]
    for m in range(SPREAD):
        outs[m][...] = slots[pl.ds(m * 104, 100), :]


def last_kernel(*refs):
    out = refs[SPREAD]
    for m in range(SPREAD):
        out[pl.ds(m * 100, 100), :] = refs[m][...]


def f32(*shape):
    return jax.ShapeDtypeStruct(shape, jnp.float32)


VMEM = pl.BlockSpec(memory_space=pltpu.VMEM)
SMEM = pl.BlockSpec(memory_space=pltpu.SMEM)
PARAMS = pltpu.CompilerParams(vmem_limit_bytes=32 * 1024 * 1024)
FACE = f32(64, LANES)
VOLUME = f32(512, LANES)


def shifted(array, axis, by, periodic):
    count = lax.axis_size(axis)
    pairs = [(i, (i + by) % count) for i in range(count) if periodic or 0 <= i + by < count]
    return lax.ppermute(array, axis, pairs)


def exchanged(sends):
    right, left, up, down = sends
    return [
        shifted(right, "blk", 1, True),
        shifted(left, "blk", -1, True),
        shifted(up, "row", 1, False),
        shifted(down, "row", -1, False),
    ]


def local(fields, orders, metric, face_turn, migration):
    by_var = jnp.transpose(fields, (0, 2, 1, 3))
    wall = lax.axis_index("row").astype(jnp.int32).reshape(1)
    rows = jnp.asarray(table_rows())
    q, tab, *faces = pl.pallas_call(
        first_kernel,
        out_shape=[VOLUME, f32(TAB_ROWS, LANES)] + [FACE] * 8,
        in_specs=[VMEM, SMEM, SMEM, VMEM],
        out_specs=[VMEM] * 10,
        scratch_shapes=[pltpu.VMEM((LANES, 512), jnp.float32), pltpu.VMEM((64, LANES), jnp.float32)],
        compiler_params=PARAMS,
    )(by_var, orders, face_turn, rows)
    arrived = exchanged(faces[4:])
    rate, middle, *next_faces = pl.pallas_call(
        second_kernel,
        out_shape=[VOLUME, VOLUME] + [FACE] * 8,
        in_specs=[VMEM, VMEM, SMEM, SMEM, SMEM] + [VMEM] * 8,
        out_specs=[VMEM] * 10,
        scratch_shapes=[pltpu.VMEM((64, LANES), jnp.float32)],
        compiler_params=PARAMS,
    )(q, tab, metric, face_turn, wall, *faces[:4], *arrived)
    arrived = exchanged(next_faces[4:])
    packed = pl.pallas_call(
        third_kernel,
        out_shape=[f32(100, LANES)] * SPREAD,
        in_specs=[VMEM, VMEM, VMEM, SMEM, SMEM, SMEM] + [VMEM] * 8,
        out_specs=[VMEM] * SPREAD,
        scratch_shapes=[
            pltpu.VMEM((512, LANES), jnp.float32),
            pltpu.VMEM((512, LANES), jnp.float32),
            pltpu.VMEM((SPREAD * 104, LANES), jnp.float32),
            pltpu.SMEM((8,), jnp.int32),
        ],
        compiler_params=PARAMS,
    )(rate, middle, tab, metric, migration, wall, *next_faces[:4], *arrived)
    pieces = [
        packed[m] if m == 2 else shifted(packed[m], "blk", m - 2, True) for m in range(SPREAD)
    ]
    moved = pl.pallas_call(
        last_kernel,
        out_shape=f32(500, LANES),
        in_specs=[VMEM] * SPREAD,
        out_specs=VMEM,
        compiler_params=PARAMS,
    )(*pieces)
    return moved.reshape(1, 1, SPREAD * CAP, VARS, 512)


def solution(mesh):
    placed = (
        P("blk", "row", None, None),
        P("blk", "row"),
        P(None, "blk", "row"),
        P(None, "blk", "row"),
        P("blk", "row", None, None),
    )
    return jax.shard_map(
        local,
        mesh=mesh,
        in_specs=placed,
        out_specs=P("blk", "row", None, None, None),
        check_vma=False,
    )
```

profile of v0, /device:TPU:1, one launch (start us, length us, event | category | flops | bytes accessed | tf_op | source)
XLA Modules:
  0.0 71.3 jit_solution(5612433108746886082)
XLA Ops:
  0.0 0.9 %copy-done = f32[408,128]{1,0:T(8,128)S(1)} copy-done((f32[408,128]{1,0:T(8,128)S(1)}, f32[408,128]{1,0:T(8,128)}, u32[]{:S(2)}) %copy-start) | copy-done | bytes 208920
  0.9 0.9 %copy-done.1 = f32[4,4,5,512]{3,1,2,0:T(4,128)S(1)} copy-done((f32[4,4,5,512]{3,1,2,0:T(4,128)S(1)}, f32[4,4,5,512]{3,1,2,0:T(4,128)}, u32[]{:S(2)}) %copy-start.1) | copy-done | bytes 163864
  1.9 0.7 copy-done.3
  2.5 0.7 copy-done.5
  3.2 1.4 %shard_map.64 = (f32[512,128]{1,0:T(8,128)S(1)}, f32[408,128]{1,0:T(8,128)S(1)}, f32[64,128]{1,0:T(8,128)S(1)}, f32[64,128]{1,0:T(8,128)S(1)}, f32[64,128]{1,0:T...) custom-call(f32[4,5,4,512]{3,2,1,0:T(4,128)S(1)} %bitcast.2, ...), custom_call_target="tpu_custom_call" | custom-call | tf_op jit(solution)/shard_map/pallas_call | solution.py:466
  4.7 4.6 %collective-permute-start = (f32[64,128]{1,0:T(8,128)S(1)}, f32[64,128]{1,0:T(8,128)S(1)}, u32[]{:S(2)}, u32[]{:S(2)}) collective-permute-start(f32[64,128]{1,0:T(8,128)S(1)} %get-tuple-element.36), channel_id=1, source_target_pairs={{0,12},{12,24},{24,36},{36,48},{48,60},{60,72},{72,84},{84,96},{96... | collective-permute-start | bytes 98312 | tf_op jit(solution)/shard_map/ppermute | solution.py:449
  9.3 9.7 %collective-permute-start.1 = (f32[64,128]{1,0:T(8,128)S(1)}, f32[64,128]{1,0:T(8,128)S(1)}, u32[]{:S(2)}, u32[]{:S(2)}) collective-permute-start(f32[64,128]{1,0:T(8,128)S(1)} %get-tuple-element.37), channel_id=1, source_target_pairs={{0,756},{12,0},{24,12},{36,24},{48,36},{60,48},{72,60},{84,72},{96... | collective-permute-start | bytes 98312 | tf_op jit(solution)/shard_map/ppermute | solution.py:449
  19.0 1.3 %collective-permute-start.2 = (f32[64,128]{1,0:T(8,128)S(1)}, f32[64,128]{1,0:T(8,128)S(1)}, u32[]{:S(2)}, u32[]{:S(2)}) collective-permute-start(f32[64,128]{1,0:T(8,128)S(1)} %get-tuple-element.38), channel_id=1, source_target_pairs={{0,1},{1,2},{2,3},{3,4},{4,5},{5,6},{6,7},{7,8},{8,9},{9,10},{10,1... | collective-permute-start | bytes 98312 | tf_op jit(solution)/shard_map/ppermute | solution.py:449
  20.3 1.3 %collective-permute-start.3 = (f32[64,128]{1,0:T(8,128)S(1)}, f32[64,128]{1,0:T(8,128)S(1)}, u32[]{:S(2)}, u32[]{:S(2)}) collective-permute-start(f32[64,128]{1,0:T(8,128)S(1)} %get-tuple-element.39), channel_id=1, source_target_pairs={{1,0},{2,1},{3,2},{4,3},{5,4},{6,5},{7,6},{8,7},{9,8},{10,9},{11,1... | collective-permute-start | bytes 98312 | tf_op jit(solution)/shard_map/ppermute | solution.py:449
  21.7 3.3 %collective-permute-done.3.rest_7_ = f32[64,128]{1,0:T(8,128)S(1)} collective-permute-done((f32[64,128]{1,0:T(8,128)S(1)}, f32[64,128]{1,0:T(8,128)S(1)}, u32[]{:S(2)}, u32[]{:S(2)}) %collective-permute-start.3) | collective-permute-done | bytes 32800 | tf_op jit(solution)/shard_map/ppermute | solution.py:449
  25.0 0.7 copy-done.2
  25.7 3.2 %shard_map.65 = (f32[512,128]{1,0:T(8,128)S(1)}, f32[512,128]{1,0:T(8,128)S(1)}, f32[64,128]{1,0:T(8,128)S(1)}, f32[64,128]{1,0:T(8,128)S(1)}, f32[64,128]{1,0:T...) custom-call(f32[512,128]{1,0:T(8,128)S(1)} %get-tuple-element.30.q, ...), custom_call_target="tpu_custom_call" | custom-call | tf_op jit(solution)/shard_map/pallas_call | solution.py:475
  28.8 1.9 %collective-permute-start.4 = (f32[64,128]{1,0:T(8,128)S(1)}, f32[64,128]{1,0:T(8,128)S(1)}, u32[]{:S(2)}, u32[]{:S(2)}) collective-permute-start(f32[64,128]{1,0:T(8,128)S(1)} %get-tuple-element.46), channel_id=1, source_target_pairs={{0,12},{12,24},{24,36},{36,48},{48,60},{60,72},{72,84},{84,96},{96... | collective-permute-start | bytes 98312 | tf_op jit(solution)/shard_map/ppermute | solution.py:449
  30.8 8.1 %collective-permute-start.5 = (f32[64,128]{1,0:T(8,128)S(1)}, f32[64,128]{1,0:T(8,128)S(1)}, u32[]{:S(2)}, u32[]{:S(2)}) collective-permute-start(f32[64,128]{1,0:T(8,128)S(1)} %get-tuple-element.47), channel_id=1, source_target_pairs={{0,756},{12,0},{24,12},{36,24},{48,36},{60,48},{72,60},{84,72},{96... | collective-permute-start | bytes 98312 | tf_op jit(solution)/shard_map/ppermute | solution.py:449
  38.9 1.3 %collective-permute-start.6 = (f32[64,128]{1,0:T(8,128)S(1)}, f32[64,128]{1,0:T(8,128)S(1)}, u32[]{:S(2)}, u32[]{:S(2)}) collective-permute-start(f32[64,128]{1,0:T(8,128)S(1)} %get-tuple-element.48), channel_id=1, source_target_pairs={{0,1},{1,2},{2,3},{3,4},{4,5},{5,6},{6,7},{7,8},{8,9},{9,10},{10,1... | collective-permute-start | bytes 98312 | tf_op jit(solution)/shard_map/ppermute | solution.py:449
  40.2 1.3 %collective-permute-start.7 = (f32[64,128]{1,0:T(8,128)S(1)}, f32[64,128]{1,0:T(8,128)S(1)}, u32[]{:S(2)}, u32[]{:S(2)}) collective-permute-start(f32[64,128]{1,0:T(8,128)S(1)} %get-tuple-element.49), channel_id=1, source_target_pairs={{1,0},{2,1},{3,2},{4,3},{5,4},{6,5},{7,6},{8,7},{9,8},{10,9},{11,1... | collective-permute-start | bytes 98312 | tf_op jit(solution)/shard_map/ppermute | solution.py:449
  41.6 3.3 %collective-permute-done.7.rest_7_ = f32[64,128]{1,0:T(8,128)S(1)} collective-permute-done((f32[64,128]{1,0:T(8,128)S(1)}, f32[64,128]{1,0:T(8,128)S(1)}, u32[]{:S(2)}, u32[]{:S(2)}) %collective-permute-start.7) | collective-permute-done | bytes 32800 | tf_op jit(solution)/shard_map/ppermute | solution.py:449
  44.9 3.1 %shard_map.66 = (f32[100,128]{1,0:T(8,128)S(1)}, f32[100,128]{1,0:T(8,128)S(1)}, f32[100,128]{1,0:T(8,128)S(1)}, f32[100,128]{1,0:T(8,128)S(1)}, f32[100,128]{1,0:T(8,128)S(1)}) custom-call(f32[512,128]{1,0:T(8,128)S(1)} %get-tuple-element.40.rate, f32[512,128]{1,0:T(8,128)S(1)} %get-tuple-element.41.middle, f32[408,128]{1,0:T(8,128)S(1)} %get-tuple-element.31.tab, ...), custom_call_target="tpu_custom_call" | custom-call | tf_op jit(solution)/shard_map/pallas_call | solution.py:484
  48.0 1.9 %collective-permute-start.10 = (f32[100,128]{1,0:T(8,128)S(1)}, f32[100,128]{1,0:T(8,128)S(1)}, u32[]{:S(2)}, u32[]{:S(2)}) collective-permute-start(f32[100,128]{1,0:T(8,128)S(1)} %get-tuple-element.53), channel_id=1, source_target_pairs={{0,12},{12,24},{24,36},{36,48},{48,60},{60,72},{72,84},{84,96},{96... | collective-permute-start | bytes 153608 | tf_op jit(solution)/shard_map/ppermute | solution.py:449
  49.9 2.8 %collective-permute-start.11 = (f32[100,128]{1,0:T(8,128)S(1)}, f32[100,128]{1,0:T(8,128)S(1)}, u32[]{:S(2)}, u32[]{:S(2)}) collective-permute-start(f32[100,128]{1,0:T(8,128)S(1)} %get-tuple-element.54), channel_id=1, source_target_pairs={{0,24},{12,36},{24,48},{36,60},{48,72},{60,84},{72,96},{84,108},{9... | collective-permute-start | bytes 153608 | tf_op jit(solution)/shard_map/ppermute | solution.py:449
  52.7 12.2 %collective-permute-start.8 = (f32[100,128]{1,0:T(8,128)S(1)}, f32[100,128]{1,0:T(8,128)S(1)}, u32[]{:S(2)}, u32[]{:S(2)}) collective-permute-start(f32[100,128]{1,0:T(8,128)S(1)} %get-tuple-element.50), channel_id=1, source_target_pairs={{0,744},{12,756},{24,0},{36,12},{48,24},{60,36},{72,48},{84,60},{9... | collective-permute-start | bytes 153608 | tf_op jit(solution)/shard_map/ppermute | solution.py:449
  64.9 2.6 %collective-permute-start.9 = (f32[100,128]{1,0:T(8,128)S(1)}, f32[100,128]{1,0:T(8,128)S(1)}, u32[]{:S(2)}, u32[]{:S(2)}) collective-permute-start(f32[100,128]{1,0:T(8,128)S(1)} %get-tuple-element.51), channel_id=1, source_target_pairs={{0,756},{12,0},{24,12},{36,24},{48,36},{60,48},{72,60},{84,72},{96... | collective-permute-start | bytes 153608 | tf_op jit(solution)/shard_map/ppermute | solution.py:449
  67.5 2.8 %collective-permute-done.9.refs_1_ = f32[100,128]{1,0:T(8,128)S(1)} collective-permute-done((f32[100,128]{1,0:T(8,128)S(1)}, f32[100,128]{1,0:T(8,128)S(1)}, u32[]{:S(2)}, u32[]{:S(2)}) %collective-permute-start.9) | collective-permute-done | bytes 51232 | tf_op jit(solution)/shard_map/ppermute | solution.py:449
  70.4 0.9 %reshape.8 = f32[1,1,25,5,512]{4,1,3,2,0:T(1,128)} reshape(f32[500,128]{1,0:T(8,128)S(1)} %shard_map.67) | data formatting | bytes 512000 | tf_op jit(solution)/shard_map/reshape | solution.py:507
  (20 shorter events, 0.2 us)
Async XLA Ops:
  0.0 0.9 %copy-start = (f32[408,128]{1,0:T(8,128)S(1)}, f32[408,128]{1,0:T(8,128)}, u32[]{:S(2)}) copy-start(f32[408,128]{1,0:T(8,128)} %constant.1.clone.rows) | copy-start | bytes 626692
  0.9 0.9 %copy-start.1 = (f32[4,4,5,512]{3,1,2,0:T(4,128)S(1)}, f32[4,4,5,512]{3,1,2,0:T(4,128)}, u32[]{:S(2)}) copy-start(f32[4,4,5,512]{3,1,2,0:T(4,128)} %param.6) | copy-start | bytes 491524
  1.8 0.7 copy-start.3
  2.5 0.7 copy-start.5
  4.7 17.0 %collective-permute-start = (f32[64,128]{1,0:T(8,128)S(1)}, f32[64,128]{1,0:T(8,128)S(1)}, u32[]{:S(2)}, u32[]{:S(2)}) collective-permute-start(f32[64,128]{1,0:T(8,128)S(1)} %get-tuple-element.36), channel_id=1, source_target_pairs={{0,12},{12,24},{24,36},{36,48},{48,60},{60,72},{72,84},{84,96},{96... | collective-permute-start | bytes 98312 | tf_op jit(solution)/shard_map/ppermute | solution.py:449
  9.3 12.4 %collective-permute-start.1 = (f32[64,128]{1,0:T(8,128)S(1)}, f32[64,128]{1,0:T(8,128)S(1)}, u32[]{:S(2)}, u32[]{:S(2)}) collective-permute-start(f32[64,128]{1,0:T(8,128)S(1)} %get-tuple-element.37), channel_id=1, source_target_pairs={{0,756},{12,0},{24,12},{36,24},{48,36},{60,48},{72,60},{84,72},{96... | collective-permute-start | bytes 98312 | tf_op jit(solution)/shard_map/ppermute | solution.py:449
  19.0 2.6 %collective-permute-start.2 = (f32[64,128]{1,0:T(8,128)S(1)}, f32[64,128]{1,0:T(8,128)S(1)}, u32[]{:S(2)}, u32[]{:S(2)}) collective-permute-start(f32[64,128]{1,0:T(8,128)S(1)} %get-tuple-element.38), channel_id=1, source_target_pairs={{0,1},{1,2},{2,3},{3,4},{4,5},{5,6},{6,7},{7,8},{8,9},{9,10},{10,1... | collective-permute-start | bytes 98312 | tf_op jit(solution)/shard_map/ppermute | solution.py:449
  20.3 4.7 %collective-permute-start.3 = (f32[64,128]{1,0:T(8,128)S(1)}, f32[64,128]{1,0:T(8,128)S(1)}, u32[]{:S(2)}, u32[]{:S(2)}) collective-permute-start(f32[64,128]{1,0:T(8,128)S(1)} %get-tuple-element.39), channel_id=1, source_target_pairs={{1,0},{2,1},{3,2},{4,3},{5,4},{6,5},{7,6},{8,7},{9,8},{10,9},{11,1... | collective-permute-start | bytes 98312 | tf_op jit(solution)/shard_map/ppermute | solution.py:449
  25.0 0.7 copy-start.2
  25.0 0.7 copy-start.4
  28.8 12.8 %collective-permute-start.4 = (f32[64,128]{1,0:T(8,128)S(1)}, f32[64,128]{1,0:T(8,128)S(1)}, u32[]{:S(2)}, u32[]{:S(2)}) collective-permute-start(f32[64,128]{1,0:T(8,128)S(1)} %get-tuple-element.46), channel_id=1, source_target_pairs={{0,12},{12,24},{24,36},{36,48},{48,60},{60,72},{72,84},{84,96},{96... | collective-permute-start | bytes 98312 | tf_op jit(solution)/shard_map/ppermute | solution.py:449
  30.8 10.9 %collective-permute-start.5 = (f32[64,128]{1,0:T(8,128)S(1)}, f32[64,128]{1,0:T(8,128)S(1)}, u32[]{:S(2)}, u32[]{:S(2)}) collective-permute-start(f32[64,128]{1,0:T(8,128)S(1)} %get-tuple-element.47), channel_id=1, source_target_pairs={{0,756},{12,0},{24,12},{36,24},{48,36},{60,48},{72,60},{84,72},{96... | collective-permute-start | bytes 98312 | tf_op jit(solution)/shard_map/ppermute | solution.py:449
  38.9 2.7 %copy-start.6 = (s32[1,1,16,1]{2,3,1,0:T(1,128)S(1)}, s32[1,1,16,1]{2,3,1,0:T(1,128)}, u32[]{:S(2)}) copy-start(s32[1,1,16,1]{2,3,1,0:T(1,128)} %param.10) | copy-start | bytes 196
  38.9 2.7 %collective-permute-start.6 = (f32[64,128]{1,0:T(8,128)S(1)}, f32[64,128]{1,0:T(8,128)S(1)}, u32[]{:S(2)}, u32[]{:S(2)}) collective-permute-start(f32[64,128]{1,0:T(8,128)S(1)} %get-tuple-element.48), channel_id=1, source_target_pairs={{0,1},{1,2},{2,3},{3,4},{4,5},{5,6},{6,7},{7,8},{8,9},{9,10},{10,1... | collective-permute-start | bytes 98312 | tf_op jit(solution)/shard_map/ppermute | solution.py:449
  40.2 4.7 %collective-permute-start.7 = (f32[64,128]{1,0:T(8,128)S(1)}, f32[64,128]{1,0:T(8,128)S(1)}, u32[]{:S(2)}, u32[]{:S(2)}) collective-permute-start(f32[64,128]{1,0:T(8,128)S(1)} %get-tuple-element.49), channel_id=1, source_target_pairs={{1,0},{2,1},{3,2},{4,3},{5,4},{6,5},{7,6},{8,7},{9,8},{10,9},{11,1... | collective-permute-start | bytes 98312 | tf_op jit(solution)/shard_map/ppermute | solution.py:449
  48.0 19.5 %collective-permute-start.10 = (f32[100,128]{1,0:T(8,128)S(1)}, f32[100,128]{1,0:T(8,128)S(1)}, u32[]{:S(2)}, u32[]{:S(2)}) collective-permute-start(f32[100,128]{1,0:T(8,128)S(1)} %get-tuple-element.53), channel_id=1, source_target_pairs={{0,12},{12,24},{24,36},{36,48},{48,60},{60,72},{72,84},{84,96},{96... | collective-permute-start | bytes 153608 | tf_op jit(solution)/shard_map/ppermute | solution.py:449
  49.9 17.6 %collective-permute-start.11 = (f32[100,128]{1,0:T(8,128)S(1)}, f32[100,128]{1,0:T(8,128)S(1)}, u32[]{:S(2)}, u32[]{:S(2)}) collective-permute-start(f32[100,128]{1,0:T(8,128)S(1)} %get-tuple-element.54), channel_id=1, source_target_pairs={{0,24},{12,36},{24,48},{36,60},{48,72},{60,84},{72,96},{84,108},{9... | collective-permute-start | bytes 153608 | tf_op jit(solution)/shard_map/ppermute | solution.py:449
  52.7 14.8 %collective-permute-start.8 = (f32[100,128]{1,0:T(8,128)S(1)}, f32[100,128]{1,0:T(8,128)S(1)}, u32[]{:S(2)}, u32[]{:S(2)}) collective-permute-start(f32[100,128]{1,0:T(8,128)S(1)} %get-tuple-element.50), channel_id=1, source_target_pairs={{0,744},{12,756},{24,0},{36,12},{48,24},{60,36},{72,48},{84,60},{9... | collective-permute-start | bytes 153608 | tf_op jit(solution)/shard_map/ppermute | solution.py:449
  64.9 5.5 %collective-permute-start.9 = (f32[100,128]{1,0:T(8,128)S(1)}, f32[100,128]{1,0:T(8,128)S(1)}, u32[]{:S(2)}, u32[]{:S(2)}) collective-permute-start(f32[100,128]{1,0:T(8,128)S(1)} %get-tuple-element.51), channel_id=1, source_target_pairs={{0,756},{12,0},{24,12},{36,24},{48,36},{60,48},{72,60},{84,72},{96... | collective-permute-start | bytes 153608 | tf_op jit(solution)/shard_map/ppermute | solution.py:449
where the time goes:
time: 71.9 us; the launch traced here: 71.3 us
  starting transfers between devices  49.1 us (68%)
  waiting for transfers between devices  9.42 us (13%)
  Pallas kernels  7.72 us (11%)
  local copies, waits for them, and re-layouts  4.95 us (7%)
    ppermute x12, starting transfers between devices, shifted(): return lax.ppermute(array, axis, pairs)  49.1 us
    ppermute x12, waiting for transfers between devices, shifted(): return lax.ppermute(array, axis, pairs)  9.42 us
    unnamed x15, local copies, waits for them, and re-layouts  4.01 us
    pallas_call x1, Pallas kernels, local(): pl.pallas_call(second_kernel, out_shape=[VOLUME, VOLUME] + [FACE] * 8, in...  3.15 us
    pallas_call x1, Pallas kernels, local(): pl.pallas_call(third_kernel, out_shape=[f32(100, LANES)] * SPREAD, in_spe...  3.1 us
    pallas_call x1, Pallas kernels, local(): pl.pallas_call(first_kernel, out_shape=[VOLUME, f32(TAB_ROWS, LANES)] + [...  1.45 us
  transfers between devices with their start and end apart: 12, of which 3 were waited for; matrix products, arithmetic and copies ran while one was open for 0% of the time, Pallas kernels for 0%

commit v1 on v0

--- a/solution.py
+++ b/solution.py
@@ -242,22 +242,49 @@
     return low, high
 
 
-def make_traces(q, tab, code_low, code_high, outs, buf):
-    tx_low, tx_high, ty_low, ty_high, right, left, up, down = outs
+def make_traces(q, tab, code_low, code_high, place, outs, buf):
+    tx_low, tx_high, ty_low, ty_high, chip_send, blk_send, pair_send, row_send = outs
+    first_core, even_row = place
     low, high = x_faces(q, tab)
-    face = turned(to_common(tab, low), code_low, buf)
-    store_face(tx_low, face)
-    store_face(left, [rolled(x, 12) for x in face])
-    face = turned(to_common(tab, high), code_high, buf)
-    store_face(tx_high, face)
-    store_face(right, [rolled(x, -12) for x in face])
+    low = turned(to_common(tab, low), code_low, buf)
+    store_face(tx_low, low)
+    high = turned(to_common(tab, high), code_high, buf)
+    store_face(tx_high, high)
+    low = [rolled(x, 12) for x in low]
+    high = [rolled(x, -12) for x in high]
+    store_face(chip_send, [jnp.where(first_core, h, l) for l, h in zip(low, high)])
+    store_face(blk_send, [jnp.where(first_core, l, h) for l, h in zip(low, high)])
     low, high = y_faces(q, tab)
-    face = to_common(tab, low)
-    store_face(ty_low, face)
-    store_face(down, [rolled(x, 3) for x in face])
-    face = to_common(tab, high)
-    store_face(ty_high, face)
-    store_face(up, [rolled(x, -3) for x in face])
+    low = to_common(tab, low)
+    store_face(ty_low, low)
+    high = to_common(tab, high)
+    store_face(ty_high, high)
+    low = [rolled(x, 3) for x in low]
+    high = [rolled(x, -3) for x in high]
+    store_face(pair_send, [jnp.where(even_row, h, l) for l, h in zip(low, high)])
+    store_face(row_send, [jnp.where(even_row, l, h) for l, h in zip(low, high)])
+
+
+def sorted_arrivals(arrived, place):
+    chip, blk, pair, row = arrived
+    first_core, even_row = place
+    chip = load_face(chip.at[jnp.where(first_core, 1, 0)])
+    pair = load_face(pair.at[jnp.where(even_row, 1, 0)])
+    blk, row = load_face(blk), load_face(row)
+
+    def pick(cond, a, b):
+        return [jnp.where(cond, x, y) for x, y in zip(a, b)]
+
+    return (
+        pick(first_core, blk, chip),
+        pick(first_core, chip, blk),
+        pick(even_row, row, pair),
+        pick(even_row, pair, row),
+    )
+
+
+def places(core_ref, row_ref):
+    return core_ref[0] == 0, lax.rem(row_ref[0], 2) == 0
 
 
 def gaps_to(q, tab, lift, traces, arrived, wall, metric, out):
@@ -268,14 +295,14 @@
     low, high = x_faces(q, tab)
     near = [
         jnp.where(elem < 4, r, rolled(t, 4))
-        for r, t in zip(load_face(from_left), load_face(tx_high))
+        for r, t in zip(from_left, load_face(tx_high))
     ]
     gap = jump_flux([n - o for n, o in zip(from_common(tab, near), low)], 0, 1.0)
     for j in range(8):
         out[node(0, j), :] = out[node(0, j), :] + scale * gap[j]
     near = [
         jnp.where(elem >= 12, r, rolled(t, -4))
-        for r, t in zip(load_face(from_right), load_face(tx_low))
+        for r, t in zip(from_right, load_face(tx_low))
     ]
     gap = jump_flux([n - o for n, o in zip(from_common(tab, near), high)], 0, -1.0)
     gap = [scale * x for x in gap]
@@ -290,14 +317,14 @@
     first = (elem & 3) == 0
     near = [
         jnp.where(first, jnp.where(wall, flip * o, r), rolled(t, 1))
-        for r, t, o in zip(load_face(from_below), load_face(ty_high), own_low)
+        for r, t, o in zip(from_below, load_face(ty_high), own_low)
     ]
     gap = jump_flux([n - o for n, o in zip(from_common(tab, near), low)], 1, 1.0)
     for i in range(8):
         out[node(i, 0), :] = out[node(i, 0), :] + scale * gap[i]
     near = [
         jnp.where((elem & 3) == 3, r, rolled(t, -1))
-        for r, t in zip(load_face(from_above), own_low)
+        for r, t in zip(from_above, own_low)
     ]
     gap = jump_flux([n - o for n, o in zip(from_common(tab, near), high)], 1, -1.0)
     gap = [scale * x for x in gap]
@@ -356,17 +383,32 @@
     return [spread(lambda x, y, s=s: turn_ref[s, x, y], jnp.int32) for s in range(2)]
 
 
-def first_kernel(fields, orders, turn, rows, q, tab, *rest):
-    outs, flat, buf = rest[:8], rest[8], rest[9]
+def fetched(pairs, sems):
+    copies = [pltpu.make_async_copy(a, b, sems.at[n]) for n, (a, b) in enumerate(pairs)]
+    for copy in copies:
+        copy.start()
+    return copies
+
+
+def first_kernel(fields_hbm, orders_hbm, turn_hbm, rows_hbm, core_ref, row_ref, q, tab, *rest):
+    outs = rest[:8]
+    flat, buf, fields, orders, turn, rows, sems = rest[8:]
+    copies = fetched(
+        [(orders_hbm, orders), (turn_hbm, turn), (rows_hbm, rows), (fields_hbm, fields)], sems
+    )
+    flat[pl.ds(80, 48), :] = jnp.zeros((48, 512), jnp.float32)
+    copies[0].wait()
+    copies[1].wait()
     order = spread(lambda x, y: orders[x, y], jnp.int32)
     level = lax.broadcasted_iota(jnp.int32, (LANES, LANES), 0) + PMIN
     one_hot = jnp.where(
         level == jnp.broadcast_to(order[0:1, :], (LANES, LANES)), 1.0, 0.0
     ).astype(jnp.float32)
+    copies[2].wait()
     tab[...] = jnp.dot(
         rows[...], one_hot, precision=lax.Precision.HIGHEST, preferred_element_type=jnp.float32
     )
-    flat[pl.ds(80, 48), :] = jnp.zeros((48, 512), jnp.float32)
+    copies[3].wait()
     for v in range(VARS):
         for x in range(4):
             flat[pl.ds(v * 16 + x * 4, 4), :] = fields[x, v]
@@ -381,55 +423,84 @@
                     block[at : at + 8] * in_ik * row_of(tab, A_AT + j)
                 )
     code_low, code_high = all_codes(turn)
-    make_traces(q, tab, code_low, code_high, outs, buf)
-
-
-def second_kernel(q, tab, metric_ref, turn, wall_ref, *rest):
+    make_traces(q, tab, code_low, code_high, places(core_ref, row_ref), outs, buf)
+
+
+def second_kernel(q, tab, metric_hbm, turn_hbm, core_ref, row_ref, *rest):
     traces, arrived = rest[:4], rest[4:8]
     rate, middle = rest[8], rest[9]
-    outs, buf = rest[10:18], rest[18]
+    outs, buf, metric_ref, turn, sems = rest[10:18], *rest[18:]
+    copies = fetched([(metric_hbm, metric_ref), (turn_hbm, turn)], sems)
+    place = places(core_ref, row_ref)
+    copies[0].wait()
+    copies[1].wait()
     metric = all_metrics(metric_ref)
     lift = tab[pl.ds(LIFT_AT, 8), :]
     volume_terms(q, tab, metric, rate)
-    gaps_to(q, tab, lift, traces, arrived, wall_ref[0] == 0, metric, rate)
+    gaps_to(
+        q, tab, lift, traces, sorted_arrivals(arrived, place), row_ref[0] == 0, metric, rate
+    )
     for n in range(64):
         at = pl.ds(8 * n, 8)
         middle[at, :] = q[at, :] + time_step * rate[at, :]
     code_low, code_high = all_codes(turn)
-    make_traces(middle, tab, code_low, code_high, outs, buf)
-
-
-def third_kernel(rate, middle, tab, metric_ref, migration, wall_ref, *rest):
+    make_traces(middle, tab, code_low, code_high, place, outs, buf)
+
+
+def third_kernel(rate, middle, tab, metric_hbm, migration_hbm, core_ref, row_ref, *rest):
     traces, arrived = rest[:4], rest[4:8]
-    outs = rest[8:13]
-    second, flat, slots, count = rest[13:]
+    outs = rest[8:12]
+    second, flat, slots, count, metric_ref, migration, sems = rest[12:]
+    copies = fetched([(metric_hbm, metric_ref), (migration_hbm, migration)], sems)
+    place = places(core_ref, row_ref)
+    copies[0].wait()
+    copies[1].wait()
     metric = all_metrics(metric_ref)
     lift = tab[pl.ds(LIFT_AT, 8), :]
     volume_terms(middle, tab, metric, second)
-    gaps_to(middle, tab, lift, traces, arrived, wall_ref[0] == 0, metric, second)
+    gaps_to(
+        middle, tab, lift, traces, sorted_arrivals(arrived, place), row_ref[0] == 0, metric, second
+    )
     for part in range(4):
         at = pl.ds(part * LANES, LANES)
-        flat[at, :] = ((0.5 * time_step) * (rate[at, :] + second[at, :])).T
+        flat[:, 0, at] = ((0.5 * time_step) * (rate[at, :] + second[at, :])).T
     slots[...] = jnp.zeros_like(slots)
     for m in range(SPREAD):
         count[m] = 0
     for e in range(NB):
-        m = migration[0, 0, e, 0]
+        m = migration[0, 0, 0, e]
         c = count[m]
         count[m] = c + 1
-        row = m * 104 + c * 20
-        for part in range(4):
-            slots[pl.ds(row + part, VARS, stride=4), :] = flat[
-                pl.ds(part * LANES + e, VARS, stride=16), :
-            ]
-    for m in range(SPREAD):
-        outs[m][...] = slots[pl.ds(m * 104, 100), :]
-
-
-def last_kernel(*refs):
-    out = refs[SPREAD]
-    for m in range(SPREAD):
-        out[pl.ds(m * 100, 100), :] = refs[m][...]
+        slot = jnp.where(core_ref[0] == 0, m, SPREAD - 1 - m) * CAP + c
+        for v in range(VARS):
+            slots[slot, v] = flat[v * 16 + e]
+    at = 0
+    for out in outs:
+        size = out.shape[0]
+        out[...] = slots[pl.ds(at, size)]
+        at += size
+
+
+def last_kernel(far, own, near, core_ref, chip, relayed, out, sems):
+    def put(groups):
+        copies = [
+            pltpu.make_async_copy(piece, out.at[pl.ds(m * CAP, CAP)], sems.at[m])
+            for m, piece in enumerate(groups)
+        ]
+        for copy in copies:
+            copy.start()
+        for copy in copies:
+            copy.wait()
+
+    first = far.at[pl.ds(0, CAP)]
+
+    @pl.when(core_ref[0] == 0)
+    def _():
+        put([first, chip.at[1], own, relayed.at[1, pl.ds(CAP, CAP)], near])
+
+    @pl.when(core_ref[0] != 0)
+    def _():
+        put([near, relayed.at[0, pl.ds(CAP, CAP)], own, chip.at[0], first])
 
 
 def f32(*shape):
@@ -438,73 +509,115 @@
 
 VMEM = pl.BlockSpec(memory_space=pltpu.VMEM)
 SMEM = pl.BlockSpec(memory_space=pltpu.SMEM)
+HBM = pl.BlockSpec(memory_space=pltpu.HBM)
+ANY = pl.BlockSpec(memory_space=pl.ANY)
 PARAMS = pltpu.CompilerParams(vmem_limit_bytes=32 * 1024 * 1024)
 FACE = f32(64, LANES)
 VOLUME = f32(512, LANES)
 
 
-def shifted(array, axis, by, periodic):
+def pairs_of(count, first):
+    return [[n, n + 1] for n in range(first, count - 1, 2)]
+
+
+def swapped(array, axis, wraps):
     count = lax.axis_size(axis)
-    pairs = [(i, (i + by) % count) for i in range(count) if periodic or 0 <= i + by < count]
-    return lax.ppermute(array, axis, pairs)
+    pairs = [(a, b) for a, b in pairs_of(count, 1)]
+    if wraps:
+        pairs.append((count - 1, 0))
+    return lax.ppermute(array, axis, pairs + [(b, a) for a, b in pairs])
+
+
+def paired(array, axis):
+    return lax.all_gather(array, axis, axis_index_groups=pairs_of(lax.axis_size(axis), 0))
 
 
 def exchanged(sends):
-    right, left, up, down = sends
-    return [
-        shifted(right, "blk", 1, True),
-        shifted(left, "blk", -1, True),
-        shifted(up, "row", 1, False),
-        shifted(down, "row", -1, False),
-    ]
+    chip, blk, pair, row = sends
+    blk = swapped(blk, "blk", True)
+    row = swapped(row, "row", False)
+    return [paired(chip, "blk"), blk, paired(pair, "row"), row]
+
+
+def hopped(array, outward):
+    count = lax.axis_size("blk")
+    step = [-2, 2] if outward else [2, -2]
+    return lax.ppermute(array, "blk", [(n, (n + step[n % 2]) % count) for n in range(count)])
+
+
+def vmem(*shape):
+    return pltpu.VMEM(shape, jnp.float32)
+
+
+def sems(count):
+    return pltpu.SemaphoreType.DMA((count,))
 
 
 def local(fields, orders, metric, face_turn, migration):
     by_var = jnp.transpose(fields, (0, 2, 1, 3))
-    wall = lax.axis_index("row").astype(jnp.int32).reshape(1)
+    core = lax.rem(lax.axis_index("blk").astype(jnp.int32), 2).reshape(1)
+    row = lax.axis_index("row").astype(jnp.int32).reshape(1)
     rows = jnp.asarray(table_rows())
+    metric_at = pltpu.SMEM((3, 4, 4), jnp.float32)
+    turn_at = pltpu.SMEM((2, 4, 4), jnp.int32)
     q, tab, *faces = pl.pallas_call(
         first_kernel,
         out_shape=[VOLUME, f32(TAB_ROWS, LANES)] + [FACE] * 8,
-        in_specs=[VMEM, SMEM, SMEM, VMEM],
+        in_specs=[HBM] * 4 + [SMEM] * 2,
         out_specs=[VMEM] * 10,
-        scratch_shapes=[pltpu.VMEM((LANES, 512), jnp.float32), pltpu.VMEM((64, LANES), jnp.float32)],
+        scratch_shapes=[
+            vmem(LANES, 512),
+            vmem(64, LANES),
+            vmem(4, VARS, 4, 512),
+            pltpu.SMEM((4, 4), jnp.int32),
+            turn_at,
+            vmem(TAB_ROWS, LANES),
+            sems(4),
+        ],
         compiler_params=PARAMS,
-    )(by_var, orders, face_turn, rows)
+    )(by_var, orders, face_turn, rows, core, row)
     arrived = exchanged(faces[4:])
     rate, middle, *next_faces = pl.pallas_call(
         second_kernel,
         out_shape=[VOLUME, VOLUME] + [FACE] * 8,
-        in_specs=[VMEM, VMEM, SMEM, SMEM, SMEM] + [VMEM] * 8,
+        in_specs=[VMEM] * 2 + [HBM] * 2 + [SMEM] * 2 + [VMEM] * 8,
         out_specs=[VMEM] * 10,
-        scratch_shapes=[pltpu.VMEM((64, LANES), jnp.float32)],
+        scratch_shapes=[vmem(64, LANES), metric_at, turn_at, sems(2)],
         compiler_params=PARAMS,
-    )(q, tab, metric, face_turn, wall, *faces[:4], *arrived)
+    )(q, tab, metric, face_turn, core, row, *faces[:4], *arrived)
     arrived = exchanged(next_faces[4:])
-    packed = pl.pallas_call(
+    outward, own, same_chip, inward = pl.pallas_call(
         third_kernel,
-        out_shape=[f32(100, LANES)] * SPREAD,
-        in_specs=[VMEM, VMEM, VMEM, SMEM, SMEM, SMEM] + [VMEM] * 8,
-        out_specs=[VMEM] * SPREAD,
+        out_shape=[f32(n, VARS, 1, 512) for n in (2 * CAP, CAP, CAP, CAP)],
+        in_specs=[VMEM] * 3 + [HBM] * 2 + [SMEM] * 2 + [VMEM] * 8,
+        out_specs=[VMEM] * 4,
         scratch_shapes=[
-            pltpu.VMEM((512, LANES), jnp.float32),
-            pltpu.VMEM((512, LANES), jnp.float32),
-            pltpu.VMEM((SPREAD * 104, LANES), jnp.float32),
+            vmem(512, LANES),
+            vmem(LANES, 1, 512),
+            vmem(SPREAD * CAP, VARS, 1, 512),
             pltpu.SMEM((8,), jnp.int32),
+            metric_at,
+            pltpu.SMEM((1, 1, 1, NB), jnp.int32),
+            sems(2),
         ],
         compiler_params=PARAMS,
-    )(rate, middle, tab, metric, migration, wall, *next_faces[:4], *arrived)
-    pieces = [
-        packed[m] if m == 2 else shifted(packed[m], "blk", m - 2, True) for m in range(SPREAD)
-    ]
+    )(
+        rate, middle, tab, metric, jnp.transpose(migration, (0, 1, 3, 2)), core, row,
+        *next_faces[:4], *arrived,
+    )
+    far = hopped(outward, True)
+    near = hopped(inward, False)
+    chip = paired(same_chip, "blk")
+    relayed = paired(far, "blk")
     moved = pl.pallas_call(
         last_kernel,
-        out_shape=f32(500, LANES),
-        in_specs=[VMEM] * SPREAD,
-        out_specs=VMEM,
+        out_shape=f32(SPREAD * CAP, VARS, 1, 512),
+        in_specs=[ANY] * 3 + [SMEM] + [ANY] * 2,
+        out_specs=HBM,
+        scratch_shapes=[sems(SPREAD)],
         compiler_params=PARAMS,
-    )(*pieces)
-    return moved.reshape(1, 1, SPREAD * CAP, VARS, 512)
+    )(far, own, near, core, chip, relayed)
+    return jnp.transpose(moved, (2, 0, 1, 3)).reshape(1, 1, SPREAD * CAP, VARS, 512)
 
 
 def solution(mesh):

time: 71.9 us -> 61.2 us (0.85)
  the two profiles are of different devices: /device:TPU:1 before, /device:TPU:128 now
where the time goes in v1:
time: 61.2 us; the launch traced here: 60.8 us
  blocking collectives  23 us (38%)
  starting transfers between devices  21.7 us (35%)
  Pallas kernels  8.5 us (14%)
  local copies, waits for them, and re-layouts  3.89 us (6%)
  waiting for transfers between devices  3.58 us (6%)
    all_gather x6, blocking collectives, paired(): lax.all_gather(array, axis, axis_index_groups=pairs_of(lax.axis_size(axis...  23 us
    ppermute x4, starting transfers between devices, swapped(): return lax.ppermute(array, axis, pairs + [(b, a) for a, b in pairs])  13.3 us
    ppermute x2, starting transfers between devices, hopped(): lax.ppermute(array, 'blk', [(n, (n + step[n % 2]) % count) for n in range...  8.42 us
    unnamed x12, local copies, waits for them, and re-layouts  3.89 us
    ppermute x2, waiting for transfers between devices, hopped(): lax.ppermute(array, 'blk', [(n, (n + step[n % 2]) % count) for n in range...  3.57 us
    pallas_call x1, Pallas kernels, local(): pl.pallas_call(second_kernel, out_shape=[VOLUME, VOLUME] + [FACE] * 8, in...  3.18 us
    pallas_call x1, Pallas kernels, local(): pl.pallas_call(third_kernel, out_shape=[f32(n, VARS, 1, 512) for n in (2...  3.05 us
    pallas_call x1, Pallas kernels, local(): pl.pallas_call(first_kernel, out_shape=[VOLUME, f32(TAB_ROWS, LANES)] + [...  1.54 us
  transfers between devices with their start and end apart: 6, of which 1 were waited for; matrix products, arithmetic and copies ran while one was open for 0% of the time, Pallas kernels for 0%

profile of v1, /device:TPU:128, one launch (start us, length us, event | category | flops | bytes accessed | tf_op | source)
XLA Modules:
  0.0 60.8 jit_solution(3154136196151608209)
XLA Ops:
  0.0 0.7 %copy-done.3 = s32[2,4,4]{2,1,0:T(4,128)S(1)} copy-done((s32[2,4,4]{2,1,0:T(4,128)S(1)}, s32[2,4,4]{2,1,0:T(4,128)}, u32[]{:S(2)}) %copy-start.3) | copy-done | bytes 152
  0.7 0.0 copy-done.4
  0.7 0.9 %copy-done = f32[408,128]{1,0:T(8,128)S(1)} copy-done((f32[408,128]{1,0:T(8,128)S(1)}, f32[408,128]{1,0:T(8,128)}, u32[]{:S(2)}) %copy-start) | copy-done | bytes 208920
  1.6 0.9 %copy-done.1 = f32[4,4,5,512]{3,1,2,0:T(4,128)S(1)} copy-done((f32[4,4,5,512]{3,1,2,0:T(4,128)S(1)}, f32[4,4,5,512]{3,1,2,0:T(4,128)}, u32[]{:S(2)}) %copy-start.1) | copy-done | bytes 163864
  2.5 1.5 %shard_map.64 = (f32[512,128]{1,0:T(8,128)S(1)}, f32[408,128]{1,0:T(8,128)S(1)}, f32[64,128]{1,0:T(8,128)S(1)}, f32[64,128]{1,0:T(8,128)S(1)}, f32[64,128]{1,0:T...) custom-call(f32[4,5,4,512]{3,2,1,0:T(4,128)S(1)} %bitcast.19, ...), custom_call_target="tpu_custom_call" | custom-call | tf_op jit(solution)/shard_map/pallas_call | solution.py:563
  4.1 7.0 %collective-permute-start = (f32[64,128]{1,0:T(8,128)S(1)}, f32[64,128]{1,0:T(8,128)S(1)}, u32[]{:S(2)}, u32[]{:S(2)}) collective-permute-start(f32[64,128]{1,0:T(8,128)S(1)} %get-tuple-element.36), channel_id=1, source_target_pairs={{12,24},{36,48},{60,72},{84,96},{108,120},{132,144},{156,168},{180... | collective-permute-start | bytes 98312 | tf_op jit(solution)/shard_map/ppermute | solution.py:528
  11.1 1.9 %collective-permute-start.1 = (f32[64,128]{1,0:T(8,128)S(1)}, f32[64,128]{1,0:T(8,128)S(1)}, u32[]{:S(2)}, u32[]{:S(2)}) collective-permute-start(f32[64,128]{1,0:T(8,128)S(1)} %get-tuple-element.38), channel_id=1, source_target_pairs={{1,2},{3,4},{5,6},{7,8},{9,10},{2,1},{4,3},{6,5},{8,7},{10,9},{13,... | collective-permute-start | bytes 98312 | tf_op jit(solution)/shard_map/ppermute | solution.py:528
  13.0 1.9 %all-gather = f32[128,128]{1,0:T(8,128)S(1)} all-gather(f32[64,128]{1,0:T(8,128)S(1)} %get-tuple-element.35), channel_id=2, replica_groups={{0,12},{24,36},{48,60},{72,84},{96,108},{120,132},{144,156},{168,180},{..., dimensions={0}, use_global_device_ids=true | all-gather | bytes 98304 | tf_op jit(solution)/shard_map/all_gather | solution.py:532
  14.9 8.5 %all-gather.1 = f32[128,128]{1,0:T(8,128)S(1)} all-gather(f32[64,128]{1,0:T(8,128)S(1)} %get-tuple-element.37), channel_id=3, replica_groups={{0,1},{2,3},{4,5},{6,7},{8,9},{10,11},{12,13},{14,15},{16,17},{18,19},{..., dimensions={0}, use_global_device_ids=true | all-gather | bytes 98304 | tf_op jit(solution)/shard_map/all_gather | solution.py:532
  23.4 0.0 collective-permute-done.rest_5_
  23.4 0.7 %copy-done.2 = f32[3,4,4]{2,1,0:T(4,128)S(1)} copy-done((f32[3,4,4]{2,1,0:T(4,128)S(1)}, f32[3,4,4]{2,1,0:T(4,128)}, u32[]{:S(2)}) %copy-start.2) | copy-done | bytes 216
  24.1 3.2 %shard_map.65 = (f32[512,128]{1,0:T(8,128)S(1)}, f32[512,128]{1,0:T(8,128)S(1)}, f32[64,128]{1,0:T(8,128)S(1)}, f32[64,128]{1,0:T(8,128)S(1)}, f32[64,128]{1,0:T...) custom-call(f32[512,128]{1,0:T(8,128)S(1)} %get-tuple-element.29.q, ...), custom_call_target="tpu_custom_call" | custom-call | tf_op jit(solution)/shard_map/pallas_call | solution.py:580
  27.3 2.2 %collective-permute-start.2 = (f32[64,128]{1,0:T(8,128)S(1)}, f32[64,128]{1,0:T(8,128)S(1)}, u32[]{:S(2)}, u32[]{:S(2)}) collective-permute-start(f32[64,128]{1,0:T(8,128)S(1)} %get-tuple-element.46), channel_id=1, source_target_pairs={{12,24},{36,48},{60,72},{84,96},{108,120},{132,144},{156,168},{180... | collective-permute-start | bytes 98312 | tf_op jit(solution)/shard_map/ppermute | solution.py:528
  29.4 2.2 %collective-permute-start.3 = (f32[64,128]{1,0:T(8,128)S(1)}, f32[64,128]{1,0:T(8,128)S(1)}, u32[]{:S(2)}, u32[]{:S(2)}) collective-permute-start(f32[64,128]{1,0:T(8,128)S(1)} %get-tuple-element.48), channel_id=1, source_target_pairs={{1,2},{3,4},{5,6},{7,8},{9,10},{2,1},{4,3},{6,5},{8,7},{10,9},{13,... | collective-permute-start | bytes 98312 | tf_op jit(solution)/shard_map/ppermute | solution.py:528
  31.6 1.9 %all-gather.2 = f32[128,128]{1,0:T(8,128)S(1)} all-gather(f32[64,128]{1,0:T(8,128)S(1)} %get-tuple-element.45), channel_id=4, replica_groups={{0,12},{24,36},{48,60},{72,84},{96,108},{120,132},{144,156},{168,180},{..., dimensions={0}, use_global_device_ids=true | all-gather | bytes 98304 | tf_op jit(solution)/shard_map/all_gather | solution.py:532
  33.5 7.0 %all-gather.3 = f32[128,128]{1,0:T(8,128)S(1)} all-gather(f32[64,128]{1,0:T(8,128)S(1)} %get-tuple-element.47), channel_id=5, replica_groups={{0,1},{2,3},{4,5},{6,7},{8,9},{10,11},{12,13},{14,15},{16,17},{18,19},{..., dimensions={0}, use_global_device_ids=true | all-gather | bytes 98304 | tf_op jit(solution)/shard_map/all_gather | solution.py:532
  40.5 0.7 %copy-done.5 = s32[1,1,16,1]{2,3,1,0:T(1,128)S(1)} copy-done((s32[1,1,16,1]{2,3,1,0:T(1,128)S(1)}, s32[1,1,16,1]{2,3,1,0:T(1,128)}, u32[]{:S(2)}) %copy-start.5) | copy-done | bytes 88
  41.1 3.1 %shard_map.66 = (f32[10,5,1,512]{3,2,1,0:T(1,128)S(1)}, f32[5,5,1,512]{3,2,1,0:T(1,128)S(1)}, f32[5,5,1,512]{3,2,1,0:T(1,128)S(1)}, f32[5,5,1,512]{3,2,1,0:T(1,128)S(1)}) custom-call(f32[512,128]{1,0:T(8,128)S(1)} %get-tuple-element.39.rate, f32[512,128]{1,0:T(8,128)S(1)} %get-tuple-element.40.middle, f32[408,128]{1,0:T(8,128)S(1)} %get-tuple-element.30.tab, ...), custom_call_target="tpu_custom_call" | custom-call | tf_op jit(solution)/shard_map/pallas_call | solution.py:589
  44.2 6.5 %collective-permute-start.4 = (f32[10,5,1,512]{3,2,1,0:T(1,128)S(1)}, f32[10,5,1,512]{3,2,1,0:T(1,128)S(1)}, u32[]{:S(2)}, u32[]{:S(2)}) collective-permute-start(f32[10,5,1,512]{3,2,1,0:T(1,128)S(1)} %get-tuple-element.49), channel_id=1, source_target_pairs={{0,744},{12,36},{24,0},{36,60},{48,24},{60,84},{72,48},{84,108},{9... | collective-permute-start | bytes 307208 | tf_op jit(solution)/shard_map/ppermute | solution.py:545
  50.7 1.9 %collective-permute-start.5 = (f32[5,5,1,512]{3,2,1,0:T(1,128)S(1)}, f32[5,5,1,512]{3,2,1,0:T(1,128)S(1)}, u32[]{:S(2)}, u32[]{:S(2)}) collective-permute-start(f32[5,5,1,512]{3,2,1,0:T(1,128)S(1)} %get-tuple-element.51), channel_id=1, source_target_pairs={{0,24},{12,756},{24,48},{36,12},{48,72},{60,36},{72,96},{84,60},{9... | collective-permute-start | bytes 153608 | tf_op jit(solution)/shard_map/ppermute | solution.py:545
  52.6 1.9 %all-gather.4 = f32[10,5,1,512]{3,2,1,0:T(1,128)S(1)} all-gather(f32[5,5,1,512]{3,2,1,0:T(1,128)S(1)} %get-tuple-element.52), channel_id=6, replica_groups={{0,12},{24,36},{48,60},{72,84},{96,108},{120,132},{144,156},{168,180},{..., dimensions={0}, use_global_device_ids=true | all-gather | bytes 153600 | tf_op jit(solution)/shard_map/all_gather | solution.py:532
  54.5 1.9 %all-gather.5 = f32[20,5,1,512]{3,2,1,0:T(1,128)S(1)} all-gather(f32[10,5,1,512]{3,2,1,0:T(1,128)S(1)} %collective-permute-done.4.far), channel_id=7, replica_groups={{0,12},{24,36},{48,60},{72,84},{96,108},{120,132},{144,156},{168,180},{..., dimensions={0}, use_global_device_ids=true | all-gather | bytes 307200 | tf_op jit(solution)/shard_map/all_gather | solution.py:532
  56.5 3.6 %collective-permute-done.5.near = f32[5,5,1,512]{3,2,1,0:T(1,128)S(1)} collective-permute-done((f32[5,5,1,512]{3,2,1,0:T(1,128)S(1)}, f32[5,5,1,512]{3,2,1,0:T(1,128)S(1)}, u32[]{:S(2)}, u32[]{:S(2)}) %collective-permute-start.5) | collective-permute-done | bytes 51232 | tf_op jit(solution)/shard_map/ppermute | solution.py:545
  60.0 0.7 %shard_map.67 = f32[25,5,1,512]{3,2,1,0:T(1,128)} custom-call(f32[10,5,1,512]{3,2,1,0:T(1,128)S(1)} %collective-permute-done.4.far, f32[5,5,1,512]{3,2,1,0:T(1,128)S(1)} %get-tuple-element.50.own, f32[5,5,1,512]{3,2,1,0:T(1,128)S(1)} %collective-permute-done.5.near, s32[1]{0:T(128)} %bitcast.1.core_ref, f32[2,5,5,1,512]{4,3,2,1,0:T(1,128)S(1)} %bitcast.14, ...), custom_call_target="tpu_custom_call" | custom-call | tf_op jit(solution)/shard_map/pallas_call | solution.py:612
  (10 shorter events, 0.0 us)
Async XLA Ops:
  0.0 0.7 %copy-start.3 = (s32[2,4,4]{2,1,0:T(4,128)S(1)}, s32[2,4,4]{2,1,0:T(4,128)}, u32[]{:S(2)}) copy-start(s32[2,4,4]{2,1,0:T(4,128)} %turn_hbm.3) | copy-start | bytes 388
  0.0 0.7 %copy-start.4 = (s32[4,4]{1,0:T(4,128)S(1)}, s32[4,4]{1,0:T(4,128)}, u32[]{:S(2)}) copy-start(s32[4,4]{1,0:T(4,128)} %orders_hbm.1) | copy-start | bytes 196
  0.7 0.9 %copy-start = (f32[408,128]{1,0:T(8,128)S(1)}, f32[408,128]{1,0:T(8,128)}, u32[]{:S(2)}) copy-start(f32[408,128]{1,0:T(8,128)} %constant.13.clone.rows_hbm) | copy-start | bytes 626692
  1.6 0.9 %copy-start.1 = (f32[4,4,5,512]{3,1,2,0:T(4,128)S(1)}, f32[4,4,5,512]{3,1,2,0:T(4,128)}, u32[]{:S(2)}) copy-start(f32[4,4,5,512]{3,1,2,0:T(4,128)} %param.6) | copy-start | bytes 491524
  4.1 19.3 %collective-permute-start = (f32[64,128]{1,0:T(8,128)S(1)}, f32[64,128]{1,0:T(8,128)S(1)}, u32[]{:S(2)}, u32[]{:S(2)}) collective-permute-start(f32[64,128]{1,0:T(8,128)S(1)} %get-tuple-element.36), channel_id=1, source_target_pairs={{12,24},{36,48},{60,72},{84,96},{108,120},{132,144},{156,168},{180... | collective-permute-start | bytes 98312 | tf_op jit(solution)/shard_map/ppermute | solution.py:528
  11.1 12.3 %collective-permute-start.1 = (f32[64,128]{1,0:T(8,128)S(1)}, f32[64,128]{1,0:T(8,128)S(1)}, u32[]{:S(2)}, u32[]{:S(2)}) collective-permute-start(f32[64,128]{1,0:T(8,128)S(1)} %get-tuple-element.38), channel_id=1, source_target_pairs={{1,2},{3,4},{5,6},{7,8},{9,10},{2,1},{4,3},{6,5},{8,7},{10,9},{13,... | collective-permute-start | bytes 98312 | tf_op jit(solution)/shard_map/ppermute | solution.py:528
  23.4 0.7 %copy-start.2 = (f32[3,4,4]{2,1,0:T(4,128)S(1)}, f32[3,4,4]{2,1,0:T(4,128)}, u32[]{:S(2)}) copy-start(f32[3,4,4]{2,1,0:T(4,128)} %metric_hbm.3) | copy-start | bytes 580
  27.3 13.2 %collective-permute-start.2 = (f32[64,128]{1,0:T(8,128)S(1)}, f32[64,128]{1,0:T(8,128)S(1)}, u32[]{:S(2)}, u32[]{:S(2)}) collective-permute-start(f32[64,128]{1,0:T(8,128)S(1)} %get-tuple-element.46), channel_id=1, source_target_pairs={{12,24},{36,48},{60,72},{84,96},{108,120},{132,144},{156,168},{180... | collective-permute-start | bytes 98312 | tf_op jit(solution)/shard_map/ppermute | solution.py:528
  29.4 11.1 %collective-permute-start.3 = (f32[64,128]{1,0:T(8,128)S(1)}, f32[64,128]{1,0:T(8,128)S(1)}, u32[]{:S(2)}, u32[]{:S(2)}) collective-permute-start(f32[64,128]{1,0:T(8,128)S(1)} %get-tuple-element.48), channel_id=1, source_target_pairs={{1,2},{3,4},{5,6},{7,8},{9,10},{2,1},{4,3},{6,5},{8,7},{10,9},{13,... | collective-permute-start | bytes 98312 | tf_op jit(solution)/shard_map/ppermute | solution.py:528
  40.5 0.7 %copy-start.5 = (s32[1,1,16,1]{2,3,1,0:T(1,128)S(1)}, s32[1,1,16,1]{2,3,1,0:T(1,128)}, u32[]{:S(2)}) copy-start(s32[1,1,16,1]{2,3,1,0:T(1,128)} %param.10) | copy-start | bytes 196
  44.2 10.3 %collective-permute-start.4 = (f32[10,5,1,512]{3,2,1,0:T(1,128)S(1)}, f32[10,5,1,512]{3,2,1,0:T(1,128)S(1)}, u32[]{:S(2)}, u32[]{:S(2)}) collective-permute-start(f32[10,5,1,512]{3,2,1,0:T(1,128)S(1)} %get-tuple-element.49), channel_id=1, source_target_pairs={{0,744},{12,36},{24,0},{36,60},{48,24},{60,84},{72,48},{84,108},{9... | collective-permute-start | bytes 307208 | tf_op jit(solution)/shard_map/ppermute | solution.py:545
  50.7 9.3 %collective-permute-start.5 = (f32[5,5,1,512]{3,2,1,0:T(1,128)S(1)}, f32[5,5,1,512]{3,2,1,0:T(1,128)S(1)}, u32[]{:S(2)}, u32[]{:S(2)}) collective-permute-start(f32[5,5,1,512]{3,2,1,0:T(1,128)S(1)} %get-tuple-element.51), channel_id=1, source_target_pairs={{0,24},{12,756},{24,48},{36,12},{48,72},{60,36},{72,96},{84,60},{9... | collective-permute-start | bytes 153608 | tf_op jit(solution)/shard_map/ppermute | solution.py:545

commit v2 on v1

--- a/solution.py
+++ b/solution.py
@@ -94,9 +94,9 @@
     return derive, to_grid, from_grid, lifting, last_node, active
 
 
-D_AT, DK_AT, I_AT, IK_AT, B_AT, BK_AT, W_AT, A_AT, LIFT_AT = (
-    0, 64, 128, 192, 256, 320, 384, 392, 400)
-TAB_ROWS = 408
+D_AT, DK_AT, I_AT, IK_AT, B_AT, BK_AT, W_AT, A_AT, LIFT_AT, DLAST_AT = (
+    0, 64, 128, 192, 256, 320, 384, 392, 400, 408)
+TAB_ROWS = 416
 
 
 def table_rows():
@@ -115,6 +115,7 @@
         rows[W_AT : W_AT + 8, level] = last_node[level]
         rows[A_AT : A_AT + 8, level] = active[level]
         rows[LIFT_AT : LIFT_AT + 8, level] = lifting[level]
+        rows[DLAST_AT : DLAST_AT + 8, level] = derive[level][PMIN + level]
     return rows.astype(np.float32)
 
 
@@ -194,12 +195,18 @@
     return source, jnp.where(has, 1.0, 0.0).astype(jnp.float32)
 
 
-def jump_flux(gap, direction, sign):
-    source, has = coupling_of(direction)
-    speed = abs(mean_flow[direction]) + 1.0
-    factor = 0.5 * (mean_flow[direction] + sign * speed)
+def jump_with(gap, coupling, factor):
+    source, has = coupling
     half = 0.5 * has
     return [factor * x + half * jnp.take_along_axis(x, source, axis=1) for x in gap]
+
+
+def jump_factor(direction, sign):
+    return 0.5 * (mean_flow[direction] + sign * (abs(mean_flow[direction]) + 1.0))
+
+
+def jump_flux(gap, direction, sign):
+    return jump_with(gap, coupling_of(direction), jump_factor(direction, sign))
 
 
 def load_face(ref):
@@ -242,49 +249,213 @@
     return low, high
 
 
-def make_traces(q, tab, code_low, code_high, place, outs, buf):
-    tx_low, tx_high, ty_low, ty_high, chip_send, blk_send, pair_send, row_send = outs
-    first_core, even_row = place
-    low, high = x_faces(q, tab)
-    low = turned(to_common(tab, low), code_low, buf)
-    store_face(tx_low, low)
-    high = turned(to_common(tab, high), code_high, buf)
-    store_face(tx_high, high)
-    low = [rolled(x, 12) for x in low]
-    high = [rolled(x, -12) for x in high]
-    store_face(chip_send, [jnp.where(first_core, h, l) for l, h in zip(low, high)])
-    store_face(blk_send, [jnp.where(first_core, l, h) for l, h in zip(low, high)])
-    low, high = y_faces(q, tab)
-    low = to_common(tab, low)
-    store_face(ty_low, low)
-    high = to_common(tab, high)
-    store_face(ty_high, high)
-    low = [rolled(x, 3) for x in low]
-    high = [rolled(x, -3) for x in high]
-    store_face(pair_send, [jnp.where(even_row, h, l) for l, h in zip(low, high)])
-    store_face(row_send, [jnp.where(even_row, l, h) for l, h in zip(low, high)])
-
-
-def sorted_arrivals(arrived, place):
-    chip, blk, pair, row = arrived
-    first_core, even_row = place
-    chip = load_face(chip.at[jnp.where(first_core, 1, 0)])
-    pair = load_face(pair.at[jnp.where(even_row, 1, 0)])
-    blk, row = load_face(blk), load_face(row)
-
-    def pick(cond, a, b):
-        return [jnp.where(cond, x, y) for x, y in zip(a, b)]
-
-    return (
-        pick(first_core, blk, chip),
-        pick(first_core, chip, blk),
-        pick(even_row, row, pair),
-        pick(even_row, pair, row),
-    )
+def end_rows(q, tab, read):
+    low = high = None
+    for n in range(NQ):
+        first, last = row_of(tab, D_AT + n), row_of(tab, DLAST_AT + n)
+        layer = read(n)
+        by_low, by_high = [first * x for x in layer], [last * x for x in layer]
+        low = by_low if low is None else [a + b for a, b in zip(low, by_low)]
+        high = by_high if high is None else [a + b for a, b in zip(high, by_high)]
+    return low, high
+
+
+def packed(kinds, where, shifts):
+    out = []
+    for a in range(8):
+        x = rolled(kinds[3][a], shifts[3])
+        for kind in range(3):
+            x = jnp.where(where == kind, rolled(kinds[kind][a], shifts[kind]), x)
+        out.append(x)
+    return out
+
+
+def make_messages(q, tab, order, metric, codes, first_core, outs, buf):
+    tx_low, tx_high, ty_low, ty_high, chip_send, blk_send, up, down = outs
+    _, elem, _ = lane_ids()
+    x_ends, y_ends = x_faces(q, tab), y_faces(q, tab)
+    tx = [turned(to_common(tab, x_ends[side]), codes[side], buf) for side in range(2)]
+    ty = [to_common(tab, y_ends[side]) for side in range(2)]
+    for ref, face in zip((tx_low, tx_high, ty_low, ty_high), tx + ty):
+        store_face(ref, face)
+    x_rows = end_rows(q, tab, lambda n: [q[node(n, j), :] for j in range(8)])
+    y_rows = end_rows(q, tab, lambda n: [q[node(i, n), :] for i in range(8)])
+    params = [order.astype(jnp.float32)] + metric
+    zero = jnp.zeros((8, LANES), jnp.float32)
+
+    def along_x(side, shifts):
+        edge = 7 * side
+        lines = [ty[0][edge], ty[1][edge]] + params + [codes[side].astype(jnp.float32), zero]
+        return packed([tx[side], x_ends[side], x_rows[side], lines], elem >> 2, shifts)
+
+    def along_y(side, shifts):
+        edge = 7 * side
+        lines = [tx[0][edge], tx[1][edge]] + params + [zero, zero]
+        return packed([ty[side], y_ends[side], y_rows[side], lines], elem & 3, shifts)
+
+    left = along_x(0, (0, 4, 8, 12))
+    right = along_x(1, (-12, -8, -4, 0))
+    store_face(chip_send, [jnp.where(first_core, r, l) for l, r in zip(left, right)])
+    store_face(blk_send, [jnp.where(first_core, l, r) for l, r in zip(left, right)])
+    store_face(down, along_y(0, (0, 1, 2, 3)))
+    store_face(up, along_y(1, (-3, -2, -1, 0)))
+
+
+def sides_of(paired_ref, other_ref, first):
+    pair = load_face(paired_ref.at[jnp.where(first, 1, 0)])
+    other = load_face(other_ref)
+    before = [jnp.where(first, o, p) for o, p in zip(other, pair)]
+    after = [jnp.where(first, p, o) for o, p in zip(other, pair)]
+    return before, after
 
 
 def places(core_ref, row_ref):
     return core_ref[0] == 0, lax.rem(row_ref[0], 2) == 0
+
+
+def halo_step(messages, traces, wall, rows, tab, q_buf):
+    left, right, below, above = messages
+    lane, elem, var = lane_ids()
+    group, pos = elem >> 2, elem & 3
+    base = lane - elem
+    across_rows = group >= 2
+    is_high = (group & 1) == 0
+
+    def collected(block, kind):
+        at = base + jnp.where(across_rows, pos * 4 + kind, kind * 4 + pos)
+        out = jnp.take_along_axis(left[block], at, axis=1)
+        for g, message in ((1, right), (2, below), (3, above)):
+            out = jnp.where(group == g, jnp.take_along_axis(message[block], at, axis=1), out)
+        return out
+
+    order = collected(2, 3)
+    level = lax.broadcasted_iota(jnp.int32, (LANES, LANES), 0) + PMIN
+    one_hot = jnp.where(
+        level.astype(jnp.float32) == jnp.broadcast_to(order[0:1, :], (LANES, LANES)), 1.0, 0.0
+    ).astype(jnp.float32)
+    tab[...] = jnp.dot(
+        rows, one_hot, precision=lax.Precision.HIGHEST, preferred_element_type=jnp.float32
+    )
+    lift = tab[pl.ds(LIFT_AT, 8), :]
+    metric_x, metric_y, metric_z = [collected(3 + d, 3) for d in range(3)]
+    metric_n = jnp.where(across_rows, metric_y, metric_x)
+    metric_t = jnp.where(across_rows, metric_x, metric_y)
+    codes = jnp.where(across_rows, 0.0, collected(6, 3)).astype(jnp.int32)
+    by_x, by_y, by_z = [coupling_of(d) for d in range(3)]
+
+    def mixed(a, b):
+        return tuple(jnp.where(across_rows, y, x) for x, y in zip(a, b))
+
+    couple_n, couple_t = mixed(by_x, by_y), mixed(by_y, by_x)
+
+    def factor(d, sign):
+        return jnp.float32(jump_factor(d, sign))
+
+    factor_n = jnp.where(
+        across_rows,
+        jnp.where(is_high, factor(1, -1.0), factor(1, 1.0)),
+        jnp.where(is_high, factor(0, -1.0), factor(0, 1.0)),
+    )
+    factor_t = [
+        jnp.where(across_rows, factor(0, sign), factor(1, sign)) for sign in (1.0, -1.0)
+    ]
+    flow_n = jnp.where(across_rows, mean_flow[1], mean_flow[0])
+    flow_t = jnp.where(across_rows, mean_flow[0], mean_flow[1])
+
+    def flux(x, flow, coupling):
+        source, has = coupling
+        return flow * x + has * jnp.take_along_axis(x, source, axis=1)
+
+    face = [collected(a, 1) for a in range(8)]
+    slope = [collected(a, 2) for a in range(8)]
+    tx_low, tx_high, ty_low, ty_high = traces
+    at = jnp.where(group == 0, pos, jnp.where(group == 1, 12 + pos, 4 * pos))
+    at = base + jnp.where(group == 3, 4 * pos + 3, at)
+    near = []
+    for a in range(8):
+        out = jnp.take_along_axis(tx_low[a], at, axis=1)
+        for g, trace in ((1, tx_high), (2, ty_low), (3, ty_high)):
+            out = jnp.where(group == g, jnp.take_along_axis(trace[a], at, axis=1), out)
+        near.append(out)
+    gap = [n - f for n, f in zip(from_common(tab, near), face)]
+    gap = jump_with(gap, couple_n, factor_n)
+    scale = metric_n * lift * jnp.where(is_high, -1.0, 1.0)
+    rate = [
+        scale * g - metric_n * flux(d, flow_n, couple_n) for g, d in zip(gap, slope)
+    ]
+    by_t = along_first(tab, D_AT, face)
+    by_k = along_second(tab, DK_AT, face)
+    scale_z = metric_z * lift
+    sub = lax.broadcasted_iota(jnp.int32, (8, LANES), 0)
+    weights = tab[pl.ds(W_AT, 8), :]
+    at_low = jnp.where(sub == 0, scale_z, 0.0)
+    at_high = -scale_z * weights
+
+    def at_k(x, k):
+        return jnp.take_along_axis(x, jnp.full((8, LANES), k, jnp.int32), axis=0)
+
+    for a in range(8):
+        low = at_k(face[a], 0)
+        high = row_of(tab, W_AT + PMIN) * at_k(face[a], PMIN)
+        for n in range(PMIN + 1, NQ):
+            high = high + row_of(tab, W_AT + n) * at_k(face[a], n)
+        gap_low = jump_flux([high - low], 2, 1.0)[0]
+        gap_high = jump_flux([low - high], 2, -1.0)[0]
+        rate[a] = (
+            rate[a]
+            - metric_t * flux(by_t[a], flow_t, couple_t)
+            - metric_z * flux(by_k[a], mean_flow[2], by_z)
+            + at_low * gap_low
+            + at_high * gap_high
+        )
+    line_low, line_high = collected(0, 3), collected(1, 3)
+    flip = jnp.where(var == 2, -1.0, 1.0).astype(jnp.float32)
+
+    def corners(side, block_below, block_above):
+        at = base + jnp.where(elem == (4 if side == 0 else 7), 15, 3)
+        if side == 1:
+            at = base + jnp.where(elem == 3, 3, 15)
+        return (
+            jnp.take_along_axis(below[block_below], at, axis=1),
+            jnp.take_along_axis(above[block_above], at, axis=1),
+        )
+
+    from_below, _ = corners(0, 7, 7)
+    at_wall = jnp.where(wall, flip * line_low, from_below)
+    from_below, from_above = corners(0, 6, 6)
+    corner = jnp.where(
+        across_rows, jnp.where(group == 2, from_below, from_above), at_wall
+    )
+    near_low = jnp.where(pos == 0, corner, rolled(line_high, 1))
+    _, beyond = corners(1, 7, 7)
+    from_below, from_above = corners(1, 6, 6)
+    corner = jnp.where(across_rows, jnp.where(group == 2, from_below, from_above), beyond)
+    near_high = jnp.where(pos == 3, corner, rolled(line_low, -1))
+    near_low, near_high = along_second(tab, BK_AT, [near_low, near_high])
+    own_high = row_of(tab, W_AT + PMIN) * face[PMIN]
+    for n in range(PMIN + 1, NQ):
+        own_high = own_high + row_of(tab, W_AT + n) * face[n]
+    scale = metric_t * lift
+    gap_low = scale * jump_with([near_low - face[0]], couple_t, factor_t[0])[0]
+    gap_high = scale * jump_with([near_high - own_high], couple_t, factor_t[1])[0]
+    rate[0] = rate[0] + gap_low
+    for n in range(PMIN, NQ):
+        rate[n] = rate[n] - row_of(tab, W_AT + n) * gap_high
+    middle = [f + time_step * r for f, r in zip(face, rate)]
+    return turned(to_common(tab, middle), codes, q_buf)
+
+
+def from_halo(face):
+    lane, elem, _ = lane_ids()
+    base = lane - elem
+    at_below = base + 8 + (elem >> 2)
+    at_above = base + 12 + (elem >> 2)
+    return (
+        face,
+        [rolled(x, 8) for x in face],
+        [jnp.take_along_axis(x, at_below, axis=1) for x in face],
+        [jnp.take_along_axis(x, at_above, axis=1) for x in face],
+    )
 
 
 def gaps_to(q, tab, lift, traces, arrived, wall, metric, out):
@@ -295,14 +466,14 @@
     low, high = x_faces(q, tab)
     near = [
         jnp.where(elem < 4, r, rolled(t, 4))
-        for r, t in zip(from_left, load_face(tx_high))
+        for r, t in zip(from_left, tx_high)
     ]
     gap = jump_flux([n - o for n, o in zip(from_common(tab, near), low)], 0, 1.0)
     for j in range(8):
         out[node(0, j), :] = out[node(0, j), :] + scale * gap[j]
     near = [
         jnp.where(elem >= 12, r, rolled(t, -4))
-        for r, t in zip(from_right, load_face(tx_low))
+        for r, t in zip(from_right, tx_low)
     ]
     gap = jump_flux([n - o for n, o in zip(from_common(tab, near), high)], 0, -1.0)
     gap = [scale * x for x in gap]
@@ -312,12 +483,12 @@
             out[node(n, j), :] = out[node(n, j), :] - w * gap[j]
     scale = lift * metric[1]
     low, high = y_faces(q, tab)
-    own_low = load_face(ty_low)
+    own_low = ty_low
     flip = jnp.where(var == 2, -1.0, 1.0).astype(jnp.float32)
     first = (elem & 3) == 0
     near = [
         jnp.where(first, jnp.where(wall, flip * o, r), rolled(t, 1))
-        for r, t, o in zip(from_below, load_face(ty_high), own_low)
+        for r, t, o in zip(from_below, ty_high, own_low)
     ]
     gap = jump_flux([n - o for n, o in zip(from_common(tab, near), low)], 1, 1.0)
     for i in range(8):
@@ -390,25 +561,34 @@
     return copies
 
 
-def first_kernel(fields_hbm, orders_hbm, turn_hbm, rows_hbm, core_ref, row_ref, q, tab, *rest):
+def first_kernel(
+    fields_hbm, orders_hbm, turn_hbm, metric_hbm, rows_hbm, core_ref, row_ref, q, tab, *rest
+):
     outs = rest[:8]
-    flat, buf, fields, orders, turn, rows, sems = rest[8:]
+    flat, buf, fields, orders, turn, metric_ref, rows, sems = rest[8:]
     copies = fetched(
-        [(orders_hbm, orders), (turn_hbm, turn), (rows_hbm, rows), (fields_hbm, fields)], sems
+        [
+            (orders_hbm, orders),
+            (turn_hbm, turn),
+            (metric_hbm, metric_ref),
+            (rows_hbm, rows),
+            (fields_hbm, fields),
+        ],
+        sems,
     )
     flat[pl.ds(80, 48), :] = jnp.zeros((48, 512), jnp.float32)
-    copies[0].wait()
-    copies[1].wait()
+    for n in range(3):
+        copies[n].wait()
     order = spread(lambda x, y: orders[x, y], jnp.int32)
     level = lax.broadcasted_iota(jnp.int32, (LANES, LANES), 0) + PMIN
     one_hot = jnp.where(
         level == jnp.broadcast_to(order[0:1, :], (LANES, LANES)), 1.0, 0.0
     ).astype(jnp.float32)
-    copies[2].wait()
+    copies[3].wait()
     tab[...] = jnp.dot(
         rows[...], one_hot, precision=lax.Precision.HIGHEST, preferred_element_type=jnp.float32
     )
-    copies[3].wait()
+    copies[4].wait()
     for v in range(VARS):
         for x in range(4):
             flat[pl.ds(v * 16 + x * 4, 4), :] = fields[x, v]
@@ -422,45 +602,84 @@
                 q[node(part * 2 + half, j), :] = (
                     block[at : at + 8] * in_ik * row_of(tab, A_AT + j)
                 )
-    code_low, code_high = all_codes(turn)
-    make_traces(q, tab, code_low, code_high, places(core_ref, row_ref), outs, buf)
-
-
-def second_kernel(q, tab, metric_hbm, turn_hbm, core_ref, row_ref, *rest):
+    first_core, _ = places(core_ref, row_ref)
+    make_messages(
+        q, tab, order, all_metrics(metric_ref), all_codes(turn), first_core, outs, buf
+    )
+
+
+def second_kernel(up, down, chip, blk, core_ref, row_ref, pair_send, row_send):
+    first_core, even_row = places(core_ref, row_ref)
+    left, right = sides_of(chip, blk, first_core)
+    _, elem, _ = lane_ids()
+    up, down = load_face(up), load_face(down)
+
+    def with_corners(message, edge, y, line):
+        at_left, at_right = elem == 3, elem == 15
+        out = message[:6]
+        out.append(
+            jnp.where(
+                at_left,
+                rolled(left[edge], 3 - y),
+                jnp.where(at_right, rolled(right[edge], 15 - y), message[6]),
+            )
+        )
+        out.append(
+            jnp.where(
+                at_left,
+                rolled(left[line], -9 - y),
+                jnp.where(at_right, rolled(right[line], 3 - y), message[7]),
+            )
+        )
+        return out
+
+    up = with_corners(up, 7, 3, 1)
+    down = with_corners(down, 0, 0, 0)
+    store_face(pair_send, [jnp.where(even_row, u, d) for u, d in zip(up, down)])
+    store_face(row_send, [jnp.where(even_row, d, u) for u, d in zip(up, down)])
+
+
+def third_kernel(
+    q, tab, metric_hbm, turn_hbm, migration_hbm, rows_hbm, core_ref, row_ref, *rest
+):
     traces, arrived = rest[:4], rest[4:8]
-    rate, middle = rest[8], rest[9]
-    outs, buf, metric_ref, turn, sems = rest[10:18], *rest[18:]
-    copies = fetched([(metric_hbm, metric_ref), (turn_hbm, turn)], sems)
-    place = places(core_ref, row_ref)
-    copies[0].wait()
-    copies[1].wait()
+    outs = rest[8:12]
+    (
+        rate, middle, second, flat, slots, count, metric_ref, turn, migration, rows, halo_tab,
+        buf, sems,
+    ) = rest[12:]
+    copies = fetched(
+        [
+            (metric_hbm, metric_ref),
+            (turn_hbm, turn),
+            (migration_hbm, migration),
+            (rows_hbm, rows),
+        ],
+        sems,
+    )
+    first_core, even_row = places(core_ref, row_ref)
+    wall = row_ref[0] == 0
+    for copy in copies:
+        copy.wait()
     metric = all_metrics(metric_ref)
     lift = tab[pl.ds(LIFT_AT, 8), :]
+    chip, blk, pair, row = arrived
+    left, right = sides_of(chip, blk, first_core)
+    below, above = sides_of(pair, row, even_row)
+    own = [load_face(ref) for ref in traces]
+    beside = halo_step((left, right, below, above), own, wall, rows[...], halo_tab, buf)
+    near = (left, [rolled(x, 12) for x in right], below, [rolled(x, 3) for x in above])
     volume_terms(q, tab, metric, rate)
-    gaps_to(
-        q, tab, lift, traces, sorted_arrivals(arrived, place), row_ref[0] == 0, metric, rate
-    )
+    gaps_to(q, tab, lift, own, near, wall, metric, rate)
     for n in range(64):
         at = pl.ds(8 * n, 8)
         middle[at, :] = q[at, :] + time_step * rate[at, :]
-    code_low, code_high = all_codes(turn)
-    make_traces(middle, tab, code_low, code_high, place, outs, buf)
-
-
-def third_kernel(rate, middle, tab, metric_hbm, migration_hbm, core_ref, row_ref, *rest):
-    traces, arrived = rest[:4], rest[4:8]
-    outs = rest[8:12]
-    second, flat, slots, count, metric_ref, migration, sems = rest[12:]
-    copies = fetched([(metric_hbm, metric_ref), (migration_hbm, migration)], sems)
-    place = places(core_ref, row_ref)
-    copies[0].wait()
-    copies[1].wait()
-    metric = all_metrics(metric_ref)
-    lift = tab[pl.ds(LIFT_AT, 8), :]
+    codes = all_codes(turn)
+    x_ends, y_ends = x_faces(middle, tab), y_faces(middle, tab)
+    own = [turned(to_common(tab, x_ends[side]), codes[side], buf) for side in range(2)]
+    own = own + [to_common(tab, y_ends[side]) for side in range(2)]
     volume_terms(middle, tab, metric, second)
-    gaps_to(
-        middle, tab, lift, traces, sorted_arrivals(arrived, place), row_ref[0] == 0, metric, second
-    )
+    gaps_to(middle, tab, lift, own, from_halo(beside), wall, metric, second)
     for part in range(4):
         at = pl.ds(part * LANES, LANES)
         flat[:, 0, at] = ((0.5 * time_step) * (rate[at, :] + second[at, :])).T
@@ -532,13 +751,6 @@
     return lax.all_gather(array, axis, axis_index_groups=pairs_of(lax.axis_size(axis), 0))
 
 
-def exchanged(sends):
-    chip, blk, pair, row = sends
-    blk = swapped(blk, "blk", True)
-    row = swapped(row, "row", False)
-    return [paired(chip, "blk"), blk, paired(pair, "row"), row]
-
-
 def hopped(array, outward):
     count = lax.axis_size("blk")
     step = [-2, 2] if outward else [2, -2]
@@ -563,7 +775,7 @@
     q, tab, *faces = pl.pallas_call(
         first_kernel,
         out_shape=[VOLUME, f32(TAB_ROWS, LANES)] + [FACE] * 8,
-        in_specs=[HBM] * 4 + [SMEM] * 2,
+        in_specs=[HBM] * 5 + [SMEM] * 2,
         out_specs=[VMEM] * 10,
         scratch_shapes=[
             vmem(LANES, 512),
@@ -571,39 +783,48 @@
             vmem(4, VARS, 4, 512),
             pltpu.SMEM((4, 4), jnp.int32),
             turn_at,
+            metric_at,
             vmem(TAB_ROWS, LANES),
-            sems(4),
+            sems(5),
         ],
         compiler_params=PARAMS,
-    )(by_var, orders, face_turn, rows, core, row)
-    arrived = exchanged(faces[4:])
-    rate, middle, *next_faces = pl.pallas_call(
+    )(by_var, orders, face_turn, metric, rows, core, row)
+    chip_send, blk_send, up, down = faces[4:]
+    blk = swapped(blk_send, "blk", True)
+    chip = paired(chip_send, "blk")
+    pair_send, row_send = pl.pallas_call(
         second_kernel,
-        out_shape=[VOLUME, VOLUME] + [FACE] * 8,
-        in_specs=[VMEM] * 2 + [HBM] * 2 + [SMEM] * 2 + [VMEM] * 8,
-        out_specs=[VMEM] * 10,
-        scratch_shapes=[vmem(64, LANES), metric_at, turn_at, sems(2)],
+        out_shape=[FACE] * 2,
+        in_specs=[VMEM] * 4 + [SMEM] * 2,
+        out_specs=[VMEM] * 2,
         compiler_params=PARAMS,
-    )(q, tab, metric, face_turn, core, row, *faces[:4], *arrived)
-    arrived = exchanged(next_faces[4:])
+    )(up, down, chip, blk, core, row)
+    beyond = swapped(row_send, "row", False)
+    pair = paired(pair_send, "row")
     outward, own, same_chip, inward = pl.pallas_call(
         third_kernel,
         out_shape=[f32(n, VARS, 1, 512) for n in (2 * CAP, CAP, CAP, CAP)],
-        in_specs=[VMEM] * 3 + [HBM] * 2 + [SMEM] * 2 + [VMEM] * 8,
+        in_specs=[VMEM] * 2 + [HBM] * 4 + [SMEM] * 2 + [VMEM] * 8,
         out_specs=[VMEM] * 4,
         scratch_shapes=[
+            vmem(512, LANES),
+            vmem(512, LANES),
             vmem(512, LANES),
             vmem(LANES, 1, 512),
             vmem(SPREAD * CAP, VARS, 1, 512),
             pltpu.SMEM((8,), jnp.int32),
             metric_at,
+            turn_at,
             pltpu.SMEM((1, 1, 1, NB), jnp.int32),
-            sems(2),
+            vmem(TAB_ROWS, LANES),
+            vmem(TAB_ROWS, LANES),
+            vmem(64, LANES),
+            sems(4),
         ],
         compiler_params=PARAMS,
     )(
-        rate, middle, tab, metric, jnp.transpose(migration, (0, 1, 3, 2)), core, row,
-        *next_faces[:4], *arrived,
+        q, tab, metric, face_turn, jnp.transpose(migration, (0, 1, 3, 2)), rows, core, row,
+        *faces[:4], chip, blk, pair, beyond,
     )
     far = hopped(outward, True)
     near = hopped(inward, False)

time: 61.2 us -> 46 us (0.75)
  the two profiles are of different devices: /device:TPU:128 before, /device:TPU:1 now
where the time goes in v2:
time: 46 us; the launch traced here: 45.7 us
  blocking collectives  19.8 us (43%)
  starting transfers between devices  14 us (30%)
  Pallas kernels  8.6 us (19%)
  local copies, waits for them, and re-layouts  3.22 us (7%)
    all_gather x4, blocking collectives, paired(): lax.all_gather(array, axis, axis_index_groups=pairs_of(lax.axis_size(axis...  19.8 us
    ppermute x2, starting transfers between devices, hopped(): lax.ppermute(array, 'blk', [(n, (n + step[n % 2]) % count) for n in range...  8.6 us
    pallas_call x1, Pallas kernels, local(): pl.pallas_call(third_kernel, out_shape=[f32(n, VARS, 1, 512) for n in (2...  6.23 us
    ppermute x2, starting transfers between devices, swapped(): return lax.ppermute(array, axis, pairs + [(b, a) for a, b in pairs])  5.38 us
    unnamed x14, local copies, waits for them, and re-layouts  3.22 us
    pallas_call x1, Pallas kernels, local(): pl.pallas_call(first_kernel, out_shape=[VOLUME, f32(TAB_ROWS, LANES)] + [...  1.56 us
  transfers between devices with their start and end apart: 4, of which 0 were waited for; matrix products, arithmetic and copies ran while one was open for 0% of the time, Pallas kernels for 0%

profile of v2, /device:TPU:1, one launch (start us, length us, event | category | flops | bytes accessed | tf_op | source)
XLA Modules:
  0.0 45.7 jit_solution(5402476659707214097)
XLA Ops:
  0.0 0.7 %copy-done.5 = s32[4,4]{1,0:T(4,128)S(1)} copy-done((s32[4,4]{1,0:T(4,128)S(1)}, s32[4,4]{1,0:T(4,128)}, u32[]{:S(2)}) %copy-start.5) | copy-done | bytes 88
  0.7 0.0 copy-done.3
  0.7 0.0 copy-done.4
  0.7 0.9 %copy-done = f32[416,128]{1,0:T(8,128)S(1)} copy-done((f32[416,128]{1,0:T(8,128)S(1)}, f32[416,128]{1,0:T(8,128)}, u32[]{:S(2)}) %copy-start) | copy-done | bytes 213016
  1.7 0.9 %copy-done.2 = f32[4,4,5,512]{3,1,2,0:T(4,128)S(1)} copy-done((f32[4,4,5,512]{3,1,2,0:T(4,128)S(1)}, f32[4,4,5,512]{3,1,2,0:T(4,128)}, u32[]{:S(2)}) %copy-start.2) | copy-done | bytes 163864
  2.6 1.6 %shard_map.64 = (f32[512,128]{1,0:T(8,128)S(1)}, f32[416,128]{1,0:T(8,128)S(1)}, f32[64,128]{1,0:T(8,128)S(1)}, f32[64,128]{1,0:T(8,128)S(1)}, f32[64,128]{1,0:T...) custom-call(f32[4,5,4,512]{3,2,1,0:T(4,128)S(1)} %bitcast.16, ...), custom_call_target="tpu_custom_call" | custom-call | tf_op jit(solution)/shard_map/pallas_call | solution.py:775
  4.1 0.0 copy-start.1
  4.1 4.7 %collective-permute-start = (f32[64,128]{1,0:T(8,128)S(1)}, f32[64,128]{1,0:T(8,128)S(1)}, u32[]{:S(2)}, u32[]{:S(2)}) collective-permute-start(f32[64,128]{1,0:T(8,128)S(1)} %get-tuple-element.28), channel_id=1, source_target_pairs={{12,24},{36,48},{60,72},{84,96},{108,120},{132,144},{156,168},{180... | collective-permute-start | bytes 98312 | tf_op jit(solution)/shard_map/ppermute | solution.py:747
  8.9 9.3 %all-gather = f32[128,128]{1,0:T(8,128)S(1)} all-gather(f32[64,128]{1,0:T(8,128)S(1)} %get-tuple-element.27), channel_id=2, replica_groups={{0,12},{24,36},{48,60},{72,84},{96,108},{120,132},{144,156},{168,180},{..., dimensions={0}, use_global_device_ids=true | all-gather | bytes 98304 | tf_op jit(solution)/shard_map/all_gather | solution.py:751
  18.2 0.0 collective-permute-done.blk.rest_5_
  18.2 0.1 shard_map.65
  18.3 0.7 %collective-permute-start.1 = (f32[64,128]{1,0:T(8,128)S(1)}, f32[64,128]{1,0:T(8,128)S(1)}, u32[]{:S(2)}, u32[]{:S(2)}) collective-permute-start(f32[64,128]{1,0:T(8,128)S(1)} %get-tuple-element.32), channel_id=1, source_target_pairs={{1,2},{3,4},{5,6},{7,8},{9,10},{2,1},{4,3},{6,5},{8,7},{10,9},{13,... | collective-permute-start | bytes 98312 | tf_op jit(solution)/shard_map/ppermute | solution.py:747
  19.0 3.8 %all-gather.1 = f32[128,128]{1,0:T(8,128)S(1)} all-gather(f32[64,128]{1,0:T(8,128)S(1)} %get-tuple-element.31), channel_id=3, replica_groups={{0,1},{2,3},{4,5},{6,7},{8,9},{10,11},{12,13},{14,15},{16,17},{18,19},{..., dimensions={0}, use_global_device_ids=true | all-gather | bytes 98304 | tf_op jit(solution)/shard_map/all_gather | solution.py:751
  22.7 0.0 collective-permute-done.1.rest_7_
  22.7 0.0 copy-done.1
  22.7 0.6 %copy-done.6 = s32[1,1,16,1]{2,3,1,0:T(1,128)S(1)} copy-done((s32[1,1,16,1]{2,3,1,0:T(1,128)S(1)}, s32[1,1,16,1]{2,3,1,0:T(1,128)}, u32[]{:S(2)}) %copy-start.6) | copy-done | bytes 88
  23.4 6.2 %shard_map.66 = (f32[10,5,1,512]{3,2,1,0:T(1,128)S(1)}, f32[5,5,1,512]{3,2,1,0:T(1,128)S(1)}, f32[5,5,1,512]{3,2,1,0:T(1,128)S(1)}, f32[5,5,1,512]{3,2,1,0:T(1,128)S(1)}) custom-call(f32[512,128]{1,0:T(8,128)S(1)} %get-tuple-element.21.q, f32[416,128]{1,0:T(8,128)S(1)} %get-tuple-element.22.tab, f32[3,4,4]{2,1,0:T(4,128)S(1)} %copy-done.3, ...), custom_call_target="tpu_custom_call" | custom-call | tf_op jit(solution)/shard_map/pallas_call | solution.py:804
  29.6 1.9 %collective-permute-start.2 = (f32[10,5,1,512]{3,2,1,0:T(1,128)S(1)}, f32[10,5,1,512]{3,2,1,0:T(1,128)S(1)}, u32[]{:S(2)}, u32[]{:S(2)}) collective-permute-start(f32[10,5,1,512]{3,2,1,0:T(1,128)S(1)} %get-tuple-element.33), channel_id=1, source_target_pairs={{0,744},{12,36},{24,0},{36,60},{48,24},{60,84},{72,48},{84,108},{9... | collective-permute-start | bytes 307208 | tf_op jit(solution)/shard_map/ppermute | solution.py:757
  31.6 6.7 %collective-permute-start.3 = (f32[5,5,1,512]{3,2,1,0:T(1,128)S(1)}, f32[5,5,1,512]{3,2,1,0:T(1,128)S(1)}, u32[]{:S(2)}, u32[]{:S(2)}) collective-permute-start(f32[5,5,1,512]{3,2,1,0:T(1,128)S(1)} %get-tuple-element.35), channel_id=1, source_target_pairs={{0,24},{12,756},{24,48},{36,12},{48,72},{60,36},{72,96},{84,60},{9... | collective-permute-start | bytes 153608 | tf_op jit(solution)/shard_map/ppermute | solution.py:757
  38.3 4.7 %all-gather.2 = f32[10,5,1,512]{3,2,1,0:T(1,128)S(1)} all-gather(f32[5,5,1,512]{3,2,1,0:T(1,128)S(1)} %get-tuple-element.36), channel_id=4, replica_groups={{0,12},{24,36},{48,60},{72,84},{96,108},{120,132},{144,156},{168,180},{..., dimensions={0}, use_global_device_ids=true | all-gather | bytes 153600 | tf_op jit(solution)/shard_map/all_gather | solution.py:751
  43.0 0.0 collective-permute-done.2.far
  43.0 1.9 %all-gather.3 = f32[20,5,1,512]{3,2,1,0:T(1,128)S(1)} all-gather(f32[10,5,1,512]{3,2,1,0:T(1,128)S(1)} %collective-permute-done.2.far), channel_id=5, replica_groups={{0,12},{24,36},{48,60},{72,84},{96,108},{120,132},{144,156},{168,180},{..., dimensions={0}, use_global_device_ids=true | all-gather | bytes 307200 | tf_op jit(solution)/shard_map/all_gather | solution.py:751
  44.9 0.0 collective-permute-done.3.near
  44.9 0.7 %shard_map.67 = f32[25,5,1,512]{3,2,1,0:T(1,128)} custom-call(f32[10,5,1,512]{3,2,1,0:T(1,128)S(1)} %collective-permute-done.2.far, f32[5,5,1,512]{3,2,1,0:T(1,128)S(1)} %get-tuple-element.34.own, f32[5,5,1,512]{3,2,1,0:T(1,128)S(1)} %collective-permute-done.3.near, s32[1]{0:T(128)} %bitcast.1.core_ref, f32[2,5,5,1,512]{4,3,2,1,0:T(1,128)S(1)} %bitcast.14, ...), custom_call_target="tpu_custom_call" | custom-call | tf_op jit(solution)/shard_map/pallas_call | solution.py:833
  (6 shorter events, 0.0 us)
Async XLA Ops:
  0.0 0.7 %copy-start.5 = (s32[4,4]{1,0:T(4,128)S(1)}, s32[4,4]{1,0:T(4,128)}, u32[]{:S(2)}) copy-start(s32[4,4]{1,0:T(4,128)} %orders_hbm.1) | copy-start | bytes 196
  0.0 0.7 %copy-start.3 = (f32[3,4,4]{2,1,0:T(4,128)S(1)}, f32[3,4,4]{2,1,0:T(4,128)}, u32[]{:S(2)}) copy-start(f32[3,4,4]{2,1,0:T(4,128)} %metric_hbm.3) | copy-start | bytes 580
  0.0 0.7 %copy-start.4 = (s32[2,4,4]{2,1,0:T(4,128)S(1)}, s32[2,4,4]{2,1,0:T(4,128)}, u32[]{:S(2)}) copy-start(s32[2,4,4]{2,1,0:T(4,128)} %turn_hbm.3) | copy-start | bytes 388
  0.7 0.9 %copy-start = (f32[416,128]{1,0:T(8,128)S(1)}, f32[416,128]{1,0:T(8,128)}, u32[]{:S(2)}) copy-start(f32[416,128]{1,0:T(8,128)} %constant.13.clone.rows_hbm) | copy-start | bytes 638980
  1.7 0.9 %copy-start.2 = (f32[4,4,5,512]{3,1,2,0:T(4,128)S(1)}, f32[4,4,5,512]{3,1,2,0:T(4,128)}, u32[]{:S(2)}) copy-start(f32[4,4,5,512]{3,1,2,0:T(4,128)} %param.6) | copy-start | bytes 491524
  4.1 18.6 %copy-start.1 = (f32[416,128]{1,0:T(8,128)S(1)}, f32[416,128]{1,0:T(8,128)}, u32[]{:S(2)}) copy-start(f32[416,128]{1,0:T(8,128)} %constant.13.clone.rows_hbm) | copy-start | bytes 638980
  4.1 14.1 %collective-permute-start = (f32[64,128]{1,0:T(8,128)S(1)}, f32[64,128]{1,0:T(8,128)S(1)}, u32[]{:S(2)}, u32[]{:S(2)}) collective-permute-start(f32[64,128]{1,0:T(8,128)S(1)} %get-tuple-element.28), channel_id=1, source_target_pairs={{12,24},{36,48},{60,72},{84,96},{108,120},{132,144},{156,168},{180... | collective-permute-start | bytes 98312 | tf_op jit(solution)/shard_map/ppermute | solution.py:747
  18.3 4.4 %collective-permute-start.1 = (f32[64,128]{1,0:T(8,128)S(1)}, f32[64,128]{1,0:T(8,128)S(1)}, u32[]{:S(2)}, u32[]{:S(2)}) collective-permute-start(f32[64,128]{1,0:T(8,128)S(1)} %get-tuple-element.32), channel_id=1, source_target_pairs={{1,2},{3,4},{5,6},{7,8},{9,10},{2,1},{4,3},{6,5},{8,7},{10,9},{13,... | collective-permute-start | bytes 98312 | tf_op jit(solution)/shard_map/ppermute | solution.py:747
  22.7 0.7 %copy-start.6 = (s32[1,1,16,1]{2,3,1,0:T(1,128)S(1)}, s32[1,1,16,1]{2,3,1,0:T(1,128)}, u32[]{:S(2)}) copy-start(s32[1,1,16,1]{2,3,1,0:T(1,128)} %param.10) | copy-start | bytes 196
  29.6 13.3 %collective-permute-start.2 = (f32[10,5,1,512]{3,2,1,0:T(1,128)S(1)}, f32[10,5,1,512]{3,2,1,0:T(1,128)S(1)}, u32[]{:S(2)}, u32[]{:S(2)}) collective-permute-start(f32[10,5,1,512]{3,2,1,0:T(1,128)S(1)} %get-tuple-element.33), channel_id=1, source_target_pairs={{0,744},{12,36},{24,0},{36,60},{48,24},{60,84},{72,48},{84,108},{9... | collective-permute-start | bytes 307208 | tf_op jit(solution)/shard_map/ppermute | solution.py:757
  31.6 13.4 %collective-permute-start.3 = (f32[5,5,1,512]{3,2,1,0:T(1,128)S(1)}, f32[5,5,1,512]{3,2,1,0:T(1,128)S(1)}, u32[]{:S(2)}, u32[]{:S(2)}) collective-permute-start(f32[5,5,1,512]{3,2,1,0:T(1,128)S(1)} %get-tuple-element.35), channel_id=1, source_target_pairs={{0,24},{12,756},{24,48},{36,12},{48,72},{60,36},{72,96},{84,60},{9... | collective-permute-start | bytes 153608 | tf_op jit(solution)/shard_map/ppermute | solution.py:757

commit v3 on v2

--- a/solution.py
+++ b/solution.py
@@ -1,7 +1,6 @@
-import functools
-
 import jax
 import jax.numpy as jnp
+import ml_dtypes
 import numpy as np
 from jax import lax
 from jax.experimental import pallas as pl
@@ -99,9 +98,9 @@
 TAB_ROWS = 416
 
 
-def table_rows():
+def table_columns():
     derive, to_grid, from_grid, lifting, last_node, active = build_tables(PMIN, PMAX)
-    rows = np.zeros((TAB_ROWS, LANES))
+    rows = np.zeros((4 * LANES, 8))
     for level in range(PMAX - PMIN + 1):
         for at, turned_at, mat in (
             (D_AT, DK_AT, derive[level]),
@@ -116,7 +115,11 @@
         rows[A_AT : A_AT + 8, level] = active[level]
         rows[LIFT_AT : LIFT_AT + 8, level] = lifting[level]
         rows[DLAST_AT : DLAST_AT + 8, level] = derive[level][PMIN + level]
-    return rows.astype(np.float32)
+    left, parts = rows.T.astype(np.float32), []
+    for _ in range(3):
+        parts.append(left.astype(ml_dtypes.bfloat16).astype(np.float32))
+        left = left - parts[-1]
+    return np.concatenate(parts)
 
 
 def lane_ids():
@@ -313,7 +316,7 @@
     return core_ref[0] == 0, lax.rem(row_ref[0], 2) == 0
 
 
-def halo_step(messages, traces, wall, rows, tab, q_buf):
+def halo_step(messages, traces, wall, columns, tab, q_buf):
     left, right, below, above = messages
     lane, elem, var = lane_ids()
     group, pos = elem >> 2, elem & 3
@@ -328,14 +331,7 @@
             out = jnp.where(group == g, jnp.take_along_axis(message[block], at, axis=1), out)
         return out
 
-    order = collected(2, 3)
-    level = lax.broadcasted_iota(jnp.int32, (LANES, LANES), 0) + PMIN
-    one_hot = jnp.where(
-        level.astype(jnp.float32) == jnp.broadcast_to(order[0:1, :], (LANES, LANES)), 1.0, 0.0
-    ).astype(jnp.float32)
-    tab[...] = jnp.dot(
-        rows, one_hot, precision=lax.Precision.HIGHEST, preferred_element_type=jnp.float32
-    )
+    table_for(columns, collected(2, 3)[0:1, :], tab)
     lift = tab[pl.ds(LIFT_AT, 8), :]
     metric_x, metric_y, metric_z = [collected(3 + d, 3) for d in range(3)]
     metric_n = jnp.where(across_rows, metric_y, metric_x)
@@ -503,6 +499,9 @@
         w = row_of(tab, W_AT + n)
         for i in range(8):
             out[node(i, n), :] = out[node(i, n), :] - w * gap[i]
+
+
+def span_terms(q, tab, lift, metric, out):
     scale = lift * metric[2]
     low, high = z_faces(q, tab)
     gap_low = jump_flux([h - o for h, o in zip(high, low)], 2, 1.0)
@@ -527,23 +526,16 @@
         mixed = has * jnp.take_along_axis(y, source, axis=1)
         return mixed if mean_flow[d] == 0.0 else mean_flow[d] * y + mixed
 
-    def along_x(j, carry):
+    for j in range(8):
         face = [q[node(i, j), :] for i in range(8)]
         for i, x in enumerate(along_first(tab, D_AT, face)):
             out[node(i, j), :] = -flux(x, 0)
-        return carry
-
-    lax.fori_loop(0, 8, along_x, 0)
-
-    def along_yz(i, carry):
+    for i in range(8):
         face = [q[node(i, j), :] for j in range(8)]
         by_y = along_first(tab, D_AT, face)
         by_z = along_second(tab, DK_AT, face)
         for j in range(8):
             out[node(i, j), :] = out[node(i, j), :] - (flux(by_y[j], 1) + flux(by_z[j], 2))
-        return carry
-
-    lax.fori_loop(0, 8, along_yz, 0)
 
 
 def all_metrics(metric_ref):
@@ -552,6 +544,29 @@
 
 def all_codes(turn_ref):
     return [spread(lambda x, y, s=s: turn_ref[s, x, y], jnp.int32) for s in range(2)]
+
+
+def kept_metrics(params):
+    return [params[pl.ds(8 * d, 8), :] for d in range(3)]
+
+
+def kept_codes(params):
+    return [params[pl.ds(24 + 8 * s, 8), :].astype(jnp.int32) for s in range(2)]
+
+
+def table_for(columns, level_row, tab):
+    level = (lax.broadcasted_iota(jnp.int32, (LANES, LANES), 0) & 7) + PMIN
+    one_hot = jnp.where(
+        level.astype(jnp.float32) == jnp.broadcast_to(level_row, (LANES, LANES)), 1.0, 0.0
+    ).astype(jnp.bfloat16)
+    pad = jnp.zeros((LANES - 24, LANES), jnp.float32)
+    for part in range(4):
+        at = part * LANES
+        size = min(LANES, TAB_ROWS - at)
+        block = jnp.concatenate([columns[:, pl.ds(at, LANES)], pad], axis=0).T
+        tab[pl.ds(at, size), :] = jnp.dot(
+            block.astype(jnp.bfloat16), one_hot, preferred_element_type=jnp.float32
+        )[:size]
 
 
 def fetched(pairs, sems):
@@ -562,36 +577,24 @@
 
 
 def first_kernel(
-    fields_hbm, orders_hbm, turn_hbm, metric_hbm, rows_hbm, core_ref, row_ref, q, tab, *rest
+    fields, columns, orders_hbm, turn_hbm, metric_hbm, core_ref, row_ref, q, tab, params, *rest
 ):
     outs = rest[:8]
-    flat, buf, fields, orders, turn, metric_ref, rows, sems = rest[8:]
+    flat, buf, orders, turn, metric_ref, sems = rest[8:]
     copies = fetched(
-        [
-            (orders_hbm, orders),
-            (turn_hbm, turn),
-            (metric_hbm, metric_ref),
-            (rows_hbm, rows),
-            (fields_hbm, fields),
-        ],
-        sems,
+        [(orders_hbm, orders), (turn_hbm, turn), (metric_hbm, metric_ref)], sems
     )
     flat[pl.ds(80, 48), :] = jnp.zeros((48, 512), jnp.float32)
-    for n in range(3):
-        copies[n].wait()
-    order = spread(lambda x, y: orders[x, y], jnp.int32)
-    level = lax.broadcasted_iota(jnp.int32, (LANES, LANES), 0) + PMIN
-    one_hot = jnp.where(
-        level == jnp.broadcast_to(order[0:1, :], (LANES, LANES)), 1.0, 0.0
-    ).astype(jnp.float32)
-    copies[3].wait()
-    tab[...] = jnp.dot(
-        rows[...], one_hot, precision=lax.Precision.HIGHEST, preferred_element_type=jnp.float32
-    )
-    copies[4].wait()
     for v in range(VARS):
         for x in range(4):
             flat[pl.ds(v * 16 + x * 4, 4), :] = fields[x, v]
+    for copy in copies:
+        copy.wait()
+    order = spread(lambda x, y: orders[x, y].astype(jnp.float32), jnp.float32)
+    metric, codes = all_metrics(metric_ref), all_codes(turn)
+    for n, x in enumerate(metric + codes):
+        params[pl.ds(8 * n, 8), :] = x.astype(jnp.float32)
+    table_for(columns, order[0:1, :], tab)
     in_k = tab[pl.ds(A_AT, 8), :]
     for part in range(4):
         block = flat[:, pl.ds(part * LANES, LANES)].T
@@ -603,12 +606,16 @@
                     block[at : at + 8] * in_ik * row_of(tab, A_AT + j)
                 )
     first_core, _ = places(core_ref, row_ref)
-    make_messages(
-        q, tab, order, all_metrics(metric_ref), all_codes(turn), first_core, outs, buf
-    )
-
-
-def second_kernel(up, down, chip, blk, core_ref, row_ref, pair_send, row_send):
+    make_messages(q, tab, order, metric, codes, first_core, outs, buf)
+
+
+def inner_kernel(q, tab, params, rate):
+    metric = kept_metrics(params)
+    volume_terms(q, tab, metric, rate)
+    span_terms(q, tab, tab[pl.ds(LIFT_AT, 8), :], metric, rate)
+
+
+def second_kernel(up, down, chip, blk, inner, core_ref, row_ref, pair_send, row_send):
     first_core, even_row = places(core_ref, row_ref)
     left, right = sides_of(chip, blk, first_core)
     _, elem, _ = lane_ids()
@@ -639,47 +646,33 @@
     store_face(row_send, [jnp.where(even_row, d, u) for u, d in zip(up, down)])
 
 
-def third_kernel(
-    q, tab, metric_hbm, turn_hbm, migration_hbm, rows_hbm, core_ref, row_ref, *rest
-):
+def third_kernel(q, tab, params, inner, columns, migration_hbm, core_ref, row_ref, *rest):
     traces, arrived = rest[:4], rest[4:8]
     outs = rest[8:12]
-    (
-        rate, middle, second, flat, slots, count, metric_ref, turn, migration, rows, halo_tab,
-        buf, sems,
-    ) = rest[12:]
-    copies = fetched(
-        [
-            (metric_hbm, metric_ref),
-            (turn_hbm, turn),
-            (migration_hbm, migration),
-            (rows_hbm, rows),
-        ],
-        sems,
-    )
+    rate, middle, second, flat, slots, count, migration, halo_tab, buf, sems = rest[12:]
+    copies = fetched([(migration_hbm, migration)], sems)
     first_core, even_row = places(core_ref, row_ref)
     wall = row_ref[0] == 0
-    for copy in copies:
-        copy.wait()
-    metric = all_metrics(metric_ref)
+    metric, codes = kept_metrics(params), kept_codes(params)
     lift = tab[pl.ds(LIFT_AT, 8), :]
     chip, blk, pair, row = arrived
     left, right = sides_of(chip, blk, first_core)
     below, above = sides_of(pair, row, even_row)
     own = [load_face(ref) for ref in traces]
-    beside = halo_step((left, right, below, above), own, wall, rows[...], halo_tab, buf)
+    beside = halo_step((left, right, below, above), own, wall, columns, halo_tab, buf)
     near = (left, [rolled(x, 12) for x in right], below, [rolled(x, 3) for x in above])
-    volume_terms(q, tab, metric, rate)
+    rate[...] = inner[...]
     gaps_to(q, tab, lift, own, near, wall, metric, rate)
     for n in range(64):
         at = pl.ds(8 * n, 8)
         middle[at, :] = q[at, :] + time_step * rate[at, :]
-    codes = all_codes(turn)
     x_ends, y_ends = x_faces(middle, tab), y_faces(middle, tab)
     own = [turned(to_common(tab, x_ends[side]), codes[side], buf) for side in range(2)]
     own = own + [to_common(tab, y_ends[side]) for side in range(2)]
     volume_terms(middle, tab, metric, second)
+    span_terms(middle, tab, lift, metric, second)
     gaps_to(middle, tab, lift, own, from_halo(beside), wall, metric, second)
+    copies[0].wait()
     for part in range(4):
         at = pl.ds(part * LANES, LANES)
         flat[:, 0, at] = ((0.5 * time_step) * (rate[at, :] + second[at, :])).T
@@ -769,42 +762,48 @@
     by_var = jnp.transpose(fields, (0, 2, 1, 3))
     core = lax.rem(lax.axis_index("blk").astype(jnp.int32), 2).reshape(1)
     row = lax.axis_index("row").astype(jnp.int32).reshape(1)
-    rows = jnp.asarray(table_rows())
-    metric_at = pltpu.SMEM((3, 4, 4), jnp.float32)
-    turn_at = pltpu.SMEM((2, 4, 4), jnp.int32)
-    q, tab, *faces = pl.pallas_call(
+    columns = jnp.asarray(table_columns())
+    q, tab, params, *faces = pl.pallas_call(
         first_kernel,
-        out_shape=[VOLUME, f32(TAB_ROWS, LANES)] + [FACE] * 8,
-        in_specs=[HBM] * 5 + [SMEM] * 2,
-        out_specs=[VMEM] * 10,
+        out_shape=[VOLUME, f32(TAB_ROWS, LANES), f32(40, LANES)] + [FACE] * 8,
+        in_specs=[VMEM] * 2 + [HBM] * 3 + [SMEM] * 2,
+        out_specs=[VMEM] * 11,
         scratch_shapes=[
             vmem(LANES, 512),
             vmem(64, LANES),
-            vmem(4, VARS, 4, 512),
             pltpu.SMEM((4, 4), jnp.int32),
-            turn_at,
-            metric_at,
-            vmem(TAB_ROWS, LANES),
-            sems(5),
+            pltpu.SMEM((2, 4, 4), jnp.int32),
+            pltpu.SMEM((3, 4, 4), jnp.float32),
+            sems(3),
         ],
         compiler_params=PARAMS,
-    )(by_var, orders, face_turn, metric, rows, core, row)
+    )(by_var, columns, orders, face_turn, metric, core, row)
     chip_send, blk_send, up, down = faces[4:]
     blk = swapped(blk_send, "blk", True)
     chip = paired(chip_send, "blk")
+    inner = pl.pallas_call(
+        inner_kernel,
+        out_shape=VOLUME,
+        in_specs=[VMEM] * 3,
+        out_specs=VMEM,
+        compiler_params=PARAMS,
+        cost_estimate=pl.CostEstimate(
+            flops=40_000_000, bytes_accessed=6_000_000, transcendentals=0
+        ),
+    )(q, tab, params)
     pair_send, row_send = pl.pallas_call(
         second_kernel,
         out_shape=[FACE] * 2,
-        in_specs=[VMEM] * 4 + [SMEM] * 2,
+        in_specs=[VMEM] * 4 + [ANY] + [SMEM] * 2,
         out_specs=[VMEM] * 2,
         compiler_params=PARAMS,
-    )(up, down, chip, blk, core, row)
+    )(up, down, chip, blk, inner, core, row)
     beyond = swapped(row_send, "row", False)
     pair = paired(pair_send, "row")
     outward, own, same_chip, inward = pl.pallas_call(
         third_kernel,
         out_shape=[f32(n, VARS, 1, 512) for n in (2 * CAP, CAP, CAP, CAP)],
-        in_specs=[VMEM] * 2 + [HBM] * 4 + [SMEM] * 2 + [VMEM] * 8,
+        in_specs=[VMEM] * 5 + [HBM] + [SMEM] * 2 + [VMEM] * 8,
         out_specs=[VMEM] * 4,
         scratch_shapes=[
             vmem(512, LANES),
@@ -813,17 +812,14 @@
             vmem(LANES, 1, 512),
             vmem(SPREAD * CAP, VARS, 1, 512),
             pltpu.SMEM((8,), jnp.int32),
-            metric_at,
-            turn_at,
             pltpu.SMEM((1, 1, 1, NB), jnp.int32),
             vmem(TAB_ROWS, LANES),
-            vmem(TAB_ROWS, LANES),
             vmem(64, LANES),
-            sems(4),
+            sems(1),
         ],
         compiler_params=PARAMS,
     )(
-        q, tab, metric, face_turn, jnp.transpose(migration, (0, 1, 3, 2)), rows, core, row,
+        q, tab, params, inner, columns, jnp.transpose(migration, (0, 1, 3, 2)), core, row,
         *faces[:4], chip, blk, pair, beyond,
     )
     far = hopped(outward, True)

time: 46 us -> 42.1 us (0.915)
  Pallas kernels: 8.6 us -> 5.72 us
  blocking collectives: 19.8 us -> 18.8 us
    pallas_call x1, Pallas kernels: 6.23 us -> 2.82 us  [local(): pl.pallas_call(third_kernel, out_shape=[f32(n, VARS, 1, 512) for n in (2...]
    all_gather x4, blocking collectives: 19.8 us -> 18.8 us  [paired(): lax.all_gather(array, axis, axis_index_groups=pairs_of(lax.axis_size(axis...]
    pallas_call x1 -> x2, Pallas kernels: 1.56 us -> 2.09 us  [the longest x1 1.38 us: local(): pl.pallas_call(first_kernel, out_shape=[VOLUME, f32(TAB_ROWS, LANES), f32...]
    unnamed x14 -> x12, local copies, waits for them, and re-layouts: 3.22 us -> 3.08 us
  transfers between devices with their start and end apart: 4 -> 4, of which waited for: 0 -> 0; matrix products, arithmetic and copies ran while one was open for 0% -> 0% of each run, Pallas kernels for 0% -> 2%
where the time goes in v3:
time: 42.1 us; the launch traced here: 41.8 us
  blocking collectives  18.8 us (45%)
  starting transfers between devices  14.1 us (33%)
  Pallas kernels  5.72 us (14%)
  local copies, waits for them, and re-layouts  3.08 us (7%)
    all_gather x4, blocking collectives, paired(): lax.all_gather(array, axis, axis_index_groups=pairs_of(lax.axis_size(axis...  18.8 us
    ppermute x2, starting transfers between devices, hopped(): lax.ppermute(array, 'blk', [(n, (n + step[n % 2]) % count) for n in range...  8.81 us
    ppermute x2, starting transfers between devices, swapped(): return lax.ppermute(array, axis, pairs + [(b, a) for a, b in pairs])  5.25 us
    unnamed x12, local copies, waits for them, and re-layouts  3.08 us
    pallas_call x1, Pallas kernels, local(): pl.pallas_call(third_kernel, out_shape=[f32(n, VARS, 1, 512) for n in (2...  2.82 us
    pallas_call x1, Pallas kernels, local(): pl.pallas_call(first_kernel, out_shape=[VOLUME, f32(TAB_ROWS, LANES), f32...  1.38 us
  transfers between devices with their start and end apart: 4, of which 0 were waited for; matrix products, arithmetic and copies ran while one was open for 0% of the time, Pallas kernels for 2%

profile of v3, /device:TPU:1, one launch (start us, length us, event | category | flops | bytes accessed | tf_op | source)
XLA Modules:
  0.0 41.8 jit_solution(14265937666546580473)
XLA Ops:
  0.0 0.0 copy-start.4
  0.0 0.7 %copy-done.4 = s32[4,4]{1,0:T(4,128)S(1)} copy-done((s32[4,4]{1,0:T(4,128)S(1)}, s32[4,4]{1,0:T(4,128)}, u32[]{:S(2)}) %copy-start.4) | copy-done | bytes 88
  0.7 0.0 copy-done.2
  0.7 0.0 copy-done.3
  0.7 0.8 %copy-done = f32[24,512]{1,0:T(8,128)S(1)} copy-done((f32[24,512]{1,0:T(8,128)S(1)}, f32[24,512]{1,0:T(8,128)}, u32[]{:S(2)}) %copy-start) | copy-done | bytes 49176
  1.5 0.9 %copy-done.1 = f32[4,4,5,512]{3,1,2,0:T(4,128)S(1)} copy-done((f32[4,4,5,512]{3,1,2,0:T(4,128)S(1)}, f32[4,4,5,512]{3,1,2,0:T(4,128)}, u32[]{:S(2)}) %copy-start.1) | copy-done | bytes 163864
  2.4 1.4 %shard_map.64 = (f32[512,128]{1,0:T(8,128)S(1)}, f32[416,128]{1,0:T(8,128)S(1)}, f32[40,128]{1,0:T(8,128)S(1)}, f32[64,128]{1,0:T(8,128)S(1)}, f32[64,128]{1,0:T...) custom-call(f32[4,5,4,512]{3,2,1,0:T(4,128)S(1)} %bitcast.16, ...), custom_call_target="tpu_custom_call" | custom-call | tf_op jit(solution)/shard_map/pallas_call | solution.py:766
  3.8 4.6 %collective-permute-start = (f32[64,128]{1,0:T(8,128)S(1)}, f32[64,128]{1,0:T(8,128)S(1)}, u32[]{:S(2)}, u32[]{:S(2)}) collective-permute-start(f32[64,128]{1,0:T(8,128)S(1)} %get-tuple-element.30), channel_id=1, source_target_pairs={{12,24},{36,48},{60,72},{84,96},{108,120},{132,144},{156,168},{180... | collective-permute-start | bytes 98312 | tf_op jit(solution)/shard_map/ppermute | solution.py:740
  8.4 0.7 %shard_map.65.inner = f32[512,128]{1,0:T(8,128)S(1)} custom-call(f32[512,128]{1,0:T(8,128)S(1)} %get-tuple-element.22.q, f32[416,128]{1,0:T(8,128)S(1)} %get-tuple-element.23.tab, f32[40,128]{1,0:T(8,128)S(1)} %get-tuple-element.24.params), custom_call_target="tpu_custom_call" | custom-call | flops 40000000 | bytes 6000000 | tf_op jit(solution)/shard_map/pallas_call | solution.py:784
  9.1 9.3 %all-gather = f32[128,128]{1,0:T(8,128)S(1)} all-gather(f32[64,128]{1,0:T(8,128)S(1)} %get-tuple-element.29), channel_id=2, replica_groups={{0,12},{24,36},{48,60},{72,84},{96,108},{120,132},{144,156},{168,180},{..., dimensions={0}, use_global_device_ids=true | all-gather | bytes 98304 | tf_op jit(solution)/shard_map/all_gather | solution.py:744
  18.5 0.0 collective-permute-done.blk.rest_5_
  18.5 0.1 shard_map.66
  18.6 0.7 %collective-permute-start.1 = (f32[64,128]{1,0:T(8,128)S(1)}, f32[64,128]{1,0:T(8,128)S(1)}, u32[]{:S(2)}, u32[]{:S(2)}) collective-permute-start(f32[64,128]{1,0:T(8,128)S(1)} %get-tuple-element.34), channel_id=1, source_target_pairs={{1,2},{3,4},{5,6},{7,8},{9,10},{2,1},{4,3},{6,5},{8,7},{10,9},{13,... | collective-permute-start | bytes 98312 | tf_op jit(solution)/shard_map/ppermute | solution.py:740
  19.2 3.5 %all-gather.1 = f32[128,128]{1,0:T(8,128)S(1)} all-gather(f32[64,128]{1,0:T(8,128)S(1)} %get-tuple-element.33), channel_id=3, replica_groups={{0,1},{2,3},{4,5},{6,7},{8,9},{10,11},{12,13},{14,15},{16,17},{18,19},{..., dimensions={0}, use_global_device_ids=true | all-gather | bytes 98304 | tf_op jit(solution)/shard_map/all_gather | solution.py:744
  22.7 0.0 collective-permute-done.1.rest_7_
  22.7 0.7 %copy-done.5 = s32[1,1,16,1]{2,3,1,0:T(1,128)S(1)} copy-done((s32[1,1,16,1]{2,3,1,0:T(1,128)S(1)}, s32[1,1,16,1]{2,3,1,0:T(1,128)}, u32[]{:S(2)}) %copy-start.5) | copy-done | bytes 88
  23.4 2.8 %shard_map.67 = (f32[10,5,1,512]{3,2,1,0:T(1,128)S(1)}, f32[5,5,1,512]{3,2,1,0:T(1,128)S(1)}, f32[5,5,1,512]{3,2,1,0:T(1,128)S(1)}, f32[5,5,1,512]{3,2,1,0:T(1,128)S(1)}) custom-call(f32[512,128]{1,0:T(8,128)S(1)} %get-tuple-element.22.q, f32[416,128]{1,0:T(8,128)S(1)} %get-tuple-element.23.tab, f32[40,128]{1,0:T(8,128)S(1)} %get-tuple-element.24.params, ...), custom_call_target="tpu_custom_call" | custom-call | tf_op jit(solution)/shard_map/pallas_call | solution.py:803
  26.2 1.9 %collective-permute-start.2 = (f32[10,5,1,512]{3,2,1,0:T(1,128)S(1)}, f32[10,5,1,512]{3,2,1,0:T(1,128)S(1)}, u32[]{:S(2)}, u32[]{:S(2)}) collective-permute-start(f32[10,5,1,512]{3,2,1,0:T(1,128)S(1)} %get-tuple-element.35), channel_id=1, source_target_pairs={{0,744},{12,36},{24,0},{36,60},{48,24},{60,84},{72,48},{84,108},{9... | collective-permute-start | bytes 307208 | tf_op jit(solution)/shard_map/ppermute | solution.py:750
  28.1 6.9 %collective-permute-start.3 = (f32[5,5,1,512]{3,2,1,0:T(1,128)S(1)}, f32[5,5,1,512]{3,2,1,0:T(1,128)S(1)}, u32[]{:S(2)}, u32[]{:S(2)}) collective-permute-start(f32[5,5,1,512]{3,2,1,0:T(1,128)S(1)} %get-tuple-element.37), channel_id=1, source_target_pairs={{0,24},{12,756},{24,48},{36,12},{48,72},{60,36},{72,96},{84,60},{9... | collective-permute-start | bytes 153608 | tf_op jit(solution)/shard_map/ppermute | solution.py:750
  35.0 4.1 %all-gather.2 = f32[10,5,1,512]{3,2,1,0:T(1,128)S(1)} all-gather(f32[5,5,1,512]{3,2,1,0:T(1,128)S(1)} %get-tuple-element.38), channel_id=4, replica_groups={{0,12},{24,36},{48,60},{72,84},{96,108},{120,132},{144,156},{168,180},{..., dimensions={0}, use_global_device_ids=true | all-gather | bytes 153600 | tf_op jit(solution)/shard_map/all_gather | solution.py:744
  39.1 0.0 collective-permute-done.2.far
  39.1 1.9 %all-gather.3 = f32[20,5,1,512]{3,2,1,0:T(1,128)S(1)} all-gather(f32[10,5,1,512]{3,2,1,0:T(1,128)S(1)} %collective-permute-done.2.far), channel_id=5, replica_groups={{0,12},{24,36},{48,60},{72,84},{96,108},{120,132},{144,156},{168,180},{..., dimensions={0}, use_global_device_ids=true | all-gather | bytes 307200 | tf_op jit(solution)/shard_map/all_gather | solution.py:744
  41.0 0.0 collective-permute-done.3.near
  41.1 0.7 %shard_map.68 = f32[25,5,1,512]{3,2,1,0:T(1,128)} custom-call(f32[10,5,1,512]{3,2,1,0:T(1,128)S(1)} %collective-permute-done.2.far, f32[5,5,1,512]{3,2,1,0:T(1,128)S(1)} %get-tuple-element.36.own, f32[5,5,1,512]{3,2,1,0:T(1,128)S(1)} %collective-permute-done.3.near, s32[1]{0:T(128)} %bitcast.1.core_ref, f32[2,5,5,1,512]{4,3,2,1,0:T(1,128)S(1)} %bitcast.14, ...), custom_call_target="tpu_custom_call" | custom-call | tf_op jit(solution)/shard_map/pallas_call | solution.py:829
  (5 shorter events, 0.0 us)
Async XLA Ops:
  0.0 0.7 %copy-start.4 = (s32[4,4]{1,0:T(4,128)S(1)}, s32[4,4]{1,0:T(4,128)}, u32[]{:S(2)}) copy-start(s32[4,4]{1,0:T(4,128)} %orders_hbm.1) | copy-start | bytes 196
  0.0 0.7 %copy-start.2 = (f32[3,4,4]{2,1,0:T(4,128)S(1)}, f32[3,4,4]{2,1,0:T(4,128)}, u32[]{:S(2)}) copy-start(f32[3,4,4]{2,1,0:T(4,128)} %metric_hbm.1) | copy-start | bytes 580
  0.0 0.7 %copy-start.3 = (s32[2,4,4]{2,1,0:T(4,128)S(1)}, s32[2,4,4]{2,1,0:T(4,128)}, u32[]{:S(2)}) copy-start(s32[2,4,4]{2,1,0:T(4,128)} %turn_hbm.1) | copy-start | bytes 388
  0.7 0.8 %copy-start = (f32[24,512]{1,0:T(8,128)S(1)}, f32[24,512]{1,0:T(8,128)}, u32[]{:S(2)}) copy-start(f32[24,512]{1,0:T(8,128)} %constant.13.clone.columns) | copy-start | bytes 147460
  1.5 0.9 %copy-start.1 = (f32[4,4,5,512]{3,1,2,0:T(4,128)S(1)}, f32[4,4,5,512]{3,1,2,0:T(4,128)}, u32[]{:S(2)}) copy-start(f32[4,4,5,512]{3,1,2,0:T(4,128)} %param.6) | copy-start | bytes 491524
  3.8 14.7 %collective-permute-start = (f32[64,128]{1,0:T(8,128)S(1)}, f32[64,128]{1,0:T(8,128)S(1)}, u32[]{:S(2)}, u32[]{:S(2)}) collective-permute-start(f32[64,128]{1,0:T(8,128)S(1)} %get-tuple-element.30), channel_id=1, source_target_pairs={{12,24},{36,48},{60,72},{84,96},{108,120},{132,144},{156,168},{180... | collective-permute-start | bytes 98312 | tf_op jit(solution)/shard_map/ppermute | solution.py:740
  18.6 4.1 %collective-permute-start.1 = (f32[64,128]{1,0:T(8,128)S(1)}, f32[64,128]{1,0:T(8,128)S(1)}, u32[]{:S(2)}, u32[]{:S(2)}) collective-permute-start(f32[64,128]{1,0:T(8,128)S(1)} %get-tuple-element.34), channel_id=1, source_target_pairs={{1,2},{3,4},{5,6},{7,8},{9,10},{2,1},{4,3},{6,5},{8,7},{10,9},{13,... | collective-permute-start | bytes 98312 | tf_op jit(solution)/shard_map/ppermute | solution.py:740
  22.7 0.7 %copy-start.5 = (s32[1,1,16,1]{2,3,1,0:T(1,128)S(1)}, s32[1,1,16,1]{2,3,1,0:T(1,128)}, u32[]{:S(2)}) copy-start(s32[1,1,16,1]{2,3,1,0:T(1,128)} %param.10) | copy-start | bytes 196
  26.2 12.9 %collective-permute-start.2 = (f32[10,5,1,512]{3,2,1,0:T(1,128)S(1)}, f32[10,5,1,512]{3,2,1,0:T(1,128)S(1)}, u32[]{:S(2)}, u32[]{:S(2)}) collective-permute-start(f32[10,5,1,512]{3,2,1,0:T(1,128)S(1)} %get-tuple-element.35), channel_id=1, source_target_pairs={{0,744},{12,36},{24,0},{36,60},{48,24},{60,84},{72,48},{84,108},{9... | collective-permute-start | bytes 307208 | tf_op jit(solution)/shard_map/ppermute | solution.py:750
  28.1 12.9 %collective-permute-start.3 = (f32[5,5,1,512]{3,2,1,0:T(1,128)S(1)}, f32[5,5,1,512]{3,2,1,0:T(1,128)S(1)}, u32[]{:S(2)}, u32[]{:S(2)}) collective-permute-start(f32[5,5,1,512]{3,2,1,0:T(1,128)S(1)} %get-tuple-element.37), channel_id=1, source_target_pairs={{0,24},{12,756},{24,48},{36,12},{48,72},{60,36},{72,96},{84,60},{9... | collective-permute-start | bytes 153608 | tf_op jit(solution)/shard_map/ppermute | solution.py:750

commit v4 on v3

--- a/solution.py
+++ b/solution.py
@@ -576,25 +576,26 @@
     return copies
 
 
-def first_kernel(
-    fields, columns, orders_hbm, turn_hbm, metric_hbm, core_ref, row_ref, q, tab, params, *rest
-):
-    outs = rest[:8]
-    flat, buf, orders, turn, metric_ref, sems = rest[8:]
+def table_kernel(columns, orders_hbm, turn_hbm, metric_hbm, _, tab, params, *rest):
+    orders, turn, metric_ref, sems = rest
     copies = fetched(
         [(orders_hbm, orders), (turn_hbm, turn), (metric_hbm, metric_ref)], sems
     )
+    for copy in copies:
+        copy.wait()
+    order = spread(lambda x, y: orders[x, y].astype(jnp.float32), jnp.float32)
+    for n, x in enumerate(all_metrics(metric_ref) + all_codes(turn) + [order]):
+        params[pl.ds(8 * n, 8), :] = x.astype(jnp.float32)
+    table_for(columns, order[0:1, :], tab)
+
+
+def first_kernel(fields, tab, params, core_ref, row_ref, q, *rest):
+    outs = rest[:8]
+    flat, buf = rest[8:]
     flat[pl.ds(80, 48), :] = jnp.zeros((48, 512), jnp.float32)
     for v in range(VARS):
         for x in range(4):
             flat[pl.ds(v * 16 + x * 4, 4), :] = fields[x, v]
-    for copy in copies:
-        copy.wait()
-    order = spread(lambda x, y: orders[x, y].astype(jnp.float32), jnp.float32)
-    metric, codes = all_metrics(metric_ref), all_codes(turn)
-    for n, x in enumerate(metric + codes):
-        params[pl.ds(8 * n, 8), :] = x.astype(jnp.float32)
-    table_for(columns, order[0:1, :], tab)
     in_k = tab[pl.ds(A_AT, 8), :]
     for part in range(4):
         block = flat[:, pl.ds(part * LANES, LANES)].T
@@ -606,7 +607,10 @@
                     block[at : at + 8] * in_ik * row_of(tab, A_AT + j)
                 )
     first_core, _ = places(core_ref, row_ref)
-    make_messages(q, tab, order, metric, codes, first_core, outs, buf)
+    order = params[pl.ds(40, 8), :]
+    make_messages(
+        q, tab, order, kept_metrics(params), kept_codes(params), first_core, outs, buf
+    )
 
 
 def inner_kernel(q, tab, params, rate):
@@ -763,21 +767,28 @@
     core = lax.rem(lax.axis_index("blk").astype(jnp.int32), 2).reshape(1)
     row = lax.axis_index("row").astype(jnp.int32).reshape(1)
     columns = jnp.asarray(table_columns())
-    q, tab, params, *faces = pl.pallas_call(
-        first_kernel,
-        out_shape=[VOLUME, f32(TAB_ROWS, LANES), f32(40, LANES)] + [FACE] * 8,
-        in_specs=[VMEM] * 2 + [HBM] * 3 + [SMEM] * 2,
-        out_specs=[VMEM] * 11,
+    targets = jnp.transpose(migration, (0, 1, 3, 2))
+    tab, params = pl.pallas_call(
+        table_kernel,
+        out_shape=[f32(TAB_ROWS, LANES), f32(48, LANES)],
+        in_specs=[VMEM] + [HBM] * 3 + [ANY],
+        out_specs=[VMEM] * 2,
         scratch_shapes=[
-            vmem(LANES, 512),
-            vmem(64, LANES),
             pltpu.SMEM((4, 4), jnp.int32),
             pltpu.SMEM((2, 4, 4), jnp.int32),
             pltpu.SMEM((3, 4, 4), jnp.float32),
             sems(3),
         ],
         compiler_params=PARAMS,
-    )(by_var, columns, orders, face_turn, metric, core, row)
+    )(columns, orders, face_turn, metric, targets)
+    q, *faces = pl.pallas_call(
+        first_kernel,
+        out_shape=[VOLUME] + [FACE] * 8,
+        in_specs=[VMEM] * 3 + [SMEM] * 2,
+        out_specs=[VMEM] * 9,
+        scratch_shapes=[vmem(LANES, 512), vmem(64, LANES)],
+        compiler_params=PARAMS,
+    )(by_var, tab, params, core, row)
     chip_send, blk_send, up, down = faces[4:]
     blk = swapped(blk_send, "blk", True)
     chip = paired(chip_send, "blk")
@@ -819,7 +830,7 @@
         ],
         compiler_params=PARAMS,
     )(
-        q, tab, params, inner, columns, jnp.transpose(migration, (0, 1, 3, 2)), core, row,
+        q, tab, params, inner, columns, targets, core, row,
         *faces[:4], chip, blk, pair, beyond,
     )
     far = hopped(outward, True)

time: 42.1 us -> 41.8 us (level)
  local copies, waits for them, and re-layouts: 3.08 us -> 2.42 us
    unnamed x12 -> x14, local copies, waits for them, and re-layouts: 3.08 us -> 2.42 us
    pallas_call x1 -> x2, Pallas kernels: 1.38 us -> 1.44 us  [the longest x1 1 us: local(): pl.pallas_call(table_kernel, out_shape=[f32(TAB_ROWS, LANES), f32(48, LAN...]
where the time goes in v4:
time: 41.8 us; the launch traced here: 41.5 us
  blocking collectives  18.9 us (45%)
  starting transfers between devices  14.1 us (34%)
  Pallas kernels  5.92 us (14%)
  local copies, waits for them, and re-layouts  2.42 us (6%)
    all_gather x4, blocking collectives, paired(): lax.all_gather(array, axis, axis_index_groups=pairs_of(lax.axis_size(axis...  18.9 us
    ppermute x2, starting transfers between devices, hopped(): lax.ppermute(array, 'blk', [(n, (n + step[n % 2]) % count) for n in range...  8.81 us
    ppermute x2, starting transfers between devices, swapped(): return lax.ppermute(array, axis, pairs + [(b, a) for a, b in pairs])  5.25 us
    pallas_call x1, Pallas kernels, local(): pl.pallas_call(third_kernel, out_shape=[f32(n, VARS, 1, 512) for n in (2...  2.93 us
    unnamed x14, local copies, waits for them, and re-layouts  2.42 us
    pallas_call x1, Pallas kernels, local(): pl.pallas_call(table_kernel, out_shape=[f32(TAB_ROWS, LANES), f32(48, LAN...  1 us
  transfers between devices with their start and end apart: 4, of which 0 were waited for; matrix products, arithmetic and copies ran while one was open for 0% of the time, Pallas kernels for 2%

profile of v4, /device:TPU:1, one launch (start us, length us, event | category | flops | bytes accessed | tf_op | source)
XLA Modules:
  0.0 41.5 jit_solution(12555168223082060049)
XLA Ops:
  0.0 0.7 %copy-done.6 = s32[4,4]{1,0:T(4,128)S(1)} copy-done((s32[4,4]{1,0:T(4,128)S(1)}, s32[4,4]{1,0:T(4,128)}, u32[]{:S(2)}) %copy-start.6) | copy-done | bytes 88
  0.7 0.0 copy-done.3
  0.7 0.0 copy-done.4
  0.7 0.8 %copy-done = f32[24,512]{1,0:T(8,128)S(1)} copy-done((f32[24,512]{1,0:T(8,128)S(1)}, f32[24,512]{1,0:T(8,128)}, u32[]{:S(2)}) %copy-start) | copy-done | bytes 49176
  1.5 1.0 %shard_map.64 = (f32[416,128]{1,0:T(8,128)S(1)}, f32[48,128]{1,0:T(8,128)S(1)}) custom-call(f32[24,512]{1,0:T(8,128)S(1)} %copy-done, s32[4,4]{1,0:T(4,128)S(1)} %copy-done.6, s32[2,4,4]{2,1,0:T(4,128)S(1)} %copy-done.4, f32[3,4,4]{2,1,0:T(4,128)S(1)} %copy-done.3, s32[1,1,1,16]{3,2,1,0:T(1,128)S(1)} %bitcast.17), custom_call_target="tpu_custom_call" | custom-call | tf_op jit(solution)/shard_map/pallas_call | solution.py:771
  2.5 0.0 copy-start.2
  2.5 0.9 %copy-done.2 = f32[4,4,5,512]{3,1,2,0:T(4,128)S(1)} copy-done((f32[4,4,5,512]{3,1,2,0:T(4,128)S(1)}, f32[4,4,5,512]{3,1,2,0:T(4,128)}, u32[]{:S(2)}) %copy-start.2) | copy-done | bytes 163864
  3.4 0.4 %shard_map.65 = (f32[512,128]{1,0:T(8,128)S(1)}, f32[64,128]{1,0:T(8,128)S(1)}, f32[64,128]{1,0:T(8,128)S(1)}, f32[64,128]{1,0:T(8,128)S(1)}, f32[64,128]{1,0:T(...) custom-call(f32[4,5,4,512]{3,2,1,0:T(4,128)S(1)} %bitcast.16, ...), custom_call_target="tpu_custom_call" | custom-call | tf_op jit(solution)/shard_map/pallas_call | solution.py:784
  3.9 4.6 %collective-permute-start = (f32[64,128]{1,0:T(8,128)S(1)}, f32[64,128]{1,0:T(8,128)S(1)}, u32[]{:S(2)}, u32[]{:S(2)}) collective-permute-start(f32[64,128]{1,0:T(8,128)S(1)} %get-tuple-element.30), channel_id=1, source_target_pairs={{12,24},{36,48},{60,72},{84,96},{108,120},{132,144},{156,168},{180... | collective-permute-start | bytes 98312 | tf_op jit(solution)/shard_map/ppermute | solution.py:744
  8.5 0.7 %shard_map.66.inner = f32[512,128]{1,0:T(8,128)S(1)} custom-call(f32[512,128]{1,0:T(8,128)S(1)} %get-tuple-element.24.q, f32[416,128]{1,0:T(8,128)S(1)} %get-tuple-element.22.tab, f32[48,128]{1,0:T(8,128)S(1)} %get-tuple-element.23.params), custom_call_target="tpu_custom_call" | custom-call | flops 40000000 | bytes 6000000 | tf_op jit(solution)/shard_map/pallas_call | solution.py:795
  9.2 9.3 %all-gather = f32[128,128]{1,0:T(8,128)S(1)} all-gather(f32[64,128]{1,0:T(8,128)S(1)} %get-tuple-element.29), channel_id=2, replica_groups={{0,12},{24,36},{48,60},{72,84},{96,108},{120,132},{144,156},{168,180},{..., dimensions={0}, use_global_device_ids=true | all-gather | bytes 98304 | tf_op jit(solution)/shard_map/all_gather | solution.py:748
  18.6 0.0 collective-permute-done.blk.rest_5_
  18.6 0.1 shard_map.67
  18.7 0.7 %collective-permute-start.1 = (f32[64,128]{1,0:T(8,128)S(1)}, f32[64,128]{1,0:T(8,128)S(1)}, u32[]{:S(2)}, u32[]{:S(2)}) collective-permute-start(f32[64,128]{1,0:T(8,128)S(1)} %get-tuple-element.34), channel_id=1, source_target_pairs={{1,2},{3,4},{5,6},{7,8},{9,10},{2,1},{4,3},{6,5},{8,7},{10,9},{13,... | collective-permute-start | bytes 98312 | tf_op jit(solution)/shard_map/ppermute | solution.py:744
  19.3 0.0 copy-start.1
  19.3 3.6 %all-gather.1 = f32[128,128]{1,0:T(8,128)S(1)} all-gather(f32[64,128]{1,0:T(8,128)S(1)} %get-tuple-element.33), channel_id=3, replica_groups={{0,1},{2,3},{4,5},{6,7},{8,9},{10,11},{12,13},{14,15},{16,17},{18,19},{..., dimensions={0}, use_global_device_ids=true | all-gather | bytes 98304 | tf_op jit(solution)/shard_map/all_gather | solution.py:748
  22.9 2.9 %shard_map.68 = (f32[10,5,1,512]{3,2,1,0:T(1,128)S(1)}, f32[5,5,1,512]{3,2,1,0:T(1,128)S(1)}, f32[5,5,1,512]{3,2,1,0:T(1,128)S(1)}, f32[5,5,1,512]{3,2,1,0:T(1,128)S(1)}) custom-call(f32[512,128]{1,0:T(8,128)S(1)} %get-tuple-element.24.q, f32[416,128]{1,0:T(8,128)S(1)} %get-tuple-element.22.tab, f32[48,128]{1,0:T(8,128)S(1)} %get-tuple-element.23.params, ...), custom_call_target="tpu_custom_call" | custom-call | tf_op jit(solution)/shard_map/pallas_call | solution.py:814
  25.9 1.9 %collective-permute-start.2 = (f32[10,5,1,512]{3,2,1,0:T(1,128)S(1)}, f32[10,5,1,512]{3,2,1,0:T(1,128)S(1)}, u32[]{:S(2)}, u32[]{:S(2)}) collective-permute-start(f32[10,5,1,512]{3,2,1,0:T(1,128)S(1)} %get-tuple-element.35), channel_id=1, source_target_pairs={{0,744},{12,36},{24,0},{36,60},{48,24},{60,84},{72,48},{84,108},{9... | collective-permute-start | bytes 307208 | tf_op jit(solution)/shard_map/ppermute | solution.py:754
  27.8 6.9 %collective-permute-start.3 = (f32[5,5,1,512]{3,2,1,0:T(1,128)S(1)}, f32[5,5,1,512]{3,2,1,0:T(1,128)S(1)}, u32[]{:S(2)}, u32[]{:S(2)}) collective-permute-start(f32[5,5,1,512]{3,2,1,0:T(1,128)S(1)} %get-tuple-element.37), channel_id=1, source_target_pairs={{0,24},{12,756},{24,48},{36,12},{48,72},{60,36},{72,96},{84,60},{9... | collective-permute-start | bytes 153608 | tf_op jit(solution)/shard_map/ppermute | solution.py:754
  34.7 4.1 %all-gather.2 = f32[10,5,1,512]{3,2,1,0:T(1,128)S(1)} all-gather(f32[5,5,1,512]{3,2,1,0:T(1,128)S(1)} %get-tuple-element.38), channel_id=4, replica_groups={{0,12},{24,36},{48,60},{72,84},{96,108},{120,132},{144,156},{168,180},{..., dimensions={0}, use_global_device_ids=true | all-gather | bytes 153600 | tf_op jit(solution)/shard_map/all_gather | solution.py:748
  38.8 0.0 collective-permute-done.2.far
  38.8 1.9 %all-gather.3 = f32[20,5,1,512]{3,2,1,0:T(1,128)S(1)} all-gather(f32[10,5,1,512]{3,2,1,0:T(1,128)S(1)} %collective-permute-done.2.far), channel_id=5, replica_groups={{0,12},{24,36},{48,60},{72,84},{96,108},{120,132},{144,156},{168,180},{..., dimensions={0}, use_global_device_ids=true | all-gather | bytes 307200 | tf_op jit(solution)/shard_map/all_gather | solution.py:748
  40.7 0.0 collective-permute-done.3.near
  40.7 0.7 %shard_map.69 = f32[25,5,1,512]{3,2,1,0:T(1,128)} custom-call(f32[10,5,1,512]{3,2,1,0:T(1,128)S(1)} %collective-permute-done.2.far, f32[5,5,1,512]{3,2,1,0:T(1,128)S(1)} %get-tuple-element.36.own, f32[5,5,1,512]{3,2,1,0:T(1,128)S(1)} %collective-permute-done.3.near, s32[1]{0:T(128)} %bitcast.2.core_ref, f32[2,5,5,1,512]{4,3,2,1,0:T(1,128)S(1)} %bitcast.14, ...), custom_call_target="tpu_custom_call" | custom-call | tf_op jit(solution)/shard_map/pallas_call | solution.py:840
  (8 shorter events, 0.0 us)
Async XLA Ops:
  0.0 0.7 %copy-start.6 = (s32[4,4]{1,0:T(4,128)S(1)}, s32[4,4]{1,0:T(4,128)}, u32[]{:S(2)}) copy-start(s32[4,4]{1,0:T(4,128)} %orders_hbm.1) | copy-start | bytes 196
  0.0 0.7 %copy-start.3 = (f32[3,4,4]{2,1,0:T(4,128)S(1)}, f32[3,4,4]{2,1,0:T(4,128)}, u32[]{:S(2)}) copy-start(f32[3,4,4]{2,1,0:T(4,128)} %metric_hbm.1) | copy-start | bytes 580
  0.0 0.7 %copy-start.4 = (s32[2,4,4]{2,1,0:T(4,128)S(1)}, s32[2,4,4]{2,1,0:T(4,128)}, u32[]{:S(2)}) copy-start(s32[2,4,4]{2,1,0:T(4,128)} %turn_hbm.1) | copy-start | bytes 388
  0.0 0.7 %copy-start.5 = (s32[1,1,16,1]{2,3,1,0:T(1,128)S(1)}, s32[1,1,16,1]{2,3,1,0:T(1,128)}, u32[]{:S(2)}) copy-start(s32[1,1,16,1]{2,3,1,0:T(1,128)} %param.10) | copy-start | bytes 196
  0.7 0.8 %copy-start = (f32[24,512]{1,0:T(8,128)S(1)}, f32[24,512]{1,0:T(8,128)}, u32[]{:S(2)}) copy-start(f32[24,512]{1,0:T(8,128)} %constant.13.clone.columns) | copy-start | bytes 147460
  2.5 0.9 %copy-start.2 = (f32[4,4,5,512]{3,1,2,0:T(4,128)S(1)}, f32[4,4,5,512]{3,1,2,0:T(4,128)}, u32[]{:S(2)}) copy-start(f32[4,4,5,512]{3,1,2,0:T(4,128)} %param.6) | copy-start | bytes 491524
  3.9 14.7 %collective-permute-start = (f32[64,128]{1,0:T(8,128)S(1)}, f32[64,128]{1,0:T(8,128)S(1)}, u32[]{:S(2)}, u32[]{:S(2)}) collective-permute-start(f32[64,128]{1,0:T(8,128)S(1)} %get-tuple-element.30), channel_id=1, source_target_pairs={{12,24},{36,48},{60,72},{84,96},{108,120},{132,144},{156,168},{180... | collective-permute-start | bytes 98312 | tf_op jit(solution)/shard_map/ppermute | solution.py:744
  18.7 4.3 %collective-permute-start.1 = (f32[64,128]{1,0:T(8,128)S(1)}, f32[64,128]{1,0:T(8,128)S(1)}, u32[]{:S(2)}, u32[]{:S(2)}) collective-permute-start(f32[64,128]{1,0:T(8,128)S(1)} %get-tuple-element.34), channel_id=1, source_target_pairs={{1,2},{3,4},{5,6},{7,8},{9,10},{2,1},{4,3},{6,5},{8,7},{10,9},{13,... | collective-permute-start | bytes 98312 | tf_op jit(solution)/shard_map/ppermute | solution.py:744
  19.3 3.6 %copy-start.1 = (f32[24,512]{1,0:T(8,128)S(1)}, f32[24,512]{1,0:T(8,128)}, u32[]{:S(2)}) copy-start(f32[24,512]{1,0:T(8,128)} %constant.13.clone.columns) | copy-start | bytes 147460
  25.9 12.9 %collective-permute-start.2 = (f32[10,5,1,512]{3,2,1,0:T(1,128)S(1)}, f32[10,5,1,512]{3,2,1,0:T(1,128)S(1)}, u32[]{:S(2)}, u32[]{:S(2)}) collective-permute-start(f32[10,5,1,512]{3,2,1,0:T(1,128)S(1)} %get-tuple-element.35), channel_id=1, source_target_pairs={{0,744},{12,36},{24,0},{36,60},{48,24},{60,84},{72,48},{84,108},{9... | collective-permute-start | bytes 307208 | tf_op jit(solution)/shard_map/ppermute | solution.py:754
  27.8 12.9 %collective-permute-start.3 = (f32[5,5,1,512]{3,2,1,0:T(1,128)S(1)}, f32[5,5,1,512]{3,2,1,0:T(1,128)S(1)}, u32[]{:S(2)}, u32[]{:S(2)}) collective-permute-start(f32[5,5,1,512]{3,2,1,0:T(1,128)S(1)} %get-tuple-element.37), channel_id=1, source_target_pairs={{0,24},{12,756},{24,48},{36,12},{48,72},{60,36},{72,96},{84,60},{9... | collective-permute-start | bytes 153608 | tf_op jit(solution)/shard_map/ppermute | solution.py:754

commit v5 on v3

--- a/solution.py
+++ b/solution.py
@@ -577,7 +577,7 @@
 
 
 def first_kernel(
-    fields, columns, orders_hbm, turn_hbm, metric_hbm, core_ref, row_ref, q, tab, params, *rest
+    fields, columns, orders_hbm, turn_hbm, metric_hbm, _, core_ref, row_ref, q, tab, params, *rest
 ):
     outs = rest[:8]
     flat, buf, orders, turn, metric_ref, sems = rest[8:]
@@ -763,10 +763,11 @@
     core = lax.rem(lax.axis_index("blk").astype(jnp.int32), 2).reshape(1)
     row = lax.axis_index("row").astype(jnp.int32).reshape(1)
     columns = jnp.asarray(table_columns())
+    targets = jnp.transpose(migration, (0, 1, 3, 2))
     q, tab, params, *faces = pl.pallas_call(
         first_kernel,
         out_shape=[VOLUME, f32(TAB_ROWS, LANES), f32(40, LANES)] + [FACE] * 8,
-        in_specs=[VMEM] * 2 + [HBM] * 3 + [SMEM] * 2,
+        in_specs=[VMEM] * 2 + [HBM] * 3 + [ANY] + [SMEM] * 2,
         out_specs=[VMEM] * 11,
         scratch_shapes=[
             vmem(LANES, 512),
@@ -777,7 +778,7 @@
             sems(3),
         ],
         compiler_params=PARAMS,
-    )(by_var, columns, orders, face_turn, metric, core, row)
+    )(by_var, columns, orders, face_turn, metric, targets, core, row)
     chip_send, blk_send, up, down = faces[4:]
     blk = swapped(blk_send, "blk", True)
     chip = paired(chip_send, "blk")
@@ -819,7 +820,7 @@
         ],
         compiler_params=PARAMS,
     )(
-        q, tab, params, inner, columns, jnp.transpose(migration, (0, 1, 3, 2)), core, row,
+        q, tab, params, inner, columns, targets, core, row,
         *faces[:4], chip, blk, pair, beyond,
     )
     far = hopped(outward, True)

time: 42.1 us -> 41.5 us (0.986)
  local copies, waits for them, and re-layouts: 3.08 us -> 2.42 us
    unnamed x12, local copies, waits for them, and re-layouts: 3.08 us -> 2.42 us
where the time goes in v5:
time: 41.5 us; the launch traced here: 41.1 us
  blocking collectives  18.8 us (45%)
  starting transfers between devices  14.1 us (34%)
  Pallas kernels  5.71 us (14%)
  local copies, waits for them, and re-layouts  2.42 us (6%)
    all_gather x4, blocking collectives, paired(): lax.all_gather(array, axis, axis_index_groups=pairs_of(lax.axis_size(axis...  18.8 us
    ppermute x2, starting transfers between devices, hopped(): lax.ppermute(array, 'blk', [(n, (n + step[n % 2]) % count) for n in range...  8.81 us
    ppermute x2, starting transfers between devices, swapped(): return lax.ppermute(array, axis, pairs + [(b, a) for a, b in pairs])  5.25 us
    pallas_call x1, Pallas kernels, local(): pl.pallas_call(third_kernel, out_shape=[f32(n, VARS, 1, 512) for n in (2...  2.82 us
    unnamed x12, local copies, waits for them, and re-layouts  2.42 us
    pallas_call x1, Pallas kernels, local(): pl.pallas_call(first_kernel, out_shape=[VOLUME, f32(TAB_ROWS, LANES), f32...  1.37 us
  transfers between devices with their start and end apart: 4, of which 0 were waited for; matrix products, arithmetic and copies ran while one was open for 0% of the time, Pallas kernels for 2%

profile of v5, /device:TPU:1, one launch (start us, length us, event | category | flops | bytes accessed | tf_op | source)
XLA Modules:
  0.0 41.1 jit_solution(6452009300413355554)
XLA Ops:
  0.0 0.0 copy-start.4
  0.0 0.7 %copy-done.5 = s32[4,4]{1,0:T(4,128)S(1)} copy-done((s32[4,4]{1,0:T(4,128)S(1)}, s32[4,4]{1,0:T(4,128)}, u32[]{:S(2)}) %copy-start.5) | copy-done | bytes 88
  0.7 0.0 copy-done.2
  0.7 0.0 copy-done.3
  0.7 0.0 copy-done.4
  0.7 0.8 %copy-done = f32[24,512]{1,0:T(8,128)S(1)} copy-done((f32[24,512]{1,0:T(8,128)S(1)}, f32[24,512]{1,0:T(8,128)}, u32[]{:S(2)}) %copy-start) | copy-done | bytes 49176
  1.5 0.9 %copy-done.1 = f32[4,4,5,512]{3,1,2,0:T(4,128)S(1)} copy-done((f32[4,4,5,512]{3,1,2,0:T(4,128)S(1)}, f32[4,4,5,512]{3,1,2,0:T(4,128)}, u32[]{:S(2)}) %copy-start.1) | copy-done | bytes 163864
  2.4 1.4 %shard_map.64 = (f32[512,128]{1,0:T(8,128)S(1)}, f32[416,128]{1,0:T(8,128)S(1)}, f32[40,128]{1,0:T(8,128)S(1)}, f32[64,128]{1,0:T(8,128)S(1)}, f32[64,128]{1,0:T...) custom-call(f32[4,5,4,512]{3,2,1,0:T(4,128)S(1)} %bitcast.16, ...), custom_call_target="tpu_custom_call" | custom-call | tf_op jit(solution)/shard_map/pallas_call | solution.py:767
  3.8 4.6 %collective-permute-start = (f32[64,128]{1,0:T(8,128)S(1)}, f32[64,128]{1,0:T(8,128)S(1)}, u32[]{:S(2)}, u32[]{:S(2)}) collective-permute-start(f32[64,128]{1,0:T(8,128)S(1)} %get-tuple-element.30), channel_id=1, source_target_pairs={{12,24},{36,48},{60,72},{84,96},{108,120},{132,144},{156,168},{180... | collective-permute-start | bytes 98312 | tf_op jit(solution)/shard_map/ppermute | solution.py:740
  8.4 0.7 %shard_map.65.inner = f32[512,128]{1,0:T(8,128)S(1)} custom-call(f32[512,128]{1,0:T(8,128)S(1)} %get-tuple-element.22.q, f32[416,128]{1,0:T(8,128)S(1)} %get-tuple-element.23.tab, f32[40,128]{1,0:T(8,128)S(1)} %get-tuple-element.24.params), custom_call_target="tpu_custom_call" | custom-call | flops 40000000 | bytes 6000000 | tf_op jit(solution)/shard_map/pallas_call | solution.py:785
  9.1 9.3 %all-gather = f32[128,128]{1,0:T(8,128)S(1)} all-gather(f32[64,128]{1,0:T(8,128)S(1)} %get-tuple-element.29), channel_id=2, replica_groups={{0,12},{24,36},{48,60},{72,84},{96,108},{120,132},{144,156},{168,180},{..., dimensions={0}, use_global_device_ids=true | all-gather | bytes 98304 | tf_op jit(solution)/shard_map/all_gather | solution.py:744
  18.5 0.0 collective-permute-done.blk.rest_5_
  18.5 0.1 shard_map.66
  18.6 0.7 %collective-permute-start.1 = (f32[64,128]{1,0:T(8,128)S(1)}, f32[64,128]{1,0:T(8,128)S(1)}, u32[]{:S(2)}, u32[]{:S(2)}) collective-permute-start(f32[64,128]{1,0:T(8,128)S(1)} %get-tuple-element.34), channel_id=1, source_target_pairs={{1,2},{3,4},{5,6},{7,8},{9,10},{2,1},{4,3},{6,5},{8,7},{10,9},{13,... | collective-permute-start | bytes 98312 | tf_op jit(solution)/shard_map/ppermute | solution.py:740
  19.2 3.5 %all-gather.1 = f32[128,128]{1,0:T(8,128)S(1)} all-gather(f32[64,128]{1,0:T(8,128)S(1)} %get-tuple-element.33), channel_id=3, replica_groups={{0,1},{2,3},{4,5},{6,7},{8,9},{10,11},{12,13},{14,15},{16,17},{18,19},{..., dimensions={0}, use_global_device_ids=true | all-gather | bytes 98304 | tf_op jit(solution)/shard_map/all_gather | solution.py:744
  22.7 0.0 collective-permute-done.1.rest_7_
  22.7 2.8 %shard_map.67 = (f32[10,5,1,512]{3,2,1,0:T(1,128)S(1)}, f32[5,5,1,512]{3,2,1,0:T(1,128)S(1)}, f32[5,5,1,512]{3,2,1,0:T(1,128)S(1)}, f32[5,5,1,512]{3,2,1,0:T(1,128)S(1)}) custom-call(f32[512,128]{1,0:T(8,128)S(1)} %get-tuple-element.22.q, f32[416,128]{1,0:T(8,128)S(1)} %get-tuple-element.23.tab, f32[40,128]{1,0:T(8,128)S(1)} %get-tuple-element.24.params, ...), custom_call_target="tpu_custom_call" | custom-call | tf_op jit(solution)/shard_map/pallas_call | solution.py:804
  25.5 1.9 %collective-permute-start.2 = (f32[10,5,1,512]{3,2,1,0:T(1,128)S(1)}, f32[10,5,1,512]{3,2,1,0:T(1,128)S(1)}, u32[]{:S(2)}, u32[]{:S(2)}) collective-permute-start(f32[10,5,1,512]{3,2,1,0:T(1,128)S(1)} %get-tuple-element.35), channel_id=1, source_target_pairs={{0,744},{12,36},{24,0},{36,60},{48,24},{60,84},{72,48},{84,108},{9... | collective-permute-start | bytes 307208 | tf_op jit(solution)/shard_map/ppermute | solution.py:750
  27.5 6.9 %collective-permute-start.3 = (f32[5,5,1,512]{3,2,1,0:T(1,128)S(1)}, f32[5,5,1,512]{3,2,1,0:T(1,128)S(1)}, u32[]{:S(2)}, u32[]{:S(2)}) collective-permute-start(f32[5,5,1,512]{3,2,1,0:T(1,128)S(1)} %get-tuple-element.37), channel_id=1, source_target_pairs={{0,24},{12,756},{24,48},{36,12},{48,72},{60,36},{72,96},{84,60},{9... | collective-permute-start | bytes 153608 | tf_op jit(solution)/shard_map/ppermute | solution.py:750
  34.4 4.1 %all-gather.2 = f32[10,5,1,512]{3,2,1,0:T(1,128)S(1)} all-gather(f32[5,5,1,512]{3,2,1,0:T(1,128)S(1)} %get-tuple-element.38), channel_id=4, replica_groups={{0,12},{24,36},{48,60},{72,84},{96,108},{120,132},{144,156},{168,180},{..., dimensions={0}, use_global_device_ids=true | all-gather | bytes 153600 | tf_op jit(solution)/shard_map/all_gather | solution.py:744
  38.4 0.0 collective-permute-done.2.far
  38.4 1.9 %all-gather.3 = f32[20,5,1,512]{3,2,1,0:T(1,128)S(1)} all-gather(f32[10,5,1,512]{3,2,1,0:T(1,128)S(1)} %collective-permute-done.2.far), channel_id=5, replica_groups={{0,12},{24,36},{48,60},{72,84},{96,108},{120,132},{144,156},{168,180},{..., dimensions={0}, use_global_device_ids=true | all-gather | bytes 307200 | tf_op jit(solution)/shard_map/all_gather | solution.py:744
  40.4 0.0 collective-permute-done.3.near
  40.4 0.7 %shard_map.68 = f32[25,5,1,512]{3,2,1,0:T(1,128)} custom-call(f32[10,5,1,512]{3,2,1,0:T(1,128)S(1)} %collective-permute-done.2.far, f32[5,5,1,512]{3,2,1,0:T(1,128)S(1)} %get-tuple-element.36.own, f32[5,5,1,512]{3,2,1,0:T(1,128)S(1)} %collective-permute-done.3.near, s32[1]{0:T(128)} %bitcast.2.core_ref, f32[2,5,5,1,512]{4,3,2,1,0:T(1,128)S(1)} %bitcast.14, ...), custom_call_target="tpu_custom_call" | custom-call | tf_op jit(solution)/shard_map/pallas_call | solution.py:830
  (5 shorter events, 0.0 us)
Async XLA Ops:
  0.0 0.7 %copy-start.5 = (s32[4,4]{1,0:T(4,128)S(1)}, s32[4,4]{1,0:T(4,128)}, u32[]{:S(2)}) copy-start(s32[4,4]{1,0:T(4,128)} %orders_hbm.1) | copy-start | bytes 196
  0.0 0.7 %copy-start.2 = (f32[3,4,4]{2,1,0:T(4,128)S(1)}, f32[3,4,4]{2,1,0:T(4,128)}, u32[]{:S(2)}) copy-start(f32[3,4,4]{2,1,0:T(4,128)} %metric_hbm.1) | copy-start | bytes 580
  0.0 0.7 %copy-start.3 = (s32[2,4,4]{2,1,0:T(4,128)S(1)}, s32[2,4,4]{2,1,0:T(4,128)}, u32[]{:S(2)}) copy-start(s32[2,4,4]{2,1,0:T(4,128)} %turn_hbm.1) | copy-start | bytes 388
  0.0 0.7 %copy-start.4 = (s32[1,1,16,1]{2,3,1,0:T(1,128)S(1)}, s32[1,1,16,1]{2,3,1,0:T(1,128)}, u32[]{:S(2)}) copy-start(s32[1,1,16,1]{2,3,1,0:T(1,128)} %param.10) | copy-start | bytes 196
  0.7 0.8 %copy-start = (f32[24,512]{1,0:T(8,128)S(1)}, f32[24,512]{1,0:T(8,128)}, u32[]{:S(2)}) copy-start(f32[24,512]{1,0:T(8,128)} %constant.13.clone.columns) | copy-start | bytes 147460
  1.5 0.9 %copy-start.1 = (f32[4,4,5,512]{3,1,2,0:T(4,128)S(1)}, f32[4,4,5,512]{3,1,2,0:T(4,128)}, u32[]{:S(2)}) copy-start(f32[4,4,5,512]{3,1,2,0:T(4,128)} %param.6) | copy-start | bytes 491524
  3.8 14.7 %collective-permute-start = (f32[64,128]{1,0:T(8,128)S(1)}, f32[64,128]{1,0:T(8,128)S(1)}, u32[]{:S(2)}, u32[]{:S(2)}) collective-permute-start(f32[64,128]{1,0:T(8,128)S(1)} %get-tuple-element.30), channel_id=1, source_target_pairs={{12,24},{36,48},{60,72},{84,96},{108,120},{132,144},{156,168},{180... | collective-permute-start | bytes 98312 | tf_op jit(solution)/shard_map/ppermute | solution.py:740
  18.6 4.1 %collective-permute-start.1 = (f32[64,128]{1,0:T(8,128)S(1)}, f32[64,128]{1,0:T(8,128)S(1)}, u32[]{:S(2)}, u32[]{:S(2)}) collective-permute-start(f32[64,128]{1,0:T(8,128)S(1)} %get-tuple-element.34), channel_id=1, source_target_pairs={{1,2},{3,4},{5,6},{7,8},{9,10},{2,1},{4,3},{6,5},{8,7},{10,9},{13,... | collective-permute-start | bytes 98312 | tf_op jit(solution)/shard_map/ppermute | solution.py:740
  25.5 12.9 %collective-permute-start.2 = (f32[10,5,1,512]{3,2,1,0:T(1,128)S(1)}, f32[10,5,1,512]{3,2,1,0:T(1,128)S(1)}, u32[]{:S(2)}, u32[]{:S(2)}) collective-permute-start(f32[10,5,1,512]{3,2,1,0:T(1,128)S(1)} %get-tuple-element.35), channel_id=1, source_target_pairs={{0,744},{12,36},{24,0},{36,60},{48,24},{60,84},{72,48},{84,108},{9... | collective-permute-start | bytes 307208 | tf_op jit(solution)/shard_map/ppermute | solution.py:750
  27.5 12.9 %collective-permute-start.3 = (f32[5,5,1,512]{3,2,1,0:T(1,128)S(1)}, f32[5,5,1,512]{3,2,1,0:T(1,128)S(1)}, u32[]{:S(2)}, u32[]{:S(2)}) collective-permute-start(f32[5,5,1,512]{3,2,1,0:T(1,128)S(1)} %get-tuple-element.37), channel_id=1, source_target_pairs={{0,24},{12,756},{24,48},{36,12},{48,72},{60,36},{72,96},{84,60},{9... | collective-permute-start | bytes 153608 | tf_op jit(solution)/shard_map/ppermute | solution.py:750

commit v6 on v5

--- a/solution.py
+++ b/solution.py
@@ -1,6 +1,5 @@
 import jax
 import jax.numpy as jnp
-import ml_dtypes
 import numpy as np
 from jax import lax
 from jax.experimental import pallas as pl
@@ -115,11 +114,7 @@
         rows[A_AT : A_AT + 8, level] = active[level]
         rows[LIFT_AT : LIFT_AT + 8, level] = lifting[level]
         rows[DLAST_AT : DLAST_AT + 8, level] = derive[level][PMIN + level]
-    left, parts = rows.T.astype(np.float32), []
-    for _ in range(3):
-        parts.append(left.astype(ml_dtypes.bfloat16).astype(np.float32))
-        left = left - parts[-1]
-    return np.concatenate(parts)
+    return np.ascontiguousarray(rows.T).astype(np.float32)
 
 
 def lane_ids():
@@ -563,7 +558,12 @@
     for part in range(4):
         at = part * LANES
         size = min(LANES, TAB_ROWS - at)
-        block = jnp.concatenate([columns[:, pl.ds(at, LANES)], pad], axis=0).T
+        left = jnp.concatenate([columns[:, pl.ds(at, LANES)], pad[:8]], axis=0)
+        cut = []
+        for _ in range(3):
+            cut.append(left.astype(jnp.bfloat16).astype(jnp.float32))
+            left = left - cut[-1]
+        block = jnp.concatenate([x[:8] for x in cut] + [pad], axis=0).T
         tab[pl.ds(at, size), :] = jnp.dot(
             block.astype(jnp.bfloat16), one_hot, preferred_element_type=jnp.float32
         )[:size]

time: 41.5 us -> 40.7 us (0.981)
  local copies, waits for them, and re-layouts: 2.42 us -> 1.63 us
    unnamed x12, local copies, waits for them, and re-layouts: 2.42 us -> 1.63 us
where the time goes in v6:
time: 40.7 us; the launch traced here: 40.3 us
  blocking collectives  18.8 us (46%)
  starting transfers between devices  14.1 us (35%)
  Pallas kernels  5.72 us (14%)
  local copies, waits for them, and re-layouts  1.63 us (4%)
    all_gather x4, blocking collectives, paired(): lax.all_gather(array, axis, axis_index_groups=pairs_of(lax.axis_size(axis...  18.8 us
    ppermute x2, starting transfers between devices, hopped(): lax.ppermute(array, 'blk', [(n, (n + step[n % 2]) % count) for n in range...  8.81 us
    ppermute x2, starting transfers between devices, swapped(): return lax.ppermute(array, axis, pairs + [(b, a) for a, b in pairs])  5.25 us
    pallas_call x1, Pallas kernels, local(): pl.pallas_call(third_kernel, out_shape=[f32(n, VARS, 1, 512) for n in (2...  2.82 us
    unnamed x12, local copies, waits for them, and re-layouts  1.63 us
    pallas_call x1, Pallas kernels, local(): pl.pallas_call(first_kernel, out_shape=[VOLUME, f32(TAB_ROWS, LANES), f32...  1.38 us
  transfers between devices with their start and end apart: 4, of which 0 were waited for; matrix products, arithmetic and copies ran while one was open for 0% of the time, Pallas kernels for 2%

profile of v6, /device:TPU:1, one launch (start us, length us, event | category | flops | bytes accessed | tf_op | source)
XLA Modules:
  0.0 40.3 jit_solution(14517632701371144238)
XLA Ops:
  0.0 0.0 copy-start.3
  0.0 0.0 copy-start.5
  0.0 0.7 %copy-done.1 = f32[8,512]{1,0:T(8,128)S(1)} copy-done((f32[8,512]{1,0:T(8,128)S(1)}, f32[8,512]{1,0:T(8,128)}, u32[]{:S(2)}) %copy-start.1) | copy-done | bytes 16408
  0.7 0.0 copy-done.4
  0.7 0.0 copy-done.2
  0.7 0.0 copy-done.3
  0.7 0.9 %copy-done = f32[4,4,5,512]{3,1,2,0:T(4,128)S(1)} copy-done((f32[4,4,5,512]{3,1,2,0:T(4,128)S(1)}, f32[4,4,5,512]{3,1,2,0:T(4,128)}, u32[]{:S(2)}) %copy-start) | copy-done | bytes 163864
  1.7 1.4 %shard_map.64 = (f32[512,128]{1,0:T(8,128)S(1)}, f32[416,128]{1,0:T(8,128)S(1)}, f32[40,128]{1,0:T(8,128)S(1)}, f32[64,128]{1,0:T(8,128)S(1)}, f32[64,128]{1,0:T...) custom-call(f32[4,5,4,512]{3,2,1,0:T(4,128)S(1)} %bitcast.16, ...), custom_call_target="tpu_custom_call" | custom-call | tf_op jit(solution)/shard_map/pallas_call | solution.py:767
  3.0 4.6 %collective-permute-start = (f32[64,128]{1,0:T(8,128)S(1)}, f32[64,128]{1,0:T(8,128)S(1)}, u32[]{:S(2)}, u32[]{:S(2)}) collective-permute-start(f32[64,128]{1,0:T(8,128)S(1)} %get-tuple-element.30), channel_id=1, source_target_pairs={{12,24},{36,48},{60,72},{84,96},{108,120},{132,144},{156,168},{180... | collective-permute-start | bytes 98312 | tf_op jit(solution)/shard_map/ppermute | solution.py:740
  7.6 0.7 %shard_map.65.inner = f32[512,128]{1,0:T(8,128)S(1)} custom-call(f32[512,128]{1,0:T(8,128)S(1)} %get-tuple-element.22.q, f32[416,128]{1,0:T(8,128)S(1)} %get-tuple-element.23.tab, f32[40,128]{1,0:T(8,128)S(1)} %get-tuple-element.24.params), custom_call_target="tpu_custom_call" | custom-call | flops 40000000 | bytes 6000000 | tf_op jit(solution)/shard_map/pallas_call | solution.py:785
  8.4 9.3 %all-gather = f32[128,128]{1,0:T(8,128)S(1)} all-gather(f32[64,128]{1,0:T(8,128)S(1)} %get-tuple-element.29), channel_id=2, replica_groups={{0,12},{24,36},{48,60},{72,84},{96,108},{120,132},{144,156},{168,180},{..., dimensions={0}, use_global_device_ids=true | all-gather | bytes 98304 | tf_op jit(solution)/shard_map/all_gather | solution.py:744
  17.7 0.0 collective-permute-done.blk.rest_5_
  17.7 0.1 shard_map.66
  17.8 0.7 %collective-permute-start.1 = (f32[64,128]{1,0:T(8,128)S(1)}, f32[64,128]{1,0:T(8,128)S(1)}, u32[]{:S(2)}, u32[]{:S(2)}) collective-permute-start(f32[64,128]{1,0:T(8,128)S(1)} %get-tuple-element.34), channel_id=1, source_target_pairs={{1,2},{3,4},{5,6},{7,8},{9,10},{2,1},{4,3},{6,5},{8,7},{10,9},{13,... | collective-permute-start | bytes 98312 | tf_op jit(solution)/shard_map/ppermute | solution.py:740
  18.4 3.5 %all-gather.1 = f32[128,128]{1,0:T(8,128)S(1)} all-gather(f32[64,128]{1,0:T(8,128)S(1)} %get-tuple-element.33), channel_id=3, replica_groups={{0,1},{2,3},{4,5},{6,7},{8,9},{10,11},{12,13},{14,15},{16,17},{18,19},{..., dimensions={0}, use_global_device_ids=true | all-gather | bytes 98304 | tf_op jit(solution)/shard_map/all_gather | solution.py:744
  21.9 0.0 collective-permute-done.1.rest_7_
  21.9 2.8 %shard_map.67 = (f32[10,5,1,512]{3,2,1,0:T(1,128)S(1)}, f32[5,5,1,512]{3,2,1,0:T(1,128)S(1)}, f32[5,5,1,512]{3,2,1,0:T(1,128)S(1)}, f32[5,5,1,512]{3,2,1,0:T(1,128)S(1)}) custom-call(f32[512,128]{1,0:T(8,128)S(1)} %get-tuple-element.22.q, f32[416,128]{1,0:T(8,128)S(1)} %get-tuple-element.23.tab, f32[40,128]{1,0:T(8,128)S(1)} %get-tuple-element.24.params, ...), custom_call_target="tpu_custom_call" | custom-call | tf_op jit(solution)/shard_map/pallas_call | solution.py:804
  24.7 1.9 %collective-permute-start.2 = (f32[10,5,1,512]{3,2,1,0:T(1,128)S(1)}, f32[10,5,1,512]{3,2,1,0:T(1,128)S(1)}, u32[]{:S(2)}, u32[]{:S(2)}) collective-permute-start(f32[10,5,1,512]{3,2,1,0:T(1,128)S(1)} %get-tuple-element.35), channel_id=1, source_target_pairs={{0,744},{12,36},{24,0},{36,60},{48,24},{60,84},{72,48},{84,108},{9... | collective-permute-start | bytes 307208 | tf_op jit(solution)/shard_map/ppermute | solution.py:750
  26.7 6.9 %collective-permute-start.3 = (f32[5,5,1,512]{3,2,1,0:T(1,128)S(1)}, f32[5,5,1,512]{3,2,1,0:T(1,128)S(1)}, u32[]{:S(2)}, u32[]{:S(2)}) collective-permute-start(f32[5,5,1,512]{3,2,1,0:T(1,128)S(1)} %get-tuple-element.37), channel_id=1, source_target_pairs={{0,24},{12,756},{24,48},{36,12},{48,72},{60,36},{72,96},{84,60},{9... | collective-permute-start | bytes 153608 | tf_op jit(solution)/shard_map/ppermute | solution.py:750
  33.6 4.1 %all-gather.2 = f32[10,5,1,512]{3,2,1,0:T(1,128)S(1)} all-gather(f32[5,5,1,512]{3,2,1,0:T(1,128)S(1)} %get-tuple-element.38), channel_id=4, replica_groups={{0,12},{24,36},{48,60},{72,84},{96,108},{120,132},{144,156},{168,180},{..., dimensions={0}, use_global_device_ids=true | all-gather | bytes 153600 | tf_op jit(solution)/shard_map/all_gather | solution.py:744
  37.7 0.0 collective-permute-done.2.far
  37.7 1.9 %all-gather.3 = f32[20,5,1,512]{3,2,1,0:T(1,128)S(1)} all-gather(f32[10,5,1,512]{3,2,1,0:T(1,128)S(1)} %collective-permute-done.2.far), channel_id=5, replica_groups={{0,12},{24,36},{48,60},{72,84},{96,108},{120,132},{144,156},{168,180},{..., dimensions={0}, use_global_device_ids=true | all-gather | bytes 307200 | tf_op jit(solution)/shard_map/all_gather | solution.py:744
  39.6 0.0 collective-permute-done.3.near
  39.6 0.7 %shard_map.68 = f32[25,5,1,512]{3,2,1,0:T(1,128)} custom-call(f32[10,5,1,512]{3,2,1,0:T(1,128)S(1)} %collective-permute-done.2.far, f32[5,5,1,512]{3,2,1,0:T(1,128)S(1)} %get-tuple-element.36.own, f32[5,5,1,512]{3,2,1,0:T(1,128)S(1)} %collective-permute-done.3.near, s32[1]{0:T(128)} %bitcast.2.core_ref, f32[2,5,5,1,512]{4,3,2,1,0:T(1,128)S(1)} %bitcast.14, ...), custom_call_target="tpu_custom_call" | custom-call | tf_op jit(solution)/shard_map/pallas_call | solution.py:830
  (5 shorter events, 0.0 us)
Async XLA Ops:
  0.0 0.7 %copy-start.1 = (f32[8,512]{1,0:T(8,128)S(1)}, f32[8,512]{1,0:T(8,128)}, u32[]{:S(2)}) copy-start(f32[8,512]{1,0:T(8,128)} %constant.13.clone.columns) | copy-start | bytes 49156
  0.0 0.7 %copy-start.4 = (s32[4,4]{1,0:T(4,128)S(1)}, s32[4,4]{1,0:T(4,128)}, u32[]{:S(2)}) copy-start(s32[4,4]{1,0:T(4,128)} %orders_hbm.1) | copy-start | bytes 196
  0.0 0.7 %copy-start.2 = (f32[3,4,4]{2,1,0:T(4,128)S(1)}, f32[3,4,4]{2,1,0:T(4,128)}, u32[]{:S(2)}) copy-start(f32[3,4,4]{2,1,0:T(4,128)} %metric_hbm.1) | copy-start | bytes 580
  0.0 0.7 %copy-start.3 = (s32[2,4,4]{2,1,0:T(4,128)S(1)}, s32[2,4,4]{2,1,0:T(4,128)}, u32[]{:S(2)}) copy-start(s32[2,4,4]{2,1,0:T(4,128)} %turn_hbm.1) | copy-start | bytes 388
  0.0 0.7 %copy-start.5 = (s32[1,1,16,1]{2,3,1,0:T(1,128)S(1)}, s32[1,1,16,1]{2,3,1,0:T(1,128)}, u32[]{:S(2)}) copy-start(s32[1,1,16,1]{2,3,1,0:T(1,128)} %param.10) | copy-start | bytes 196
  0.7 0.9 %copy-start = (f32[4,4,5,512]{3,1,2,0:T(4,128)S(1)}, f32[4,4,5,512]{3,1,2,0:T(4,128)}, u32[]{:S(2)}) copy-start(f32[4,4,5,512]{3,1,2,0:T(4,128)} %param.6) | copy-start | bytes 491524
  3.0 14.7 %collective-permute-start = (f32[64,128]{1,0:T(8,128)S(1)}, f32[64,128]{1,0:T(8,128)S(1)}, u32[]{:S(2)}, u32[]{:S(2)}) collective-permute-start(f32[64,128]{1,0:T(8,128)S(1)} %get-tuple-element.30), channel_id=1, source_target_pairs={{12,24},{36,48},{60,72},{84,96},{108,120},{132,144},{156,168},{180... | collective-permute-start | bytes 98312 | tf_op jit(solution)/shard_map/ppermute | solution.py:740
  17.8 4.1 %collective-permute-start.1 = (f32[64,128]{1,0:T(8,128)S(1)}, f32[64,128]{1,0:T(8,128)S(1)}, u32[]{:S(2)}, u32[]{:S(2)}) collective-permute-start(f32[64,128]{1,0:T(8,128)S(1)} %get-tuple-element.34), channel_id=1, source_target_pairs={{1,2},{3,4},{5,6},{7,8},{9,10},{2,1},{4,3},{6,5},{8,7},{10,9},{13,... | collective-permute-start | bytes 98312 | tf_op jit(solution)/shard_map/ppermute | solution.py:740
  24.7 12.9 %collective-permute-start.2 = (f32[10,5,1,512]{3,2,1,0:T(1,128)S(1)}, f32[10,5,1,512]{3,2,1,0:T(1,128)S(1)}, u32[]{:S(2)}, u32[]{:S(2)}) collective-permute-start(f32[10,5,1,512]{3,2,1,0:T(1,128)S(1)} %get-tuple-element.35), channel_id=1, source_target_pairs={{0,744},{12,36},{24,0},{36,60},{48,24},{60,84},{72,48},{84,108},{9... | collective-permute-start | bytes 307208 | tf_op jit(solution)/shard_map/ppermute | solution.py:750
  26.7 12.9 %collective-permute-start.3 = (f32[5,5,1,512]{3,2,1,0:T(1,128)S(1)}, f32[5,5,1,512]{3,2,1,0:T(1,128)S(1)}, u32[]{:S(2)}, u32[]{:S(2)}) collective-permute-start(f32[5,5,1,512]{3,2,1,0:T(1,128)S(1)} %get-tuple-element.37), channel_id=1, source_target_pairs={{0,24},{12,756},{24,48},{36,12},{48,72},{60,36},{72,96},{84,60},{9... | collective-permute-start | bytes 153608 | tf_op jit(solution)/shard_map/ppermute | solution.py:750

commit v7 on v6

--- a/solution.py
+++ b/solution.py
@@ -269,7 +269,7 @@
 
 
 def make_messages(q, tab, order, metric, codes, first_core, outs, buf):
-    tx_low, tx_high, ty_low, ty_high, chip_send, blk_send, up, down = outs
+    tx_low, tx_high, ty_low, ty_high, chip_send, blk_send = outs
     _, elem, _ = lane_ids()
     x_ends, y_ends = x_faces(q, tab), y_faces(q, tab)
     tx = [turned(to_common(tab, x_ends[side]), codes[side], buf) for side in range(2)]
@@ -277,7 +277,6 @@
     for ref, face in zip((tx_low, tx_high, ty_low, ty_high), tx + ty):
         store_face(ref, face)
     x_rows = end_rows(q, tab, lambda n: [q[node(n, j), :] for j in range(8)])
-    y_rows = end_rows(q, tab, lambda n: [q[node(i, n), :] for i in range(8)])
     params = [order.astype(jnp.float32)] + metric
     zero = jnp.zeros((8, LANES), jnp.float32)
 
@@ -286,17 +285,24 @@
         lines = [ty[0][edge], ty[1][edge]] + params + [codes[side].astype(jnp.float32), zero]
         return packed([tx[side], x_ends[side], x_rows[side], lines], elem >> 2, shifts)
 
-    def along_y(side, shifts):
-        edge = 7 * side
-        lines = [tx[0][edge], tx[1][edge]] + params + [zero, zero]
-        return packed([ty[side], y_ends[side], y_rows[side], lines], elem & 3, shifts)
-
     left = along_x(0, (0, 4, 8, 12))
     right = along_x(1, (-12, -8, -4, 0))
     store_face(chip_send, [jnp.where(first_core, r, l) for l, r in zip(left, right)])
     store_face(blk_send, [jnp.where(first_core, l, r) for l, r in zip(left, right)])
-    store_face(down, along_y(0, (0, 1, 2, 3)))
-    store_face(up, along_y(1, (-3, -2, -1, 0)))
+
+
+def make_row_messages(q, tab, order, metric, traces, up, down):
+    tx, ty = traces[:2], traces[2:]
+    _, elem, _ = lane_ids()
+    y_ends = y_faces(q, tab)
+    y_rows = end_rows(q, tab, lambda n: [q[node(i, n), :] for i in range(8)])
+    zero = jnp.zeros((8, LANES), jnp.float32)
+    for side, ref, shifts in ((0, down, (0, 1, 2, 3)), (1, up, (-3, -2, -1, 0))):
+        edge = 7 * side
+        lines = [tx[0][edge], tx[1][edge], order] + metric + [zero, zero]
+        store_face(
+            ref, packed([ty[side], y_ends[side], y_rows[side], lines], elem & 3, shifts)
+        )
 
 
 def sides_of(paired_ref, other_ref, first):
@@ -579,8 +585,8 @@
 def first_kernel(
     fields, columns, orders_hbm, turn_hbm, metric_hbm, _, core_ref, row_ref, q, tab, params, *rest
 ):
-    outs = rest[:8]
-    flat, buf, orders, turn, metric_ref, sems = rest[8:]
+    outs = rest[:6]
+    flat, buf, orders, turn, metric_ref, sems = rest[6:]
     copies = fetched(
         [(orders_hbm, orders), (turn_hbm, turn), (metric_hbm, metric_ref)], sems
     )
@@ -592,7 +598,7 @@
         copy.wait()
     order = spread(lambda x, y: orders[x, y].astype(jnp.float32), jnp.float32)
     metric, codes = all_metrics(metric_ref), all_codes(turn)
-    for n, x in enumerate(metric + codes):
+    for n, x in enumerate(metric + codes + [order]):
         params[pl.ds(8 * n, 8), :] = x.astype(jnp.float32)
     table_for(columns, order[0:1, :], tab)
     in_k = tab[pl.ds(A_AT, 8), :]
@@ -609,8 +615,10 @@
     make_messages(q, tab, order, metric, codes, first_core, outs, buf)
 
 
-def inner_kernel(q, tab, params, rate):
+def inner_kernel(q, tab, params, *rest):
+    traces, (rate, up, down) = [load_face(ref) for ref in rest[:4]], rest[4:]
     metric = kept_metrics(params)
+    make_row_messages(q, tab, params[pl.ds(40, 8), :], metric, traces, up, down)
     volume_terms(q, tab, metric, rate)
     span_terms(q, tab, tab[pl.ds(LIFT_AT, 8), :], metric, rate)
 
@@ -766,9 +774,9 @@
     targets = jnp.transpose(migration, (0, 1, 3, 2))
     q, tab, params, *faces = pl.pallas_call(
         first_kernel,
-        out_shape=[VOLUME, f32(TAB_ROWS, LANES), f32(40, LANES)] + [FACE] * 8,
+        out_shape=[VOLUME, f32(TAB_ROWS, LANES), f32(48, LANES)] + [FACE] * 6,
         in_specs=[VMEM] * 2 + [HBM] * 3 + [ANY] + [SMEM] * 2,
-        out_specs=[VMEM] * 11,
+        out_specs=[VMEM] * 9,
         scratch_shapes=[
             vmem(LANES, 512),
             vmem(64, LANES),
@@ -779,19 +787,19 @@
         ],
         compiler_params=PARAMS,
     )(by_var, columns, orders, face_turn, metric, targets, core, row)
-    chip_send, blk_send, up, down = faces[4:]
+    chip_send, blk_send = faces[4:]
     blk = swapped(blk_send, "blk", True)
     chip = paired(chip_send, "blk")
-    inner = pl.pallas_call(
+    inner, up, down = pl.pallas_call(
         inner_kernel,
-        out_shape=VOLUME,
-        in_specs=[VMEM] * 3,
-        out_specs=VMEM,
+        out_shape=[VOLUME, FACE, FACE],
+        in_specs=[VMEM] * 7,
+        out_specs=[VMEM] * 3,
         compiler_params=PARAMS,
         cost_estimate=pl.CostEstimate(
             flops=40_000_000, bytes_accessed=6_000_000, transcendentals=0
         ),
-    )(q, tab, params)
+    )(q, tab, params, *faces[:4])
     pair_send, row_send = pl.pallas_call(
         second_kernel,
         out_shape=[FACE] * 2,

time: 40.7 us -> 40.8 us (level)
  no operation moved by 1% of the time
where the time goes in v7:
time: 40.8 us; the launch traced here: 40.4 us
  blocking collectives  18.8 us (46%)
  starting transfers between devices  14.1 us (35%)
  Pallas kernels  5.9 us (14%)
  local copies, waits for them, and re-layouts  1.63 us (4%)
    all_gather x4, blocking collectives, paired(): lax.all_gather(array, axis, axis_index_groups=pairs_of(lax.axis_size(axis...  18.8 us
    ppermute x2, starting transfers between devices, hopped(): lax.ppermute(array, 'blk', [(n, (n + step[n % 2]) % count) for n in range...  8.81 us
    ppermute x2, starting transfers between devices, swapped(): return lax.ppermute(array, axis, pairs + [(b, a) for a, b in pairs])  5.25 us
    pallas_call x1, Pallas kernels, local(): pl.pallas_call(third_kernel, out_shape=[f32(n, VARS, 1, 512) for n in (2...  2.94 us
    unnamed x12, local copies, waits for them, and re-layouts  1.63 us
    pallas_call x1, Pallas kernels, local(): pl.pallas_call(first_kernel, out_shape=[VOLUME, f32(TAB_ROWS, LANES), f32...  1.36 us
  transfers between devices with their start and end apart: 4, of which 0 were waited for; matrix products, arithmetic and copies ran while one was open for 0% of the time, Pallas kernels for 2%

profile of v7, /device:TPU:1, one launch (start us, length us, event | category | flops | bytes accessed | tf_op | source)
XLA Modules:
  0.0 40.4 jit_solution(3138883020549323379)
XLA Ops:
  0.0 0.0 copy-start.3
  0.0 0.0 copy-start.5
  0.0 0.7 %copy-done.1 = f32[8,512]{1,0:T(8,128)S(1)} copy-done((f32[8,512]{1,0:T(8,128)S(1)}, f32[8,512]{1,0:T(8,128)}, u32[]{:S(2)}) %copy-start.1) | copy-done | bytes 16408
  0.7 0.0 copy-done.4
  0.7 0.0 copy-done.2
  0.7 0.0 copy-done.3
  0.7 0.9 %copy-done = f32[4,4,5,512]{3,1,2,0:T(4,128)S(1)} copy-done((f32[4,4,5,512]{3,1,2,0:T(4,128)S(1)}, f32[4,4,5,512]{3,1,2,0:T(4,128)}, u32[]{:S(2)}) %copy-start) | copy-done | bytes 163864
  1.7 1.4 %shard_map.64 = (f32[512,128]{1,0:T(8,128)S(1)}, f32[416,128]{1,0:T(8,128)S(1)}, f32[48,128]{1,0:T(8,128)S(1)}, f32[64,128]{1,0:T(8,128)S(1)}, f32[64,128]{1,0:T...) custom-call(f32[4,5,4,512]{3,2,1,0:T(4,128)S(1)} %bitcast.16, ...), custom_call_target="tpu_custom_call" | custom-call | tf_op jit(solution)/shard_map/pallas_call | solution.py:775
  3.0 4.6 %collective-permute-start = (f32[64,128]{1,0:T(8,128)S(1)}, f32[64,128]{1,0:T(8,128)S(1)}, u32[]{:S(2)}, u32[]{:S(2)}) collective-permute-start(f32[64,128]{1,0:T(8,128)S(1)} %get-tuple-element.32), channel_id=1, source_target_pairs={{12,24},{36,48},{60,72},{84,96},{108,120},{132,144},{156,168},{180... | collective-permute-start | bytes 98312 | tf_op jit(solution)/shard_map/ppermute | solution.py:748
  7.6 0.8 %shard_map.65 = (f32[512,128]{1,0:T(8,128)S(1)}, f32[64,128]{1,0:T(8,128)S(1)}, f32[64,128]{1,0:T(8,128)S(1)}) custom-call(f32[512,128]{1,0:T(8,128)S(1)} %get-tuple-element.23.q, f32[416,128]{1,0:T(8,128)S(1)} %get-tuple-element.24.tab, f32[48,128]{1,0:T(8,128)S(1)} %get-tuple-element.25.params, f32[64,128]{1,0:T(8,128)S(1)} %get-tuple-element.26.rest_0_, ...), custom_call_target="tpu_custom_call" | custom-call | flops 40000000 | bytes 6000000 | tf_op jit(solution)/shard_map/pallas_call | solution.py:793
  8.4 9.3 %all-gather = f32[128,128]{1,0:T(8,128)S(1)} all-gather(f32[64,128]{1,0:T(8,128)S(1)} %get-tuple-element.31), channel_id=2, replica_groups={{0,12},{24,36},{48,60},{72,84},{96,108},{120,132},{144,156},{168,180},{..., dimensions={0}, use_global_device_ids=true | all-gather | bytes 98304 | tf_op jit(solution)/shard_map/all_gather | solution.py:752
  17.8 0.0 collective-permute-done.blk.rest_5_
  17.8 0.1 shard_map.66
  17.9 0.7 %collective-permute-start.1 = (f32[64,128]{1,0:T(8,128)S(1)}, f32[64,128]{1,0:T(8,128)S(1)}, u32[]{:S(2)}, u32[]{:S(2)}) collective-permute-start(f32[64,128]{1,0:T(8,128)S(1)} %get-tuple-element.36), channel_id=1, source_target_pairs={{1,2},{3,4},{5,6},{7,8},{9,10},{2,1},{4,3},{6,5},{8,7},{10,9},{13,... | collective-permute-start | bytes 98312 | tf_op jit(solution)/shard_map/ppermute | solution.py:748
  18.5 3.5 %all-gather.1 = f32[128,128]{1,0:T(8,128)S(1)} all-gather(f32[64,128]{1,0:T(8,128)S(1)} %get-tuple-element.35), channel_id=3, replica_groups={{0,1},{2,3},{4,5},{6,7},{8,9},{10,11},{12,13},{14,15},{16,17},{18,19},{..., dimensions={0}, use_global_device_ids=true | all-gather | bytes 98304 | tf_op jit(solution)/shard_map/all_gather | solution.py:752
  22.0 0.0 collective-permute-done.1.rest_7_
  22.0 2.9 %shard_map.67 = (f32[10,5,1,512]{3,2,1,0:T(1,128)S(1)}, f32[5,5,1,512]{3,2,1,0:T(1,128)S(1)}, f32[5,5,1,512]{3,2,1,0:T(1,128)S(1)}, f32[5,5,1,512]{3,2,1,0:T(1,128)S(1)}) custom-call(f32[512,128]{1,0:T(8,128)S(1)} %get-tuple-element.23.q, f32[416,128]{1,0:T(8,128)S(1)} %get-tuple-element.24.tab, f32[48,128]{1,0:T(8,128)S(1)} %get-tuple-element.25.params, ...), custom_call_target="tpu_custom_call" | custom-call | tf_op jit(solution)/shard_map/pallas_call | solution.py:812
  24.9 1.9 %collective-permute-start.2 = (f32[10,5,1,512]{3,2,1,0:T(1,128)S(1)}, f32[10,5,1,512]{3,2,1,0:T(1,128)S(1)}, u32[]{:S(2)}, u32[]{:S(2)}) collective-permute-start(f32[10,5,1,512]{3,2,1,0:T(1,128)S(1)} %get-tuple-element.37), channel_id=1, source_target_pairs={{0,744},{12,36},{24,0},{36,60},{48,24},{60,84},{72,48},{84,108},{9... | collective-permute-start | bytes 307208 | tf_op jit(solution)/shard_map/ppermute | solution.py:758
  26.9 6.9 %collective-permute-start.3 = (f32[5,5,1,512]{3,2,1,0:T(1,128)S(1)}, f32[5,5,1,512]{3,2,1,0:T(1,128)S(1)}, u32[]{:S(2)}, u32[]{:S(2)}) collective-permute-start(f32[5,5,1,512]{3,2,1,0:T(1,128)S(1)} %get-tuple-element.39), channel_id=1, source_target_pairs={{0,24},{12,756},{24,48},{36,12},{48,72},{60,36},{72,96},{84,60},{9... | collective-permute-start | bytes 153608 | tf_op jit(solution)/shard_map/ppermute | solution.py:758
  33.8 4.0 %all-gather.2 = f32[10,5,1,512]{3,2,1,0:T(1,128)S(1)} all-gather(f32[5,5,1,512]{3,2,1,0:T(1,128)S(1)} %get-tuple-element.40), channel_id=4, replica_groups={{0,12},{24,36},{48,60},{72,84},{96,108},{120,132},{144,156},{168,180},{..., dimensions={0}, use_global_device_ids=true | all-gather | bytes 153600 | tf_op jit(solution)/shard_map/all_gather | solution.py:752
  37.8 0.0 collective-permute-done.2.far
  37.8 1.9 %all-gather.3 = f32[20,5,1,512]{3,2,1,0:T(1,128)S(1)} all-gather(f32[10,5,1,512]{3,2,1,0:T(1,128)S(1)} %collective-permute-done.2.far), channel_id=5, replica_groups={{0,12},{24,36},{48,60},{72,84},{96,108},{120,132},{144,156},{168,180},{..., dimensions={0}, use_global_device_ids=true | all-gather | bytes 307200 | tf_op jit(solution)/shard_map/all_gather | solution.py:752
  39.7 0.0 collective-permute-done.3.near
  39.7 0.7 %shard_map.68 = f32[25,5,1,512]{3,2,1,0:T(1,128)} custom-call(f32[10,5,1,512]{3,2,1,0:T(1,128)S(1)} %collective-permute-done.2.far, f32[5,5,1,512]{3,2,1,0:T(1,128)S(1)} %get-tuple-element.38.own, f32[5,5,1,512]{3,2,1,0:T(1,128)S(1)} %collective-permute-done.3.near, s32[1]{0:T(128)} %bitcast.2.core_ref, f32[2,5,5,1,512]{4,3,2,1,0:T(1,128)S(1)} %bitcast.14, ...), custom_call_target="tpu_custom_call" | custom-call | tf_op jit(solution)/shard_map/pallas_call | solution.py:838
  (5 shorter events, 0.0 us)
Async XLA Ops:
  0.0 0.7 %copy-start.1 = (f32[8,512]{1,0:T(8,128)S(1)}, f32[8,512]{1,0:T(8,128)}, u32[]{:S(2)}) copy-start(f32[8,512]{1,0:T(8,128)} %constant.13.clone.columns) | copy-start | bytes 49156
  0.0 0.7 %copy-start.4 = (s32[4,4]{1,0:T(4,128)S(1)}, s32[4,4]{1,0:T(4,128)}, u32[]{:S(2)}) copy-start(s32[4,4]{1,0:T(4,128)} %orders_hbm.1) | copy-start | bytes 196
  0.0 0.7 %copy-start.2 = (f32[3,4,4]{2,1,0:T(4,128)S(1)}, f32[3,4,4]{2,1,0:T(4,128)}, u32[]{:S(2)}) copy-start(f32[3,4,4]{2,1,0:T(4,128)} %metric_hbm.1) | copy-start | bytes 580
  0.0 0.7 %copy-start.3 = (s32[2,4,4]{2,1,0:T(4,128)S(1)}, s32[2,4,4]{2,1,0:T(4,128)}, u32[]{:S(2)}) copy-start(s32[2,4,4]{2,1,0:T(4,128)} %turn_hbm.1) | copy-start | bytes 388
  0.0 0.7 %copy-start.5 = (s32[1,1,16,1]{2,3,1,0:T(1,128)S(1)}, s32[1,1,16,1]{2,3,1,0:T(1,128)}, u32[]{:S(2)}) copy-start(s32[1,1,16,1]{2,3,1,0:T(1,128)} %param.10) | copy-start | bytes 196
  0.7 0.9 %copy-start = (f32[4,4,5,512]{3,1,2,0:T(4,128)S(1)}, f32[4,4,5,512]{3,1,2,0:T(4,128)}, u32[]{:S(2)}) copy-start(f32[4,4,5,512]{3,1,2,0:T(4,128)} %param.6) | copy-start | bytes 491524
  3.0 14.8 %collective-permute-start = (f32[64,128]{1,0:T(8,128)S(1)}, f32[64,128]{1,0:T(8,128)S(1)}, u32[]{:S(2)}, u32[]{:S(2)}) collective-permute-start(f32[64,128]{1,0:T(8,128)S(1)} %get-tuple-element.32), channel_id=1, source_target_pairs={{12,24},{36,48},{60,72},{84,96},{108,120},{132,144},{156,168},{180... | collective-permute-start | bytes 98312 | tf_op jit(solution)/shard_map/ppermute | solution.py:748
  17.9 4.1 %collective-permute-start.1 = (f32[64,128]{1,0:T(8,128)S(1)}, f32[64,128]{1,0:T(8,128)S(1)}, u32[]{:S(2)}, u32[]{:S(2)}) collective-permute-start(f32[64,128]{1,0:T(8,128)S(1)} %get-tuple-element.36), channel_id=1, source_target_pairs={{1,2},{3,4},{5,6},{7,8},{9,10},{2,1},{4,3},{6,5},{8,7},{10,9},{13,... | collective-permute-start | bytes 98312 | tf_op jit(solution)/shard_map/ppermute | solution.py:748
  24.9 12.8 %collective-permute-start.2 = (f32[10,5,1,512]{3,2,1,0:T(1,128)S(1)}, f32[10,5,1,512]{3,2,1,0:T(1,128)S(1)}, u32[]{:S(2)}, u32[]{:S(2)}) collective-permute-start(f32[10,5,1,512]{3,2,1,0:T(1,128)S(1)} %get-tuple-element.37), channel_id=1, source_target_pairs={{0,744},{12,36},{24,0},{36,60},{48,24},{60,84},{72,48},{84,108},{9... | collective-permute-start | bytes 307208 | tf_op jit(solution)/shard_map/ppermute | solution.py:758
  26.9 12.9 %collective-permute-start.3 = (f32[5,5,1,512]{3,2,1,0:T(1,128)S(1)}, f32[5,5,1,512]{3,2,1,0:T(1,128)S(1)}, u32[]{:S(2)}, u32[]{:S(2)}) collective-permute-start(f32[5,5,1,512]{3,2,1,0:T(1,128)S(1)} %get-tuple-element.39), channel_id=1, source_target_pairs={{0,24},{12,756},{24,48},{36,12},{48,72},{60,36},{72,96},{84,60},{9... | collective-permute-start | bytes 153608 | tf_op jit(solution)/shard_map/ppermute | solution.py:758
